TPU v7x, 32 devices: a whole 2x2x4 slice. The times are simulated.
32 devices in a mesh: groups: 2 (over x), ctx: 16 (over z, y, core).
Axes of the slice: x: 2, y: 2, z: 4, core: 2. Of those that a mesh axis runs over, the one named last changes fastest.
Arguments:
- hidden_in: bfloat16 [4096, 2048], P(('groups', 'ctx')), parts along dimension 0, may hold values from -6 to 6
- queries: bfloat16 [4096, 2048], P(('groups', 'ctx')), parts along dimension 0, may hold values from -48 to 48
- keys: bfloat16 [4096, 128], P(('groups', 'ctx')), parts along dimension 0, may hold values from -8 to 8
- values: bfloat16 [4096, 128], P(('groups', 'ctx')), parts along dimension 0, may hold values from -16 to 16
- norm_gain: bfloat16 [2048], replicated, may hold values from 0.25 to 1.75
- router: bfloat16 [2048, 16], replicated, may hold values from -0.125 to 0.125
- w_gate: bfloat16 [16, 2048, 768], P('ctx'), may hold values from -0.125 to 0.125
- w_up: bfloat16 [16, 2048, 768], P('ctx'), may hold values from -0.125 to 0.125
- w_down: bfloat16 [16, 768, 2048], P('ctx'), may hold values from -0.21875 to 0.21875
- expert_ids: int32 [4096, 4], P(('groups', 'ctx')), parts along dimension 0, may hold values from 0 to 15, all different within a row; in each aligned block of 128 rows (0 to 127, 128 to 255, ...) at most 64 rows name the same one
Outputs:
- layer_out: bfloat16 [4096, 2048], P(('groups', 'ctx')), parts along dimension 0
There are 2 independent parts, one for each index of `groups`. A program takes and returns all parts, laid end to end along the dimension named above; an argument that names none is the same for every part. Nothing has to cross between parts.
Inputs may be any that keep to these rules, and one draw needn't show every extreme that they name: `expert_ids`: each row names 4 different experts. Within the rows of one device (aligned blocks of 128 rows) no expert is named more than 64 times, a bound that some block reaches.
All inputs are finite; a program needn't handle non-finite values.
Results may differ from a plain program's by a relative error of at most 0.006.
Values may be sent and summed in bfloat16 or wider, within the bound.
No kernel may reach another device: no remote copies, remote signals or barrier semaphores. Data moves between devices by JAX's collectives and lax.ppermute only.
A program may use at most 128 MiB of HBM per device.

v0:
```python
import math

import jax
import jax.numpy as jnp
from jax import lax
from jax.sharding import PartitionSpec as P

D = 2048
Q_HEADS = 32
KV_HEADS = 2
HEAD_DIM = 64
TOP = 4


def local(hidden_in, queries, keys, values, norm_gain, router, w_gate, w_up, w_down, expert_ids):
    rows = queries.shape[0]
    group = Q_HEADS // KV_HEADS
    inv_scale = 1.0 / math.sqrt(HEAD_DIM)
    my_start = lax.axis_index("ctx") * rows
    query_heads = queries.reshape(rows, KV_HEADS, group, HEAD_DIM)
    query_pos = my_start + jnp.arange(rows, dtype=jnp.int32)

    def one_block(carry, key_block, value_block, block_start):
        run_max, run_sum, run_acc = carry
        scores = (
            jnp.einsum("qgjd,kgd->qgjk", query_heads, key_block, preferred_element_type=jnp.float32)
            * inv_scale
        )
        key_pos = block_start + jnp.arange(key_block.shape[0], dtype=jnp.int32)
        allowed = (key_pos[None, :] <= query_pos[:, None])[:, None, None, :]
        scores = jnp.where(allowed, scores, -1e30)
        new_max = jnp.maximum(run_max, jnp.max(scores, axis=-1))
        factor = jnp.exp(run_max - new_max)
        weights = jnp.where(allowed, jnp.exp(scores - new_max[..., None]), 0.0)
        run_sum = run_sum * factor + jnp.sum(weights, axis=-1)
        update = jnp.einsum(
            "qgjk,kgd->qgjd",
            weights.astype(jnp.bfloat16),
            value_block,
            preferred_element_type=jnp.float32,
        )
        run_acc = run_acc * factor[..., None] + update
        return (new_max, run_sum, run_acc)

    init = (
        jnp.full((rows, KV_HEADS, group), -1e30, jnp.float32),
        jnp.zeros((rows, KV_HEADS, group), jnp.float32),
        jnp.zeros((rows, KV_HEADS, group, HEAD_DIM), jnp.float32),
    )
    key_piece = lax.all_gather(keys, "ctx", axis=0, tiled=True)
    value_piece = lax.all_gather(values, "ctx", axis=0, tiled=True)
    count = key_piece.shape[0]
    key_rows = key_piece.reshape(count, KV_HEADS, HEAD_DIM)
    value_rows = value_piece.reshape(count, KV_HEADS, HEAD_DIM)

    def compute(state):
        steps_in = count // 512
        key_split = key_rows.reshape(steps_in, 512, KV_HEADS, HEAD_DIM)
        value_split = value_rows.reshape(steps_in, 512, KV_HEADS, HEAD_DIM)
        offsets = jnp.arange(steps_in, dtype=jnp.int32) * 512

        def scan_step(inner, triple):
            return (one_block(inner, triple[0], triple[1], triple[2]), None)

        final, unused = lax.scan(scan_step, state, (key_split, value_split, offsets))
        return final

    run_max, run_sum, run_acc = lax.cond(
        jnp.int32(0) < my_start + rows, compute, lambda state: state, init
    )
    attn = (run_acc / run_sum[..., None]).reshape(rows, D).astype(jnp.bfloat16)
    mixed = hidden_in.astype(jnp.float32) + attn.astype(jnp.float32)
    mean_sq = jnp.mean(mixed * mixed, axis=-1, keepdims=True)
    normed = (mixed * lax.rsqrt(mean_sq + 1e-06) * norm_gain.astype(jnp.float32)).astype(
        jnp.bfloat16
    )
    logits = jnp.dot(normed, router, preferred_element_type=jnp.float32)
    chosen = jnp.take_along_axis(logits, expert_ids, axis=1)
    sig = jax.nn.sigmoid(chosen)
    gates = sig / jnp.sum(sig, axis=-1, keepdims=True)
    experts_all = router.shape[1]
    local_experts = w_gate.shape[0]
    devices = lax.axis_size("ctx")
    capacity = 2 * rows * TOP // experts_all
    flat_ids = expert_ids.reshape(-1)
    onehot = (flat_ids[:, None] == jnp.arange(experts_all, dtype=jnp.int32)[None, :]).astype(
        jnp.int32
    )
    ranks = jnp.cumsum(onehot, axis=0) - onehot
    slots = jnp.sum(ranks * onehot, axis=-1)
    position = flat_ids * capacity + slots
    token_of = jnp.arange(rows * TOP, dtype=jnp.int32) // TOP
    outgoing = (
        jnp.zeros((experts_all * capacity, D), jnp.bfloat16).at[position].set(normed[token_of])
    )
    outgoing = outgoing.reshape(devices, local_experts, capacity, D)
    arrived = lax.all_to_all(outgoing, "ctx", split_axis=0, concat_axis=0, tiled=True)
    gate_val = jnp.einsum("sfcd,fdh->sfch", arrived, w_gate, preferred_element_type=jnp.float32)
    up_val = jnp.einsum("sfcd,fdh->sfch", arrived, w_up, preferred_element_type=jnp.float32)
    up_part = (jax.nn.silu(gate_val) * up_val).astype(jnp.bfloat16)
    produced = jnp.einsum(
        "sfch,fhd->sfcd", up_part, w_down, preferred_element_type=jnp.float32
    ).astype(jnp.bfloat16)
    returned = lax.all_to_all(produced, "ctx", split_axis=0, concat_axis=0, tiled=True)
    returned = returned.reshape(experts_all * capacity, D)
    picked = returned[position].astype(jnp.float32).reshape(rows, TOP, D)
    combined = jnp.sum(picked * gates[:, :, None], axis=1)
    return (mixed + combined).astype(jnp.bfloat16)


def solution(mesh):
    placed = (
        P(("groups", "ctx"), None),
        P(("groups", "ctx"), None),
        P(("groups", "ctx"), None),
        P(("groups", "ctx"), None),
        P(),
        P(),
        P("ctx", None, None),
        P("ctx", None, None),
        P("ctx", None, None),
        P(("groups", "ctx"), None),
    )
    return jax.shard_map(
        local, mesh=mesh, in_specs=placed, out_specs=P(("groups", "ctx"), None), check_vma=False
    )
```

profile of v0, /device:TPU:13, one launch (start us, length us, event | category | flops | bytes accessed | tf_op | source)
XLA Modules:
  0.0 386.2 jit_solution(18261940834644575845)
XLA Ops:
  0.0 0.9 copy.57
  1.9 0.9 copy.52
  2.7 18.5 %all_gather.6 = bf16[2048,128]{0,1:T(8,128)(2,1)} all-gather(bf16[128,128]{0,1:T(8,128)(2,1)S(1)} %copy.52), channel_id=1, replica_groups=mesh['groups'=2,'ctx'=16] {'ctx'}, dimensions={0}, use_global_device_ids=true | all-gather | bytes 557056 | tf_op jit(solution)/shard_map/all_gather | solution.py:50
  21.2 0.9 copy.53
  22.1 24.4 %all_gather.7 = bf16[2048,128]{0,1:T(8,128)(2,1)} all-gather(bf16[128,128]{0,1:T(8,128)(2,1)S(1)} %copy.53), channel_id=1, replica_groups=mesh['groups'=2,'ctx'=16] {'ctx'}, dimensions={0}, use_global_device_ids=true | all-gather | bytes 557056 | tf_op jit(solution)/shard_map/all_gather | solution.py:51
  46.5 80.8 %conditional.1 = (f32[128,2,16]{0,2,1:T(8,128)}, f32[128,2,16,64]{0,3,2,1:T(8,128)}) conditional(s32[]{:T(128)} %convert_element_type.58, () %tuple.17, (bf16[2048,128]{0,1:T(8,128)(2,1)}, bf16[2048,128]{0,1:T(8,128)(2,1)}, bf16[128,2048]{1,0:T(8,128)(2,1)}, s32[]{:T(128)}, s32[128]{0:T(128)S(1)}) %tuple.18), branch_computations={%region_0.0_spmd, %region_1.6_spmd} | conditional | flops 565006976 | bytes 67377960 | solution.py:68
  46.5 2.2 reshape_reshape.4
  48.7 2.0 copy.50
  50.6 2.2 reshape_reshape.5
  52.9 1.9 copy.51
  54.8 2.0 copy.54
  56.9 70.4 %while.14 = (s32[]{:T(128)}, f32[128,2,16]{0,2,1:T(8,128)S(1)}, f32[128,2,16]{0,2,1:T(8,128)}, f32[128,2,16,64]{0,3,2,1:T(8,128)}, s32[4]{0:T(128)S(1)}, /*index...) while((s32[]{:T(128)}, f32[128,2,16]{0,2,1:T(8,128)S(1)}, ...), condition=%wide.region_5.5_spmd.clone, body=%wide.region_2.4_spmd.clone.sunk | while | flops 565006848 | bytes 62133924 | solution.py:65
  57.5 0.7 iota_add_fusion.2
  58.4 5.6 %fusion.69 = (f32[128,2,16]{0,2,1:T(8,128)S(1)}, f32[2,512,128,16]{2,1,3,0:T(8,128)}) fusion(pred[128,512]{0,1:T(8,128)(4,1)S(1)} %broadcast_compare_fusion.2, bf16[128,2,16,64]{0,3,2,1:T(8,128)(2,1)} %get-tuple-element.268, bf16[4,512,2,64]{1,3,2,0:T(8,128)(2,1)} %get-tuple-element.267, s32[]{:T(128)} %get-tuple-element.250), kind=kOutput, calls=%fused_computation.6.clone.1 | convolution fusion | flops 274722816 | bytes 9126400 | tf_op jit(solution)/shard_map/cond/branch_1_fun/while/body/eval_jaxpr/qgjd,kgd->qgjk/dot_general | solution.py:26
  64.0 4.7 %fusion.70 = f32[128,2,16]{0,2,1:T(8,128)S(1)} fusion(f32[2,512,128,16]{2,1,3,0:T(8,128)} %get-tuple-element.236, f32[128,2,16]{0,2,1:T(8,128)S(1)} %select_maximum_fusion.2, pred[128,512]{0,1:T(8,128)(4,1)S(1)} %broadcast_compare_fusion.2), kind=kLoop, calls=%fused_computation.8.clone.1 | loop fusion | flops 10481664 | bytes 8486912 | tf_op jit(solution)/shard_map/cond/branch_1_fun/while/body/eval_jaxpr/reduce_sum | solution.py:35
  69.9 4.1 %fusion.72 = f32[128,2,16,64]{0,3,2,1:T(8,128)} fusion(f32[2,512,128,16]{2,1,3,0:T(8,128)S(1)} %copy-done.1, f32[128,2,16]{0,2,1:T(8,128)S(1)} %select_maximum_fusion.2, pred[128,512]{0,1:T(8,128)(4,1)S(1)} %broadcast_compare_fusion.2, f32[128,2,16,64]{0,3,2,1:T(8,128)} %get-tuple-element.253, f32[128,2,16]{0,2,1:T(8,128)S(1)} %get-tuple-element.238, ...), kind=kOutput, calls=%fused_computation.12.clone.1 | convolution fusion | flops 279707648 | bytes 10715649 | tf_op jit(solution)/shard_map/cond/branch_1_fun/while/body/eval_jaxpr/qgjk,kgd->qgjd/dot_general | solution.py:36
  74.6 0.7 iota_add_fusion.2
  75.4 5.6 %fusion.69 = (f32[128,2,16]{0,2,1:T(8,128)S(1)}, f32[2,512,128,16]{2,1,3,0:T(8,128)}) fusion(pred[128,512]{0,1:T(8,128)(4,1)S(1)} %broadcast_compare_fusion.2, bf16[128,2,16,64]{0,3,2,1:T(8,128)(2,1)} %get-tuple-element.268, bf16[4,512,2,64]{1,3,2,0:T(8,128)(2,1)} %get-tuple-element.267, s32[]{:T(128)} %get-tuple-element.250), kind=kOutput, calls=%fused_computation.6.clone.1 | convolution fusion | flops 274722816 | bytes 9126400 | tf_op jit(solution)/shard_map/cond/branch_1_fun/while/body/eval_jaxpr/qgjd,kgd->qgjk/dot_general | solution.py:26
  81.1 4.7 %fusion.70 = f32[128,2,16]{0,2,1:T(8,128)S(1)} fusion(f32[2,512,128,16]{2,1,3,0:T(8,128)} %get-tuple-element.236, f32[128,2,16]{0,2,1:T(8,128)S(1)} %select_maximum_fusion.2, pred[128,512]{0,1:T(8,128)(4,1)S(1)} %broadcast_compare_fusion.2), kind=kLoop, calls=%fused_computation.8.clone.1 | loop fusion | flops 10481664 | bytes 8486912 | tf_op jit(solution)/shard_map/cond/branch_1_fun/while/body/eval_jaxpr/reduce_sum | solution.py:35
  85.8 1.5 fusion.71
  87.3 4.5 %fusion.72 = f32[128,2,16,64]{0,3,2,1:T(8,128)} fusion(f32[2,512,128,16]{2,1,3,0:T(8,128)S(1)} %copy-done.1, f32[128,2,16]{0,2,1:T(8,128)S(1)} %select_maximum_fusion.2, pred[128,512]{0,1:T(8,128)(4,1)S(1)} %broadcast_compare_fusion.2, f32[128,2,16,64]{0,3,2,1:T(8,128)} %get-tuple-element.253, f32[128,2,16]{0,2,1:T(8,128)S(1)} %get-tuple-element.238, ...), kind=kOutput, calls=%fused_computation.12.clone.1 | convolution fusion | flops 279707648 | bytes 10715649 | tf_op jit(solution)/shard_map/cond/branch_1_fun/while/body/eval_jaxpr/qgjk,kgd->qgjd/dot_general | solution.py:36
  93.2 5.6 %fusion.69 = (f32[128,2,16]{0,2,1:T(8,128)S(1)}, f32[2,512,128,16]{2,1,3,0:T(8,128)}) fusion(pred[128,512]{0,1:T(8,128)(4,1)S(1)} %broadcast_compare_fusion.2, bf16[128,2,16,64]{0,3,2,1:T(8,128)(2,1)} %get-tuple-element.268, bf16[4,512,2,64]{1,3,2,0:T(8,128)(2,1)} %get-tuple-element.267, s32[]{:T(128)} %get-tuple-element.250), kind=kOutput, calls=%fused_computation.6.clone.1 | convolution fusion | flops 274722816 | bytes 9126400 | tf_op jit(solution)/shard_map/cond/branch_1_fun/while/body/eval_jaxpr/qgjd,kgd->qgjk/dot_general | solution.py:26
  98.9 4.7 %fusion.70 = f32[128,2,16]{0,2,1:T(8,128)S(1)} fusion(f32[2,512,128,16]{2,1,3,0:T(8,128)} %get-tuple-element.236, f32[128,2,16]{0,2,1:T(8,128)S(1)} %select_maximum_fusion.2, pred[128,512]{0,1:T(8,128)(4,1)S(1)} %broadcast_compare_fusion.2), kind=kLoop, calls=%fused_computation.8.clone.1 | loop fusion | flops 10481664 | bytes 8486912 | tf_op jit(solution)/shard_map/cond/branch_1_fun/while/body/eval_jaxpr/reduce_sum | solution.py:35
  103.5 1.5 fusion.71
  105.0 4.5 %fusion.72 = f32[128,2,16,64]{0,3,2,1:T(8,128)} fusion(f32[2,512,128,16]{2,1,3,0:T(8,128)S(1)} %copy-done.1, f32[128,2,16]{0,2,1:T(8,128)S(1)} %select_maximum_fusion.2, pred[128,512]{0,1:T(8,128)(4,1)S(1)} %broadcast_compare_fusion.2, f32[128,2,16,64]{0,3,2,1:T(8,128)} %get-tuple-element.253, f32[128,2,16]{0,2,1:T(8,128)S(1)} %get-tuple-element.238, ...), kind=kOutput, calls=%fused_computation.12.clone.1 | convolution fusion | flops 279707648 | bytes 10715649 | tf_op jit(solution)/shard_map/cond/branch_1_fun/while/body/eval_jaxpr/qgjk,kgd->qgjd/dot_general | solution.py:36
  111.0 5.6 %fusion.69 = (f32[128,2,16]{0,2,1:T(8,128)S(1)}, f32[2,512,128,16]{2,1,3,0:T(8,128)}) fusion(pred[128,512]{0,1:T(8,128)(4,1)S(1)} %broadcast_compare_fusion.2, bf16[128,2,16,64]{0,3,2,1:T(8,128)(2,1)} %get-tuple-element.268, bf16[4,512,2,64]{1,3,2,0:T(8,128)(2,1)} %get-tuple-element.267, s32[]{:T(128)} %get-tuple-element.250), kind=kOutput, calls=%fused_computation.6.clone.1 | convolution fusion | flops 274722816 | bytes 9126400 | tf_op jit(solution)/shard_map/cond/branch_1_fun/while/body/eval_jaxpr/qgjd,kgd->qgjk/dot_general | solution.py:26
  116.7 4.7 %fusion.70 = f32[128,2,16]{0,2,1:T(8,128)S(1)} fusion(f32[2,512,128,16]{2,1,3,0:T(8,128)} %get-tuple-element.236, f32[128,2,16]{0,2,1:T(8,128)S(1)} %select_maximum_fusion.2, pred[128,512]{0,1:T(8,128)(4,1)S(1)} %broadcast_compare_fusion.2), kind=kLoop, calls=%fused_computation.8.clone.1 | loop fusion | flops 10481664 | bytes 8486912 | tf_op jit(solution)/shard_map/cond/branch_1_fun/while/body/eval_jaxpr/reduce_sum | solution.py:35
  121.3 1.5 fusion.71
  122.8 4.5 %fusion.72 = f32[128,2,16,64]{0,3,2,1:T(8,128)} fusion(f32[2,512,128,16]{2,1,3,0:T(8,128)S(1)} %copy-done.1, f32[128,2,16]{0,2,1:T(8,128)S(1)} %select_maximum_fusion.2, pred[128,512]{0,1:T(8,128)(4,1)S(1)} %broadcast_compare_fusion.2, f32[128,2,16,64]{0,3,2,1:T(8,128)} %get-tuple-element.253, f32[128,2,16]{0,2,1:T(8,128)S(1)} %get-tuple-element.238, ...), kind=kOutput, calls=%fused_computation.12.clone.1 | convolution fusion | flops 279707648 | bytes 10715649 | tf_op jit(solution)/shard_map/cond/branch_1_fun/while/body/eval_jaxpr/qgjk,kgd->qgjd/dot_general | solution.py:36
  127.3 1.4 divide_convert_fusion
  128.7 1.1 bitcast_convert_fusion
  129.8 2.5 copy.55
  132.3 1.6 multiply_reduce_fusion.1
  133.9 1.2 reduce-window.6
  135.6 2.3 multiply_convert_fusion
  138.0 13.0 %scatter_custom_fusion = bf16[1024,2048]{1,0:T(8,128)(2,1)} fusion(s32[512]{0:T(512)S(1)} %bitcast.164, bf16[128,2048]{1,0:T(8,128)(2,1)} %multiply_convert_fusion, s32[1024]{0:T(1024)S(1)} %pad_clamp_fusion.1, bf16[]{:T(256)} %constant.77.clone.1), kind=kCustom, calls=%fused_computation.48 | custom fusion | bytes 4194816 | tf_op jit(solution)/shard_map/scatter | solution.py:94
  151.0 98.8 %all_to_all.10 = bf16[16,1,64,2048]{3,2,1,0:T(8,128)(2,1)S(1)} all-to-all(bf16[16,1,64,2048]{3,2,1,0:T(8,128)(2,1)} %bitcast.163), channel_id=1, replica_groups=mesh['groups'=2,'ctx'=16] {'ctx'}, dimensions={0} | all-to-all | bytes 8388608 | tf_op jit(solution)/shard_map/all_to_all | solution.py:97
  249.8 2.0 copy-done.4
  251.8 5.2 %fusion.23 = f32[16,64,768]{2,1,0:T(8,128)} fusion(bf16[16,1,64,2048]{3,2,1,0:T(8,128)(2,1)S(1)} %all_to_all.10, bf16[1,2048,768]{2,1,0:T(8,128)(2,1)S(1)} %copy-done.8), kind=kOutput, calls=%fused_computation.32 | convolution fusion | flops 3221225472 | bytes 10485760 | tf_op jit(solution)/shard_map/sfcd,fdh->sfch/dot_general | solution.py:99
  257.0 12.3 %convert_bitcast_fusion = bf16[16,1,64,2048]{3,2,1,0:T(8,128)(2,1)} fusion(bf16[1,768,2048]{2,1,0:T(8,128)(2,1)S(1)} %copy-done, f32[16,64,768]{2,1,0:T(8,128)} %fusion.23, bf16[1,2048,768]{2,1,0:T(8,128)(2,1)} %param.20, bf16[16,1,64,2048]{3,2,1,0:T(8,128)(2,1)} %copy-done.4), kind=kOutput, calls=%fused_computation.37 | convolution fusion | flops 6449266688 | bytes 17825792 | tf_op jit(solution)/shard_map/sfch,fhd->sfcd/dot_general | solution.py:101
  269.3 5.2 %all-to-all-start.1 = ((bf16[16,1,64,2048]{3,2,1,0:T(8,128)(2,1)}), bf16[16,1,64,2048]{3,2,1,0:T(8,128)(2,1)}, u32[]{:S(2)}, u32[]{:S(2)}) async-start(bf16[16,1,64,2048]{3,2,1,0:T(8,128)(2,1)} %convert_bitcast_fusion), calls=%async_computation.1 | async-start | bytes 8388608 | tf_op jit(solution)/shard_map/all_to_all | solution.py:104
  274.7 1.3 fusion.55
  276.0 3.8 gather_fusion.1
  280.1 86.8 %all-to-all-done.1 = bf16[16,1,64,2048]{3,2,1,0:T(8,128)(2,1)} async-done(((bf16[16,1,64,2048]{3,2,1,0:T(8,128)(2,1)}), bf16[16,1,64,2048]{3,2,1,0:T(8,128)(2,1)}, u32[]{:S(2)}, u32[]{:S(2)}) %all-to-all-start.1) | async-done | bytes 4194336 | tf_op jit(solution)/shard_map/all_to_all | solution.py:104
  366.9 8.0 %gather_fusion = bf16[512,2048]{1,0:T(8,128)(2,1)} fusion(bf16[1024,2048]{1,0:T(8,128)(2,1)} %bitcast.27, s32[1024]{0:T(1024)S(1)} %pad_clamp_fusion), kind=kCustom, calls=%fused_computation.1 | custom fusion | bytes 4196352 | tf_op jit(solution)/shard_map/gather | solution.py:106
  374.9 4.8 %reshape.200 = f32[128,4,2048]{2,1,0:T(4,128)} reshape(bf16[512,2048]{1,0:T(8,128)(2,1)} %gather_fusion) | data formatting | bytes 6291456 | tf_op jit(solution)/shard_map/convert_element_type | solution.py:106
  379.6 5.5 %multiply_reduce_fusion = f32[128,2048]{1,0:T(8,128)S(1)} fusion(f32[128,4,2048]{2,1,0:T(4,128)} %reshape.200, f32[128,4]{1,0:T(8,128)S(1)} %copy.63), kind=kLoop, calls=%fused_computation.36 | loop fusion | flops 1835008 | bytes 5244928 | tf_op jit(solution)/shard_map/reduce_sum | solution.py:107
  385.2 1.0 add_convert_fusion
  (72 shorter events, 7.9 us)
Async XLA Ops:
  0.0 257.0 %copy-start = (bf16[1,768,2048]{2,1,0:T(8,128)(2,1)S(1)}, bf16[1,768,2048]{2,1,0:T(8,128)(2,1)}, u32[]{:S(2)}) copy-start(bf16[1,768,2048]{2,1,0:T(8,128)(2,1)} %param.22) | copy-start | bytes 9437188
  64.0 5.8 %copy-start.1 = (f32[2,512,128,16]{2,1,3,0:T(8,128)S(1)}, f32[2,512,128,16]{2,1,3,0:T(8,128)}, u32[]{:S(2)}) copy-start(f32[2,512,128,16]{2,1,3,0:T(8,128)} %get-tuple-element.236) | copy-start | bytes 25165828 | tf_op jit(solution)/shard_map/cond/branch_1_fun/while
  81.1 6.2 %copy-start.1 = (f32[2,512,128,16]{2,1,3,0:T(8,128)S(1)}, f32[2,512,128,16]{2,1,3,0:T(8,128)}, u32[]{:S(2)}) copy-start(f32[2,512,128,16]{2,1,3,0:T(8,128)} %get-tuple-element.236) | copy-start | bytes 25165828 | tf_op jit(solution)/shard_map/cond/branch_1_fun/while
  98.9 6.2 %copy-start.1 = (f32[2,512,128,16]{2,1,3,0:T(8,128)S(1)}, f32[2,512,128,16]{2,1,3,0:T(8,128)}, u32[]{:S(2)}) copy-start(f32[2,512,128,16]{2,1,3,0:T(8,128)} %get-tuple-element.236) | copy-start | bytes 25165828 | tf_op jit(solution)/shard_map/cond/branch_1_fun/while
  116.7 6.2 %copy-start.1 = (f32[2,512,128,16]{2,1,3,0:T(8,128)S(1)}, f32[2,512,128,16]{2,1,3,0:T(8,128)}, u32[]{:S(2)}) copy-start(f32[2,512,128,16]{2,1,3,0:T(8,128)} %get-tuple-element.236) | copy-start | bytes 25165828 | tf_op jit(solution)/shard_map/cond/branch_1_fun/while
  127.3 6.6 %copy-start.7 = (bf16[2048]{0:T(1024)(128)(2,1)S(1)}, bf16[2048]{0:T(1024)(128)(2,1)}, u32[]{:S(2)}) copy-start(bf16[2048]{0:T(1024)(128)(2,1)} %param.18) | copy-start | bytes 12292
  151.0 100.8 %copy-start.8 = (bf16[1,2048,768]{2,1,0:T(8,128)(2,1)S(1)}, bf16[1,2048,768]{2,1,0:T(8,128)(2,1)}, u32[]{:S(2)}) copy-start(bf16[1,2048,768]{2,1,0:T(8,128)(2,1)} %param.21) | copy-start | bytes 9437188
  249.8 2.0 copy-start.4
  269.3 5.2 %copy-start.6 = (s32[128,4]{0,1:T(4,128)S(1)}, s32[128,4]{0,1:T(4,128)}, u32[]{:S(2)}) copy-start(s32[128,4]{0,1:T(4,128)} %param.23) | copy-start | bytes 6148
  269.3 5.4 %copy-start.5 = (bf16[2048,16]{0,1:T(8,128)(2,1)S(1)}, bf16[2048,16]{0,1:T(8,128)(2,1)}, u32[]{:S(2)}) copy-start(bf16[2048,16]{0,1:T(8,128)(2,1)} %param.19) | copy-start | bytes 196612
  269.3 97.6 %all-to-all-start.1 = ((bf16[16,1,64,2048]{3,2,1,0:T(8,128)(2,1)}), bf16[16,1,64,2048]{3,2,1,0:T(8,128)(2,1)}, u32[]{:S(2)}, u32[]{:S(2)}) async-start(bf16[16,1,64,2048]{3,2,1,0:T(8,128)(2,1)} %convert_bitcast_fusion), calls=%async_computation.1 | async-start | bytes 8388608 | tf_op jit(solution)/shard_map/all_to_all | solution.py:104
  379.6 5.5 %copy-start.2 = (f32[128,2048]{1,0:T(8,128)S(1)}, f32[128,2048]{1,0:T(8,128)}, u32[]{:S(2)}) copy-start(f32[128,2048]{1,0:T(8,128)} %copy.55) | copy-start | bytes 3145732
  379.6 5.6 %copy-start.3 = (bf16[128,2048]{1,0:T(8,128)(2,1)S(1)}, bf16[128,2048]{1,0:T(8,128)(2,1)}, u32[]{:S(2)}) copy-start(bf16[128,2048]{1,0:T(8,128)(2,1)} %param.14) | copy-start | bytes 1572868
where the time goes:
time: 387 us; the launch traced here: 386 us
  blocking collectives  142 us (37%)
  waiting for transfers between devices  86.8 us (22%)
  matrix products  58.8 us (15%)
  local copies, waits for them, and re-layouts  51.4 us (13%)
  other arithmetic  42 us (11%)
  starting transfers between devices  5.17 us (1%)
    all_to_all x1, blocking collectives, local(): lax.all_to_all(outgoing, 'ctx', split_axis=0, concat_axis=0, tiled=True)  98.8 us
    all_to_all x1, waiting for transfers between devices, local(): lax.all_to_all(produced, 'ctx', split_axis=0, concat_axis=0, tiled=True)  86.8 us
    all_gather x1, blocking collectives, local(): value_piece = lax.all_gather(values, 'ctx', axis=0, tiled=True)  24.4 us
    dot_general x4, matrix products, one_block(): jnp.einsum('qgjd,kgd->qgjk', query_heads, key_block, preferred_element_ty...  22.6 us
    reduce_sum x4, other arithmetic, one_block(): run_sum = run_sum * factor + jnp.sum(weights, axis=-1)  18.7 us
    all_gather x1, blocking collectives, local(): key_piece = lax.all_gather(keys, 'ctx', axis=0, tiled=True)  18.5 us
    dot_general x4, matrix products, one_block(): jnp.einsum('qgjk,kgd->qgjd', weights.astype(jnp.bfloat16), value_block, p...  17.4 us
    scatter x1, local copies, waits for them, and re-layouts, local(): jnp.zeros((experts_all * capacity, D), jnp.bfloat16).at[position]  13 us
  transfers between devices with their start and end apart: 1, of which 1 were waited for; matrix products, arithmetic and copies ran while one was open for 1% of the time, Pallas kernels for 0%

commit v1 on v0

v1 whole, which is shorter than its diff:
```python
import functools

import jax
import jax.numpy as jnp
import numpy as np
from jax import lax
from jax.experimental import pallas as pl
from jax.experimental.pallas import tpu as pltpu
from jax.sharding import PartitionSpec as P

D = 2048
HEAD_DIM = 64
KV_HEADS = 2
TOP = 4
LANES = 128
PARTS = 2
BF = jnp.bfloat16
F32 = jnp.float32
VMEM_LIMIT = 56 * 1024 * 1024


def chip_ring(chips):
    if chips == 8:
        return [0, 2, 4, 6, 7, 5, 3, 1]
    return list(range(chips))


def ring_perm(ring, step):
    chips = len(ring)
    return [
        (ring[i] * 2 + core, ring[(i + step) % chips] * 2 + core)
        for i in range(chips)
        for core in range(2)
    ]


def core_perm(chips):
    return [(i, i ^ 1) for i in range(2 * chips)]


def meta_table(ring):
    chips = len(ring)
    long, short = chips // 2, chips - 1 - chips // 2
    table = np.zeros((2 * chips, chips + 2), np.int32)
    for place, chip in enumerate(ring):
        offsets = [0] + [-s for s in range(1, long + 1)] + [s for s in range(1, short + 1)]
        earlier = [i for i, off in enumerate(offsets) if ring[(place + off) % chips] < chip]
        for core in range(2):
            row = table[chip * 2 + core]
            row[0] = core
            row[1] = len(earlier)
            row[2 : 2 + len(earlier)] = earlier
    return table


def attend_kernel(
    part, chips, experts, meta, q_ref, hid_ref, kv0, kv1, gain, router, ids,
    msg_ref, mixed_ref, kbuf, vbuf, s_scr, mx, tot, acc, attn_scr,
):
    rows = q_ref.shape[0]
    pairs = D // LANES // KV_HEADS
    core, count = meta[0], meta[1]

    def swap_halves(a):
        return jnp.concatenate([a[:, HEAD_DIM:], a[:, :HEAD_DIM]], axis=1)

    for t in range(chips):
        at = slice(t * 128, (t + 1) * 128)
        k = jnp.concatenate([kv0[at, :LANES], kv1[at, :LANES]], axis=0)
        v = jnp.concatenate([kv0[at, LANES:], kv1[at, LANES:]], axis=0)
        kbuf[0, t], kbuf[1, t] = k, swap_halves(k)
        vbuf[0, t], vbuf[1, t] = v, swap_halves(v)

    m_rows = pairs * rows
    lane = lax.broadcasted_iota(jnp.int32, (m_rows, LANES), 1)
    row_in = lax.rem(lax.broadcasted_iota(jnp.int32, (m_rows, 2 * LANES), 0), rows) + part * rows
    col = lax.broadcasted_iota(jnp.int32, (m_rows, 2 * LANES), 1)
    allowed = col <= jnp.where(col < LANES, row_in, core * (4 * LANES) - 1)

    for g in range(KV_HEADS):
        q = jnp.concatenate(
            [q_ref[:, (g * pairs + j) * LANES : (g * pairs + j + 1) * LANES] for j in range(pairs)],
            axis=0,
        )
        q = q.astype(F32) * (HEAD_DIM**-0.5)
        for par in range(2):
            sel = 0 if par == g else 1
            q_par = jnp.where((lane < HEAD_DIM) == (par == 0), q, 0.0).astype(BF)

            def score(idx):
                return lax.dot_general(
                    q_par, kbuf[sel, idx], (((1,), (1,)), ((), ())), preferred_element_type=F32
                )

            s = jnp.where(allowed, score(0), -1e30)
            s_scr[0] = s
            mx[...] = jnp.maximum(s[:, :LANES], s[:, LANES:])

            def first(t, carry):
                s = score(meta[2 + t])
                s_scr[t + 1] = s
                mx[...] = jnp.maximum(mx[...], jnp.maximum(s[:, :LANES], s[:, LANES:]))
                return carry

            lax.fori_loop(0, count, first, 0)
            row_max = jnp.max(mx[...], axis=1, keepdims=True)
            mx[...] = jnp.broadcast_to(row_max, (m_rows, LANES))

            def weigh(slot, idx):
                top = mx[...]
                p = jnp.exp(s_scr[slot] - jnp.concatenate([top, top], axis=1))
                part_sum = p[:, :LANES] + p[:, LANES:]
                part_acc = jnp.dot(p.astype(BF), vbuf[sel, idx], preferred_element_type=F32)
                return part_sum, part_acc

            tot[...], acc[...] = weigh(0, 0)

            def second(t, carry):
                part_sum, part_acc = weigh(t + 1, meta[2 + t])
                tot[...] += part_sum
                acc[...] += part_acc
                return carry

            lax.fori_loop(0, count, second, 0)
            row_sum = jnp.sum(tot[...], axis=1, keepdims=True)
            out = acc[...] / row_sum
            if par == 0:
                even = out
        out = jnp.where(lane < HEAD_DIM, even, out).astype(BF)
        for j in range(pairs):
            c = (g * pairs + j) * LANES
            attn_scr[:, c : c + LANES] = out[j * rows : (j + 1) * rows]

    mixed = hid_ref[...].astype(F32) + attn_scr[...].astype(F32)
    mixed_ref[...] = mixed
    mean_sq = jnp.mean(mixed * mixed, axis=-1, keepdims=True)
    normed = (mixed * lax.rsqrt(mean_sq + 1e-06) * gain[...].astype(F32)).astype(BF)
    msg_ref[:, :D] = normed
    logits = jnp.dot(normed, router[...], preferred_element_type=F32)
    expert = lax.broadcasted_iota(jnp.int32, (rows, LANES), 1)
    picked = expert == ids[:, 0:1]
    for k in range(1, TOP):
        picked = jnp.logical_or(picked, expert == ids[:, k : k + 1])
    sig = jnp.where(picked, 1.0 / (1.0 + jnp.exp(-logits)), 0.0)
    gates = sig / jnp.sum(sig, axis=-1, keepdims=True)
    high = gates.astype(BF).astype(F32)
    low = gates - high
    low = jnp.concatenate([low[:, HEAD_DIM:], low[:, :HEAD_DIM]], axis=1)
    msg_ref[:, D:] = jnp.where(expert < HEAD_DIM, high, low).astype(BF)


def attend(part, chips, experts, meta, queries, hidden, kv0, kv1, gain, router, ids):
    rows = queries.shape[0] // PARTS
    m_rows = D // LANES // KV_HEADS * rows
    whole = lambda a: pl.BlockSpec(a.shape, lambda i: (0,) * a.ndim)
    piece = lambda a: pl.BlockSpec((rows, a.shape[1]), lambda i: (part, 0))
    keys = 2 * kv0.shape[0]
    return pl.pallas_call(
        functools.partial(attend_kernel, part, chips, experts),
        grid=(1,),
        in_specs=[
            pl.BlockSpec(memory_space=pltpu.SMEM),
            piece(queries), piece(hidden), whole(kv0), whole(kv1), whole(gain), whole(router),
            piece(ids),
        ],
        out_specs=[
            pl.BlockSpec((rows, D + LANES), lambda i: (0, 0)),
            pl.BlockSpec((rows, D), lambda i: (0, 0)),
        ],
        out_shape=[
            jax.ShapeDtypeStruct((rows, D + LANES), BF),
            jax.ShapeDtypeStruct((rows, D), F32),
        ],
        scratch_shapes=[
            pltpu.VMEM((2, chips, 2 * LANES, LANES), BF),
            pltpu.VMEM((2, chips, 2 * LANES, LANES), BF),
            pltpu.VMEM((chips, m_rows, 2 * LANES), F32),
            pltpu.VMEM((m_rows, LANES), F32),
            pltpu.VMEM((m_rows, LANES), F32),
            pltpu.VMEM((m_rows, LANES), F32),
            pltpu.VMEM((rows, D), BF),
        ],
        compiler_params=pltpu.CompilerParams(vmem_limit_bytes=VMEM_LIMIT),
        cost_estimate=pl.CostEstimate(
            flops=4 * rows * keys * D * 4, bytes_accessed=4 * 1024 * 1024,
            transcendentals=rows * keys * 32,
        ),
        name="attend",
    )(meta, queries, hidden, kv0, kv1, gain, router, ids)


def expert_kernel(blocks, last, which, *refs):
    meta, refs = refs[0], refs[1:]
    msgs, refs = refs[:blocks], refs[blocks:]
    if last:
        prev, refs = refs[0], refs[1:]
    wg, wu, wd = refs[:3]
    outs, (x, acc) = refs[3:-2], refs[-2:]
    step, steps = pl.program_id(0), pl.num_programs(0)
    rows = msgs[0].shape[0]

    @pl.when(step == 0)
    def _():
        for b in range(blocks):
            x[b * rows : (b + 1) * rows] = msgs[b][:, :D]

    gate_val = jnp.dot(x[...], wg[0], preferred_element_type=F32)
    up_val = jnp.dot(x[...], wu[0], preferred_element_type=F32)
    up_part = (gate_val / (1.0 + jnp.exp(-gate_val)) * up_val).astype(BF)
    product = jnp.dot(up_part, wd[0], preferred_element_type=F32)

    @pl.when(step == 0)
    def _():
        acc[...] = product

    @pl.when(step > 0)
    def _():
        acc[...] += product

    @pl.when(step == steps - 1)
    def _():
        if not last:
            outs[0][...] = acc[...].astype(BF)
            return
        lane = lax.broadcasted_iota(jnp.int32, (rows, LANES), 1)
        half = lax.rem(lane, HEAD_DIM)
        for b in range(blocks):
            at = slice(b * rows, (b + 1) * rows)
            gates = msgs[b][:, D:].astype(F32)
            gate0 = jnp.sum(jnp.where(half == meta[0], gates, 0.0), axis=1, keepdims=True)
            gate1 = jnp.sum(jnp.where(half == meta[1], gates, 0.0), axis=1, keepdims=True)
            mine = acc[at].astype(BF).astype(F32)
            outs[b][...] = (gate0 * prev[at].astype(F32) + gate1 * mine).astype(BF)


def expert(meta, msgs, prev, wg, wu, wd):
    blocks, rows, last = len(msgs), msgs[0].shape[0], prev is not None
    hidden = wg.shape[2]
    tile = 256 if hidden % 256 == 0 else hidden
    m_rows = blocks * rows
    whole = lambda a: pl.BlockSpec(a.shape, lambda i: (0,) * a.ndim)
    ins = list(msgs) + ([prev] if last else [])
    if last:
        out_shape = [jax.ShapeDtypeStruct((rows, D), BF)] * blocks
    else:
        out_shape = [jax.ShapeDtypeStruct((m_rows, D), BF)]
    return pl.pallas_call(
        functools.partial(expert_kernel, blocks, last, 0),
        grid=(hidden // tile,),
        in_specs=[pl.BlockSpec(memory_space=pltpu.SMEM)]
        + [whole(a) for a in ins]
        + [
            pl.BlockSpec((1, D, tile), lambda i: (0, 0, i)),
            pl.BlockSpec((1, D, tile), lambda i: (0, 0, i)),
            pl.BlockSpec((1, tile, D), lambda i: (0, i, 0)),
        ],
        out_specs=[whole(a) for a in out_shape],
        out_shape=out_shape,
        scratch_shapes=[pltpu.VMEM((m_rows, D), BF), pltpu.VMEM((m_rows, D), F32)],
        compiler_params=pltpu.CompilerParams(vmem_limit_bytes=VMEM_LIMIT),
        cost_estimate=pl.CostEstimate(
            flops=6 * m_rows * D * hidden, bytes_accessed=6 * D * hidden, transcendentals=0
        ),
        name="experts",
    )(meta, *ins, wg, wu, wd)


def experts_of(meta, msgs, own, other):
    out = []
    for first in range(0, len(msgs), 8):
        some = msgs[first : first + 8]
        prev = expert(meta, some, None, *own)[0]
        out += expert(meta, some, prev, *other)
    return out


def add(a, b):
    return (a.astype(F32) + b.astype(F32)).astype(BF)


def spread(block, ring, sign):
    chips = len(ring)
    behind, ahead = [], []
    now = block
    for _ in range(chips // 2):
        now = lax.ppermute(now, "ctx", ring_perm(ring, sign))
        behind.append(now)
    now = block
    for _ in range(chips - 1 - chips // 2):
        now = lax.ppermute(now, "ctx", ring_perm(ring, -sign))
        ahead.append(now)
    return behind, ahead


def collect(behind, ahead, ring, sign):
    now = behind[-1]
    for term in ahead[::-1]:
        now = add(lax.ppermute(now, "ctx", ring_perm(ring, sign)), term)
    one = lax.ppermute(now, "ctx", ring_perm(ring, sign))
    now = behind[-2]
    for term in behind[:-2][::-1]:
        now = add(lax.ppermute(now, "ctx", ring_perm(ring, -sign)), term)
    two = lax.ppermute(now, "ctx", ring_perm(ring, -sign))
    return one, two


def local(hidden_in, queries, keys, values, norm_gain, router, w_gate, w_up, w_down, expert_ids):
    chips = lax.axis_size("ctx") // 2
    ring = chip_ring(chips)
    experts = router.shape[1]
    me = lax.axis_index("ctx")
    meta = jnp.asarray(meta_table(ring))[me]
    names = jnp.stack([me, me ^ 1]).astype(jnp.int32)
    router_wide = jnp.pad(router, ((0, 0), (0, LANES - experts)))
    gain = norm_gain.reshape(1, D)

    swap = core_perm(chips)
    kv = jnp.concatenate([keys, values], axis=1)
    behind, ahead = spread(kv, ring, 1)
    kv0 = jnp.concatenate([kv] + behind + ahead, axis=0)
    kv1 = lax.ppermute(kv0, "ctx", swap)
    own = (w_gate, w_up, w_down)
    other = tuple(lax.ppermute(w, "ctx", swap) for w in own)

    signs = [1, -1]
    outs = []
    sent = [
        attend(part, chips, experts, meta, queries, hidden_in, kv0, kv1, gain, router_wide, expert_ids)
        for part in range(PARTS)
    ]
    for part in range(PARTS):
        msg, mixed = sent[part]
        behind, ahead = spread(msg, ring, signs[part])
        terms = experts_of(names, [msg] + behind + ahead, own, other)
        mid = 1 + len(behind)
        one, two = collect(terms[1:mid], terms[mid:], ring, signs[part])
        total = mixed + (terms[0].astype(F32) + one.astype(F32) + two.astype(F32))
        outs.append(total.astype(BF))
    return jnp.concatenate(outs, axis=0)


def solution(mesh):
    placed = (
        P(("groups", "ctx"), None),
        P(("groups", "ctx"), None),
        P(("groups", "ctx"), None),
        P(("groups", "ctx"), None),
        P(),
        P(),
        P("ctx", None, None),
        P("ctx", None, None),
        P("ctx", None, None),
        P(("groups", "ctx"), None),
    )
    return jax.shard_map(
        local, mesh=mesh, in_specs=placed, out_specs=P(("groups", "ctx"), None), check_vma=False
    )
```

time: 387 us -> 198 us (0.51)
  the two profiles are of different devices: /device:TPU:13 before, /device:TPU:0 now
where the time goes in v1:
time: 198 us; the launch traced here: 197 us
  starting transfers between devices  75 us (38%)
  Pallas kernels  58.1 us (29%)
  waiting for transfers between devices  49.7 us (25%)
  local copies, waits for them, and re-layouts  9.86 us (5%)
  other arithmetic  4.38 us (2%)
    pallas_call x4, Pallas kernels, expert(): pl.pallas_call(functools.partial(expert_kernel, blocks, last, 0), grid=(h...  47.6 us
    ppermute x12, starting transfers between devices, spread(): now = lax.ppermute(now, 'ctx', ring_perm(ring, sign))  40.2 us
    ppermute x12, waiting for transfers between devices, spread(): now = lax.ppermute(now, 'ctx', ring_perm(ring, sign))  23.1 us
    ppermute x9, starting transfers between devices, spread(): now = lax.ppermute(now, 'ctx', ring_perm(ring, -sign))  18 us
    pallas_call x2, Pallas kernels, attend(): pl.pallas_call(functools.partial(attend_kernel, part, chips, experts), gr...  10.6 us
    ppermute x4, waiting for transfers between devices, collect(): now = add(lax.ppermute(now, 'ctx', ring_perm(ring, -sign)), term)  9.78 us
    ppermute x6, waiting for transfers between devices, collect(): now = add(lax.ppermute(now, 'ctx', ring_perm(ring, sign)), term)  6.29 us
    ppermute x9, waiting for transfers between devices, spread(): now = lax.ppermute(now, 'ctx', ring_perm(ring, -sign))  6.2 us
  transfers between devices with their start and end apart: 39, of which 19 were waited for; matrix products, arithmetic and copies ran while one was open for 5% of the time, Pallas kernels for 23%

profile of v1, /device:TPU:0, one launch (start us, length us, event | category | flops | bytes accessed | tf_op | source)
XLA Modules:
  0.0 197.5 jit_solution(6411394749976030660)
XLA Ops:
  1.6 3.1 %collective-permute-start = (bf16[128,256]{1,0:T(8,128)(2,1)S(1)}, bf16[128,256]{1,0:T(8,128)(2,1)S(1)}, u32[]{:S(2)}, u32[]{:S(2)}) collective-permute-start(bf16[128,256]{1,0:T(8,128)(2,1)S(1)} %get-tuple-element.45), channel_id=1, source_target_pairs={{0,4},{1,5},{4,8},{5,9},{8,12},{9,13},{12,14},{13,15},{14,10},{15,... | collective-permute-start | bytes 196616 | tf_op jit(solution)/shard_map/ppermute | solution.py:286
  4.6 2.2 %collective-permute-done = bf16[128,256]{1,0:T(8,128)(2,1)S(1)} collective-permute-done((bf16[128,256]{1,0:T(8,128)(2,1)S(1)}, bf16[128,256]{1,0:T(8,128)(2,1)S(1)}, u32[]{:S(2)}, u32[]{:S(2)}) %collective-permute-start) | collective-permute-done | bytes 65568 | tf_op jit(solution)/shard_map/ppermute | solution.py:286
  6.8 2.1 %collective-permute-start.1 = (bf16[128,256]{1,0:T(8,128)(2,1)S(1)}, bf16[128,256]{1,0:T(8,128)(2,1)S(1)}, u32[]{:S(2)}, u32[]{:S(2)}) collective-permute-start(bf16[128,256]{1,0:T(8,128)(2,1)S(1)} %collective-permute-done), channel_id=1, source_target_pairs={{0,4},{1,5},{4,8},{5,9},{8,12},{9,13},{12,14},{13,15},{14,10},{15,... | collective-permute-start | bytes 196616 | tf_op jit(solution)/shard_map/ppermute | solution.py:286
  8.9 2.2 %collective-permute-done.1 = bf16[128,256]{1,0:T(8,128)(2,1)S(1)} collective-permute-done((bf16[128,256]{1,0:T(8,128)(2,1)S(1)}, bf16[128,256]{1,0:T(8,128)(2,1)S(1)}, u32[]{:S(2)}, u32[]{:S(2)}) %collective-permute-start.1) | collective-permute-done | bytes 65568 | tf_op jit(solution)/shard_map/ppermute | solution.py:286
  11.1 2.1 %collective-permute-start.2 = (bf16[128,256]{1,0:T(8,128)(2,1)S(1)}, bf16[128,256]{1,0:T(8,128)(2,1)S(1)}, u32[]{:S(2)}, u32[]{:S(2)}) collective-permute-start(bf16[128,256]{1,0:T(8,128)(2,1)S(1)} %collective-permute-done.1), channel_id=1, source_target_pairs={{0,4},{1,5},{4,8},{5,9},{8,12},{9,13},{12,14},{13,15},{14,10},{15,... | collective-permute-start | bytes 196616 | tf_op jit(solution)/shard_map/ppermute | solution.py:286
  13.2 2.8 %collective-permute-done.2 = bf16[128,256]{1,0:T(8,128)(2,1)S(1)} collective-permute-done((bf16[128,256]{1,0:T(8,128)(2,1)S(1)}, bf16[128,256]{1,0:T(8,128)(2,1)S(1)}, u32[]{:S(2)}, u32[]{:S(2)}) %collective-permute-start.2) | collective-permute-done | bytes 65568 | tf_op jit(solution)/shard_map/ppermute | solution.py:286
  16.0 1.8 collective-permute-start.3
  17.8 2.4 %collective-permute-done.3 = bf16[128,256]{1,0:T(8,128)(2,1)S(1)} collective-permute-done((bf16[128,256]{1,0:T(8,128)(2,1)S(1)}, bf16[128,256]{1,0:T(8,128)(2,1)S(1)}, u32[]{:S(2)}, u32[]{:S(2)}) %collective-permute-start.3) | collective-permute-done | bytes 65568 | tf_op jit(solution)/shard_map/ppermute | solution.py:286
  21.4 1.2 dynamic-slice_bitcast_fusion.meta
  22.6 1.3 reshape.3.gain
  25.0 1.4 copy.13.ids
  28.2 5.3 %attend.3 = (bf16[64,2176]{1,0:T(8,128)(2,1)}, f32[64,2048]{1,0:T(8,128)}) custom-call(s32[10]{0:T(128)} %dynamic-slice_bitcast_fusion.meta, bf16[128,2048]{1,0:T(8,128)(2,1)} %q_ref.3, bf16[128,2048]{1,0:T(8,128)(2,1)} %hid_ref.3, bf16[1024,256]{1,0:T(8,128)(2,1)} %copy-done.12, bf16[1024,256]{1,0:T(8,128)(2,1)} %copy-done.13, ...), custom_call_target="tpu_custom_call" | custom-call | flops 4294967296 | bytes 4194304 | tf_op jit(solution)/shard_map/attend/pallas_call | solution.py:158
  33.4 3.7 %collective-permute-start.25 = (bf16[64,2176]{1,0:T(8,128)(2,1)}, bf16[64,2176]{1,0:T(8,128)(2,1)S(1)}, u32[]{:S(2)}, u32[]{:S(2)}) collective-permute-start(bf16[64,2176]{1,0:T(8,128)(2,1)} %get-tuple-element.36.refs_1_), channel_id=1, source_target_pairs={{0,2},{1,3},{4,0},{5,1},{8,4},{9,5},{12,8},{13,9},{14,12},{15,13},... | collective-permute-start | bytes 835592 | tf_op jit(solution)/shard_map/ppermute | solution.py:286
  37.1 2.0 collective-permute-start.29
  39.1 5.3 %attend.2 = (bf16[64,2176]{1,0:T(8,128)(2,1)}, f32[64,2048]{1,0:T(8,128)}) custom-call(s32[10]{0:T(128)} %dynamic-slice_bitcast_fusion.meta, bf16[128,2048]{1,0:T(8,128)(2,1)} %q_ref.3, bf16[128,2048]{1,0:T(8,128)(2,1)} %hid_ref.3, bf16[1024,256]{1,0:T(8,128)(2,1)} %copy-done.12, bf16[1024,256]{1,0:T(8,128)(2,1)} %copy-done.13, ...), custom_call_target="tpu_custom_call" | custom-call | flops 4294967296 | bytes 4194304 | tf_op jit(solution)/shard_map/attend/pallas_call | solution.py:158
  44.3 1.8 collective-permute-done.25.refs_2_
  46.1 7.3 %collective-permute-start.8 = (bf16[64,2176]{1,0:T(8,128)(2,1)}, bf16[64,2176]{1,0:T(8,128)(2,1)S(1)}, u32[]{:S(2)}, u32[]{:S(2)}) collective-permute-start(bf16[64,2176]{1,0:T(8,128)(2,1)} %get-tuple-element.26.refs_1_), channel_id=1, source_target_pairs={{0,4},{1,5},{4,8},{5,9},{8,12},{9,13},{12,14},{13,15},{14,10},{15,... | collective-permute-start | bytes 835592 | tf_op jit(solution)/shard_map/ppermute | solution.py:286
  53.5 1.4 collective-permute-start.12
  54.8 4.8 %collective-permute-done.8.refs_2_ = bf16[64,2176]{1,0:T(8,128)(2,1)S(1)} collective-permute-done((bf16[64,2176]{1,0:T(8,128)(2,1)}, bf16[64,2176]{1,0:T(8,128)(2,1)S(1)}, u32[]{:S(2)}, u32[]{:S(2)}) %collective-permute-start.8) | collective-permute-done | bytes 278560 | tf_op jit(solution)/shard_map/ppermute | solution.py:286
  59.6 6.1 %collective-permute-start.26 = (bf16[64,2176]{1,0:T(8,128)(2,1)S(1)}, bf16[64,2176]{1,0:T(8,128)(2,1)S(1)}, u32[]{:S(2)}, u32[]{:S(2)}) collective-permute-start(bf16[64,2176]{1,0:T(8,128)(2,1)S(1)} %collective-permute-done.25.refs_2_), channel_id=1, source_target_pairs={{0,2},{1,3},{4,0},{5,1},{8,4},{9,5},{12,8},{13,9},{14,12},{15,13},... | collective-permute-start | bytes 835592 | tf_op jit(solution)/shard_map/ppermute | solution.py:286
  65.7 4.3 %collective-permute-done.12.refs_6_ = bf16[64,2176]{1,0:T(8,128)(2,1)S(1)} collective-permute-done((bf16[64,2176]{1,0:T(8,128)(2,1)}, bf16[64,2176]{1,0:T(8,128)(2,1)S(1)}, u32[]{:S(2)}, u32[]{:S(2)}) %collective-permute-start.12) | collective-permute-done | bytes 278560 | tf_op jit(solution)/shard_map/ppermute | solution.py:290
  70.0 7.1 %collective-permute-start.30 = (bf16[64,2176]{1,0:T(8,128)(2,1)S(1)}, bf16[64,2176]{1,0:T(8,128)(2,1)S(1)}, u32[]{:S(2)}, u32[]{:S(2)}) collective-permute-start(bf16[64,2176]{1,0:T(8,128)(2,1)S(1)} %collective-permute-done.29.refs_6_), channel_id=1, source_target_pairs={{0,4},{1,5},{4,8},{5,9},{8,12},{9,13},{12,14},{13,15},{14,10},{15,... | collective-permute-start | bytes 835592 | tf_op jit(solution)/shard_map/ppermute | solution.py:290
  77.1 5.4 %collective-permute-start.9 = (bf16[64,2176]{1,0:T(8,128)(2,1)S(1)}, bf16[64,2176]{1,0:T(8,128)(2,1)S(1)}, u32[]{:S(2)}, u32[]{:S(2)}) collective-permute-start(bf16[64,2176]{1,0:T(8,128)(2,1)S(1)} %collective-permute-done.8.refs_2_), channel_id=1, source_target_pairs={{0,4},{1,5},{4,8},{5,9},{8,12},{9,13},{12,14},{13,15},{14,10},{15,... | collective-permute-start | bytes 835592 | tf_op jit(solution)/shard_map/ppermute | solution.py:286
  82.5 4.9 %collective-permute-start.13 = (bf16[64,2176]{1,0:T(8,128)(2,1)S(1)}, bf16[64,2176]{1,0:T(8,128)(2,1)S(1)}, u32[]{:S(2)}, u32[]{:S(2)}) collective-permute-start(bf16[64,2176]{1,0:T(8,128)(2,1)S(1)} %collective-permute-done.12.refs_6_), channel_id=1, source_target_pairs={{0,2},{1,3},{4,0},{5,1},{8,4},{9,5},{12,8},{13,9},{14,12},{15,13},... | collective-permute-start | bytes 835592 | tf_op jit(solution)/shard_map/ppermute | solution.py:290
  87.5 4.4 %collective-permute-start.27 = (bf16[64,2176]{1,0:T(8,128)(2,1)S(1)}, bf16[64,2176]{1,0:T(8,128)(2,1)S(1)}, u32[]{:S(2)}, u32[]{:S(2)}) collective-permute-start(bf16[64,2176]{1,0:T(8,128)(2,1)S(1)} %collective-permute-done.26.refs_3_), channel_id=1, source_target_pairs={{0,2},{1,3},{4,0},{5,1},{8,4},{9,5},{12,8},{13,9},{14,12},{15,13},... | collective-permute-start | bytes 835592 | tf_op jit(solution)/shard_map/ppermute | solution.py:286
  91.9 1.3 collective-permute-done.13.refs_7_
  94.1 3.4 %collective-permute-done.27.refs_4_ = bf16[64,2176]{1,0:T(8,128)(2,1)S(1)} collective-permute-done((bf16[64,2176]{1,0:T(8,128)(2,1)S(1)}, bf16[64,2176]{1,0:T(8,128)(2,1)S(1)}, u32[]{:S(2)}, u32[]{:S(2)}) %collective-permute-start.27) | collective-permute-done | bytes 278560 | tf_op jit(solution)/shard_map/ppermute | solution.py:286
  97.5 1.7 collective-permute-start.10
  99.9 1.6 collective-permute-start.28
  102.2 3.5 %collective-permute-done.10.refs_4_ = bf16[64,2176]{1,0:T(8,128)(2,1)S(1)} collective-permute-done((bf16[64,2176]{1,0:T(8,128)(2,1)S(1)}, bf16[64,2176]{1,0:T(8,128)(2,1)S(1)}, u32[]{:S(2)}, u32[]{:S(2)}) %collective-permute-start.10) | collective-permute-done | bytes 278560 | tf_op jit(solution)/shard_map/ppermute | solution.py:286
  105.6 1.7 collective-permute-start.14
  108.3 11.1 %experts.6.refs_9_ = bf16[512,2048]{1,0:T(8,128)(2,1)} custom-call(s32[2]{0:T(128)} %pad_add_fusion.refs_0_, bf16[64,2176]{1,0:T(8,128)(2,1)} %get-tuple-element.36.refs_1_, bf16[64,2176]{1,0:T(8,128)(2,1)} %copy-done.16, bf16[64,2176]{1,0:T(8,128)(2,1)} %copy-done.20, bf16[64,2176]{1,0:T(8,128)(2,1)} %copy-done.23, bf16[64,2176]{1,0:T(8,128)(2,1)} %copy-done.27, ...), custom_call_target="tpu_custom_call" | custom-call | flops 4831838208 | bytes 9437184 | tf_op jit(solution)/shard_map/experts/pallas_call | solution.py:247
  121.0 11.1 %experts.4.refs_9_ = bf16[512,2048]{1,0:T(8,128)(2,1)} custom-call(s32[2]{0:T(128)} %pad_add_fusion.refs_0_, bf16[64,2176]{1,0:T(8,128)(2,1)} %get-tuple-element.26.refs_1_, bf16[64,2176]{1,0:T(8,128)(2,1)} %copy-done.14, bf16[64,2176]{1,0:T(8,128)(2,1)} %copy-done.18, bf16[64,2176]{1,0:T(8,128)(2,1)} %copy-done.22, bf16[64,2176]{1,0:T(8,128)(2,1)} %copy-done.26, ...), custom_call_target="tpu_custom_call" | custom-call | flops 4831838208 | bytes 9437184 | tf_op jit(solution)/shard_map/experts/pallas_call | solution.py:247
  132.1 12.7 %experts.7 = (bf16[64,2048]{1,0:T(8,128)(2,1)}, bf16[64,2048]{1,0:T(8,128)(2,1)}, bf16[64,2048]{1,0:T(8,128)(2,1)}, bf16[64,2048]{1,0:T(8,128)(2,1)}, bf16[64,20...) custom-call(s32[2]{0:T(128)} %pad_add_fusion.refs_0_, ...), custom_call_target="tpu_custom_call" | custom-call | flops 4831838208 | bytes 9437184 | tf_op jit(solution)/shard_map/experts/pallas_call | solution.py:247
  144.8 2.0 collective-permute-start.36
  146.8 12.7 %experts.5 = (bf16[64,2048]{1,0:T(8,128)(2,1)}, bf16[64,2048]{1,0:T(8,128)(2,1)}, bf16[64,2048]{1,0:T(8,128)(2,1)}, bf16[64,2048]{1,0:T(8,128)(2,1)}, bf16[64,20...) custom-call(s32[2]{0:T(128)} %pad_add_fusion.refs_0_, ...), custom_call_target="tpu_custom_call" | custom-call | flops 4831838208 | bytes 9437184 | tf_op jit(solution)/shard_map/experts/pallas_call | solution.py:247
  160.6 1.3 collective-permute-start.18
  162.0 2.0 %collective-permute-start.37 = (bf16[64,2048]{1,0:T(8,128)(2,1)S(1)}, bf16[64,2048]{1,0:T(8,128)(2,1)S(1)}, u32[]{:S(2)}, u32[]{:S(2)}) collective-permute-start(bf16[64,2048]{1,0:T(8,128)(2,1)S(1)} %add_convert_fusion.2), channel_id=1, source_target_pairs={{0,4},{1,5},{4,8},{5,9},{8,12},{9,13},{12,14},{13,15},{14,10},{15,... | collective-permute-start | bytes 786440 | tf_op jit(solution)/shard_map/ppermute | solution.py:302
  164.2 5.1 %collective-permute-done.22 = bf16[64,2048]{1,0:T(8,128)(2,1)S(1)} collective-permute-done((bf16[64,2048]{1,0:T(8,128)(2,1)}, bf16[64,2048]{1,0:T(8,128)(2,1)S(1)}, u32[]{:S(2)}, u32[]{:S(2)}) %collective-permute-start.22) | collective-permute-done | bytes 262176 | tf_op jit(solution)/shard_map/ppermute | solution.py:302
  172.2 1.3 collective-permute-start.19
  173.5 1.3 collective-permute-done.37
  176.0 1.2 collective-permute-start.34
  177.2 3.4 %collective-permute-done.23 = bf16[64,2048]{1,0:T(8,128)(2,1)S(1)} collective-permute-done((bf16[64,2048]{1,0:T(8,128)(2,1)S(1)}, bf16[64,2048]{1,0:T(8,128)(2,1)S(1)}, u32[]{:S(2)}, u32[]{:S(2)}) %collective-permute-start.23) | collective-permute-done | bytes 262176 | tf_op jit(solution)/shard_map/ppermute | solution.py:302
  181.6 1.3 collective-permute-start.20
  182.9 3.2 %collective-permute-done.34 = bf16[64,2048]{1,0:T(8,128)(2,1)S(1)} collective-permute-done((bf16[64,2048]{1,0:T(8,128)(2,1)S(1)}, bf16[64,2048]{1,0:T(8,128)(2,1)S(1)}, u32[]{:S(2)}, u32[]{:S(2)}) %collective-permute-start.34) | collective-permute-done | bytes 262176 | tf_op jit(solution)/shard_map/ppermute | solution.py:298
  187.0 3.0 %collective-permute-done.20 = bf16[64,2048]{1,0:T(8,128)(2,1)S(1)} collective-permute-done((bf16[64,2048]{1,0:T(8,128)(2,1)S(1)}, bf16[64,2048]{1,0:T(8,128)(2,1)S(1)}, u32[]{:S(2)}, u32[]{:S(2)}) %collective-permute-start.20) | collective-permute-done | bytes 262176 | tf_op jit(solution)/shard_map/ppermute | solution.py:298
  190.1 1.9 collective-permute-start.21
  192.9 3.6 %collective-permute-done.21 = bf16[64,2048]{1,0:T(8,128)(2,1)S(1)} collective-permute-done((bf16[64,2048]{1,0:T(8,128)(2,1)S(1)}, bf16[64,2048]{1,0:T(8,128)(2,1)S(1)}, u32[]{:S(2)}, u32[]{:S(2)}) %collective-permute-start.21) | collective-permute-done | bytes 262176 | tf_op jit(solution)/shard_map/ppermute | solution.py:299
  (120 shorter events, 19.8 us)
Async XLA Ops:
  1.6 5.3 %collective-permute-start = (bf16[128,256]{1,0:T(8,128)(2,1)S(1)}, bf16[128,256]{1,0:T(8,128)(2,1)S(1)}, u32[]{:S(2)}, u32[]{:S(2)}) collective-permute-start(bf16[128,256]{1,0:T(8,128)(2,1)S(1)} %get-tuple-element.45), channel_id=1, source_target_pairs={{0,4},{1,5},{4,8},{5,9},{8,12},{9,13},{12,14},{13,15},{14,10},{15,... | collective-permute-start | bytes 196616 | tf_op jit(solution)/shard_map/ppermute | solution.py:286
  4.6 4.3 %collective-permute-start.4 = (bf16[128,256]{1,0:T(8,128)(2,1)S(1)}, bf16[128,256]{1,0:T(8,128)(2,1)S(1)}, u32[]{:S(2)}, u32[]{:S(2)}) collective-permute-start(bf16[128,256]{1,0:T(8,128)(2,1)S(1)} %get-tuple-element.45), channel_id=1, source_target_pairs={{0,2},{1,3},{4,0},{5,1},{8,4},{9,5},{12,8},{13,9},{14,12},{15,13},... | collective-permute-start | bytes 196616 | tf_op jit(solution)/shard_map/ppermute | solution.py:290
  6.8 4.3 %collective-permute-start.1 = (bf16[128,256]{1,0:T(8,128)(2,1)S(1)}, bf16[128,256]{1,0:T(8,128)(2,1)S(1)}, u32[]{:S(2)}, u32[]{:S(2)}) collective-permute-start(bf16[128,256]{1,0:T(8,128)(2,1)S(1)} %collective-permute-done), channel_id=1, source_target_pairs={{0,4},{1,5},{4,8},{5,9},{8,12},{9,13},{12,14},{13,15},{14,10},{15,... | collective-permute-start | bytes 196616 | tf_op jit(solution)/shard_map/ppermute | solution.py:286
  8.9 4.3 %collective-permute-start.5 = (bf16[128,256]{1,0:T(8,128)(2,1)S(1)}, bf16[128,256]{1,0:T(8,128)(2,1)S(1)}, u32[]{:S(2)}, u32[]{:S(2)}) collective-permute-start(bf16[128,256]{1,0:T(8,128)(2,1)S(1)} %collective-permute-done.4), channel_id=1, source_target_pairs={{0,2},{1,3},{4,0},{5,1},{8,4},{9,5},{12,8},{13,9},{14,12},{15,13},... | collective-permute-start | bytes 196616 | tf_op jit(solution)/shard_map/ppermute | solution.py:290
  11.1 4.9 %collective-permute-start.2 = (bf16[128,256]{1,0:T(8,128)(2,1)S(1)}, bf16[128,256]{1,0:T(8,128)(2,1)S(1)}, u32[]{:S(2)}, u32[]{:S(2)}) collective-permute-start(bf16[128,256]{1,0:T(8,128)(2,1)S(1)} %collective-permute-done.1), channel_id=1, source_target_pairs={{0,4},{1,5},{4,8},{5,9},{8,12},{9,13},{12,14},{13,15},{14,10},{15,... | collective-permute-start | bytes 196616 | tf_op jit(solution)/shard_map/ppermute | solution.py:286
  13.2 7.1 %collective-permute-start.6 = (bf16[128,256]{1,0:T(8,128)(2,1)S(1)}, bf16[128,256]{1,0:T(8,128)(2,1)S(1)}, u32[]{:S(2)}, u32[]{:S(2)}) collective-permute-start(bf16[128,256]{1,0:T(8,128)(2,1)S(1)} %collective-permute-done.5), channel_id=1, source_target_pairs={{0,2},{1,3},{4,0},{5,1},{8,4},{9,5},{12,8},{13,9},{14,12},{15,13},... | collective-permute-start | bytes 196616 | tf_op jit(solution)/shard_map/ppermute | solution.py:290
  16.0 4.3 %collective-permute-start.3 = (bf16[128,256]{1,0:T(8,128)(2,1)S(1)}, bf16[128,256]{1,0:T(8,128)(2,1)S(1)}, u32[]{:S(2)}, u32[]{:S(2)}) collective-permute-start(bf16[128,256]{1,0:T(8,128)(2,1)S(1)} %collective-permute-done.2), channel_id=1, source_target_pairs={{0,4},{1,5},{4,8},{5,9},{8,12},{9,13},{12,14},{13,15},{14,10},{15,... | collective-permute-start | bytes 196616 | tf_op jit(solution)/shard_map/ppermute | solution.py:286
  20.3 7.0 %collective-permute-start.7 = (bf16[1024,256]{1,0:T(8,128)(2,1)S(1)}, bf16[1024,256]{1,0:T(8,128)(2,1)S(1)}, u32[]{:S(2)}, u32[]{:S(2)}) collective-permute-start(bf16[1024,256]{1,0:T(8,128)(2,1)S(1)} %constant_dynamic-update-slice_fusion.2.kv0), channel_id=1, source_target_pairs={{0,1},{1,0},{2,3},{3,2},{4,5},{5,4},{6,7},{7,6},{8,9},{9,8},{10,11... | collective-permute-start | bytes 1572872 | tf_op jit(solution)/shard_map/ppermute | solution.py:321
  20.4 111.7 %collective-permute-start.15 = (bf16[1,2048,768]{2,1,0:T(8,128)(2,1)}, bf16[1,2048,768]{2,1,0:T(8,128)(2,1)}, u32[]{:S(2)}, u32[]{:S(2)}) collective-permute-start(bf16[1,2048,768]{2,1,0:T(8,128)(2,1)} %refs_9_.3), channel_id=1, source_target_pairs={{0,1},{1,0},{2,3},{3,2},{4,5},{5,4},{6,7},{7,6},{8,9},{9,8},{10,11... | collective-permute-start | bytes 9437192 | tf_op jit(solution)/shard_map/ppermute | solution.py:323
  20.9 111.2 %collective-permute-start.16 = (bf16[1,2048,768]{2,1,0:T(8,128)(2,1)}, bf16[1,2048,768]{2,1,0:T(8,128)(2,1)}, u32[]{:S(2)}, u32[]{:S(2)}) collective-permute-start(bf16[1,2048,768]{2,1,0:T(8,128)(2,1)} %refs_10_.3), channel_id=1, source_target_pairs={{0,1},{1,0},{2,3},{3,2},{4,5},{5,4},{6,7},{7,6},{8,9},{9,8},{10,11... | collective-permute-start | bytes 9437192 | tf_op jit(solution)/shard_map/ppermute | solution.py:323
  21.0 111.2 %collective-permute-start.17 = (bf16[1,768,2048]{2,1,0:T(8,128)(2,1)}, bf16[1,768,2048]{2,1,0:T(8,128)(2,1)}, u32[]{:S(2)}, u32[]{:S(2)}) collective-permute-start(bf16[1,768,2048]{2,1,0:T(8,128)(2,1)} %refs_11_.3), channel_id=1, source_target_pairs={{0,1},{1,0},{2,3},{3,2},{4,5},{5,4},{6,7},{7,6},{8,9},{9,8},{10,11... | collective-permute-start | bytes 9437192 | tf_op jit(solution)/shard_map/ppermute | solution.py:323
  33.4 12.7 %collective-permute-start.25 = (bf16[64,2176]{1,0:T(8,128)(2,1)}, bf16[64,2176]{1,0:T(8,128)(2,1)S(1)}, u32[]{:S(2)}, u32[]{:S(2)}) collective-permute-start(bf16[64,2176]{1,0:T(8,128)(2,1)} %get-tuple-element.36.refs_1_), channel_id=1, source_target_pairs={{0,2},{1,3},{4,0},{5,1},{8,4},{9,5},{12,8},{13,9},{14,12},{15,13},... | collective-permute-start | bytes 835592 | tf_op jit(solution)/shard_map/ppermute | solution.py:286
  37.1 16.4 %collective-permute-start.29 = (bf16[64,2176]{1,0:T(8,128)(2,1)}, bf16[64,2176]{1,0:T(8,128)(2,1)S(1)}, u32[]{:S(2)}, u32[]{:S(2)}) collective-permute-start(bf16[64,2176]{1,0:T(8,128)(2,1)} %get-tuple-element.36.refs_1_), channel_id=1, source_target_pairs={{0,4},{1,5},{4,8},{5,9},{8,12},{9,13},{12,14},{13,15},{14,10},{15,... | collective-permute-start | bytes 835592 | tf_op jit(solution)/shard_map/ppermute | solution.py:290
  46.1 62.2 %copy-start.16 = (bf16[64,2176]{1,0:T(8,128)(2,1)}, bf16[64,2176]{1,0:T(8,128)(2,1)S(1)}, u32[]{:S(2)}) copy-start(bf16[64,2176]{1,0:T(8,128)(2,1)S(1)} %collective-permute-done.25.refs_2_) | copy-start | bytes 835588
  46.1 13.5 %collective-permute-start.8 = (bf16[64,2176]{1,0:T(8,128)(2,1)}, bf16[64,2176]{1,0:T(8,128)(2,1)S(1)}, u32[]{:S(2)}, u32[]{:S(2)}) collective-permute-start(bf16[64,2176]{1,0:T(8,128)(2,1)} %get-tuple-element.26.refs_1_), channel_id=1, source_target_pairs={{0,4},{1,5},{4,8},{5,9},{8,12},{9,13},{12,14},{13,15},{14,10},{15,... | collective-permute-start | bytes 835592 | tf_op jit(solution)/shard_map/ppermute | solution.py:286
  53.4 54.8 %copy-start.17 = (bf16[64,2176]{1,0:T(8,128)(2,1)}, bf16[64,2176]{1,0:T(8,128)(2,1)S(1)}, u32[]{:S(2)}) copy-start(bf16[64,2176]{1,0:T(8,128)(2,1)S(1)} %collective-permute-done.29.refs_6_) | copy-start | bytes 835588
  53.5 16.5 %collective-permute-start.12 = (bf16[64,2176]{1,0:T(8,128)(2,1)}, bf16[64,2176]{1,0:T(8,128)(2,1)S(1)}, u32[]{:S(2)}, u32[]{:S(2)}) collective-permute-start(bf16[64,2176]{1,0:T(8,128)(2,1)} %get-tuple-element.26.refs_1_), channel_id=1, source_target_pairs={{0,2},{1,3},{4,0},{5,1},{8,4},{9,5},{12,8},{13,9},{14,12},{15,13},... | collective-permute-start | bytes 835592 | tf_op jit(solution)/shard_map/ppermute | solution.py:290
  59.6 59.9 %copy-start.14 = (bf16[64,2176]{1,0:T(8,128)(2,1)}, bf16[64,2176]{1,0:T(8,128)(2,1)S(1)}, u32[]{:S(2)}) copy-start(bf16[64,2176]{1,0:T(8,128)(2,1)S(1)} %collective-permute-done.8.refs_2_) | copy-start | bytes 835588
  59.6 17.5 %collective-permute-start.26 = (bf16[64,2176]{1,0:T(8,128)(2,1)S(1)}, bf16[64,2176]{1,0:T(8,128)(2,1)S(1)}, u32[]{:S(2)}, u32[]{:S(2)}) collective-permute-start(bf16[64,2176]{1,0:T(8,128)(2,1)S(1)} %collective-permute-done.25.refs_2_), channel_id=1, source_target_pairs={{0,2},{1,3},{4,0},{5,1},{8,4},{9,5},{12,8},{13,9},{14,12},{15,13},... | collective-permute-start | bytes 835592 | tf_op jit(solution)/shard_map/ppermute | solution.py:286
  70.0 49.5 %copy-start.15 = (bf16[64,2176]{1,0:T(8,128)(2,1)}, bf16[64,2176]{1,0:T(8,128)(2,1)S(1)}, u32[]{:S(2)}) copy-start(bf16[64,2176]{1,0:T(8,128)(2,1)S(1)} %collective-permute-done.12.refs_6_) | copy-start | bytes 835588
  70.0 12.5 %collective-permute-start.30 = (bf16[64,2176]{1,0:T(8,128)(2,1)S(1)}, bf16[64,2176]{1,0:T(8,128)(2,1)S(1)}, u32[]{:S(2)}, u32[]{:S(2)}) collective-permute-start(bf16[64,2176]{1,0:T(8,128)(2,1)S(1)} %collective-permute-done.29.refs_6_), channel_id=1, source_target_pairs={{0,4},{1,5},{4,8},{5,9},{8,12},{9,13},{12,14},{13,15},{14,10},{15,... | collective-permute-start | bytes 835592 | tf_op jit(solution)/shard_map/ppermute | solution.py:290
  77.1 31.2 %copy-start.20 = (bf16[64,2176]{1,0:T(8,128)(2,1)}, bf16[64,2176]{1,0:T(8,128)(2,1)S(1)}, u32[]{:S(2)}) copy-start(bf16[64,2176]{1,0:T(8,128)(2,1)S(1)} %collective-permute-done.26.refs_3_) | copy-start | bytes 835588
  77.1 10.4 %collective-permute-start.9 = (bf16[64,2176]{1,0:T(8,128)(2,1)S(1)}, bf16[64,2176]{1,0:T(8,128)(2,1)S(1)}, u32[]{:S(2)}, u32[]{:S(2)}) collective-permute-start(bf16[64,2176]{1,0:T(8,128)(2,1)S(1)} %collective-permute-done.8.refs_2_), channel_id=1, source_target_pairs={{0,4},{1,5},{4,8},{5,9},{8,12},{9,13},{12,14},{13,15},{14,10},{15,... | collective-permute-start | bytes 835592 | tf_op jit(solution)/shard_map/ppermute | solution.py:286
  82.5 25.8 %copy-start.21 = (bf16[64,2176]{1,0:T(8,128)(2,1)}, bf16[64,2176]{1,0:T(8,128)(2,1)S(1)}, u32[]{:S(2)}) copy-start(bf16[64,2176]{1,0:T(8,128)(2,1)S(1)} %collective-permute-done.30.refs_7_) | copy-start | bytes 835588
  82.5 10.6 %collective-permute-start.13 = (bf16[64,2176]{1,0:T(8,128)(2,1)S(1)}, bf16[64,2176]{1,0:T(8,128)(2,1)S(1)}, u32[]{:S(2)}, u32[]{:S(2)}) collective-permute-start(bf16[64,2176]{1,0:T(8,128)(2,1)S(1)} %collective-permute-done.12.refs_6_), channel_id=1, source_target_pairs={{0,2},{1,3},{4,0},{5,1},{8,4},{9,5},{12,8},{13,9},{14,12},{15,13},... | collective-permute-start | bytes 835592 | tf_op jit(solution)/shard_map/ppermute | solution.py:290
  87.5 32.0 %copy-start.18 = (bf16[64,2176]{1,0:T(8,128)(2,1)}, bf16[64,2176]{1,0:T(8,128)(2,1)S(1)}, u32[]{:S(2)}) copy-start(bf16[64,2176]{1,0:T(8,128)(2,1)S(1)} %collective-permute-done.9.refs_3_) | copy-start | bytes 835588
  87.5 10.1 %collective-permute-start.27 = (bf16[64,2176]{1,0:T(8,128)(2,1)S(1)}, bf16[64,2176]{1,0:T(8,128)(2,1)S(1)}, u32[]{:S(2)}, u32[]{:S(2)}) collective-permute-start(bf16[64,2176]{1,0:T(8,128)(2,1)S(1)} %collective-permute-done.26.refs_3_), channel_id=1, source_target_pairs={{0,2},{1,3},{4,0},{5,1},{8,4},{9,5},{12,8},{13,9},{14,12},{15,13},... | collective-permute-start | bytes 835592 | tf_op jit(solution)/shard_map/ppermute | solution.py:286
  93.1 26.4 %copy-start.19 = (bf16[64,2176]{1,0:T(8,128)(2,1)}, bf16[64,2176]{1,0:T(8,128)(2,1)S(1)}, u32[]{:S(2)}) copy-start(bf16[64,2176]{1,0:T(8,128)(2,1)S(1)} %collective-permute-done.13.refs_7_) | copy-start | bytes 835588
  93.1 6.8 %collective-permute-start.31 = (bf16[64,2176]{1,0:T(8,128)(2,1)S(1)}, bf16[64,2176]{1,0:T(8,128)(2,1)S(1)}, u32[]{:S(2)}, u32[]{:S(2)}) collective-permute-start(bf16[64,2176]{1,0:T(8,128)(2,1)S(1)} %collective-permute-done.30.refs_7_), channel_id=1, source_target_pairs={{0,4},{1,5},{4,8},{5,9},{8,12},{9,13},{12,14},{13,15},{14,10},{15,... | collective-permute-start | bytes 835592 | tf_op jit(solution)/shard_map/ppermute | solution.py:290
  97.5 8.1 %collective-permute-start.10 = (bf16[64,2176]{1,0:T(8,128)(2,1)S(1)}, bf16[64,2176]{1,0:T(8,128)(2,1)S(1)}, u32[]{:S(2)}, u32[]{:S(2)}) collective-permute-start(bf16[64,2176]{1,0:T(8,128)(2,1)S(1)} %collective-permute-done.9.refs_3_), channel_id=1, source_target_pairs={{0,4},{1,5},{4,8},{5,9},{8,12},{9,13},{12,14},{13,15},{14,10},{15,... | collective-permute-start | bytes 835592 | tf_op jit(solution)/shard_map/ppermute | solution.py:286
  99.9 7.4 %collective-permute-start.28 = (bf16[64,2176]{1,0:T(8,128)(2,1)S(1)}, bf16[64,2176]{1,0:T(8,128)(2,1)S(1)}, u32[]{:S(2)}, u32[]{:S(2)}) collective-permute-start(bf16[64,2176]{1,0:T(8,128)(2,1)S(1)} %collective-permute-done.27.refs_4_), channel_id=1, source_target_pairs={{0,2},{1,3},{4,0},{5,1},{8,4},{9,5},{12,8},{13,9},{14,12},{15,13},... | collective-permute-start | bytes 835592 | tf_op jit(solution)/shard_map/ppermute | solution.py:286
  105.6 13.9 %collective-permute-start.14 = (bf16[64,2176]{1,0:T(8,128)(2,1)S(1)}, bf16[64,2176]{1,0:T(8,128)(2,1)S(1)}, u32[]{:S(2)}, u32[]{:S(2)}) collective-permute-start(bf16[64,2176]{1,0:T(8,128)(2,1)S(1)} %collective-permute-done.13.refs_7_), channel_id=1, source_target_pairs={{0,2},{1,3},{4,0},{5,1},{8,4},{9,5},{12,8},{13,9},{14,12},{15,13},... | collective-permute-start | bytes 835592 | tf_op jit(solution)/shard_map/ppermute | solution.py:290
  107.3 12.2 %collective-permute-start.11 = (bf16[64,2176]{1,0:T(8,128)(2,1)S(1)}, bf16[64,2176]{1,0:T(8,128)(2,1)S(1)}, u32[]{:S(2)}, u32[]{:S(2)}) collective-permute-start(bf16[64,2176]{1,0:T(8,128)(2,1)S(1)} %collective-permute-done.10.refs_4_), channel_id=1, source_target_pairs={{0,4},{1,5},{4,8},{5,9},{8,12},{9,13},{12,14},{13,15},{14,10},{15,... | collective-permute-start | bytes 835592 | tf_op jit(solution)/shard_map/ppermute | solution.py:286
  144.8 17.1 %collective-permute-start.36 = (bf16[64,2048]{1,0:T(8,128)(2,1)}, bf16[64,2048]{1,0:T(8,128)(2,1)S(1)}, u32[]{:S(2)}, u32[]{:S(2)}) collective-permute-start(bf16[64,2048]{1,0:T(8,128)(2,1)} %get-tuple-element.42), channel_id=1, source_target_pairs={{0,4},{1,5},{4,8},{5,9},{8,12},{9,13},{12,14},{13,15},{14,10},{15,... | collective-permute-start | bytes 786440 | tf_op jit(solution)/shard_map/ppermute | solution.py:302
  146.7 17.3 %collective-permute-start.32 = (bf16[64,2048]{1,0:T(8,128)(2,1)}, bf16[64,2048]{1,0:T(8,128)(2,1)S(1)}, u32[]{:S(2)}, u32[]{:S(2)}) collective-permute-start(bf16[64,2048]{1,0:T(8,128)(2,1)} %get-tuple-element.38), channel_id=1, source_target_pairs={{0,2},{1,3},{4,0},{5,1},{8,4},{9,5},{12,8},{13,9},{14,12},{15,13},... | collective-permute-start | bytes 786440 | tf_op jit(solution)/shard_map/ppermute | solution.py:298
  159.5 9.8 %collective-permute-start.22 = (bf16[64,2048]{1,0:T(8,128)(2,1)}, bf16[64,2048]{1,0:T(8,128)(2,1)S(1)}, u32[]{:S(2)}, u32[]{:S(2)}) collective-permute-start(bf16[64,2048]{1,0:T(8,128)(2,1)} %get-tuple-element.32), channel_id=1, source_target_pairs={{0,2},{1,3},{4,0},{5,1},{8,4},{9,5},{12,8},{13,9},{14,12},{15,13},... | collective-permute-start | bytes 786440 | tf_op jit(solution)/shard_map/ppermute | solution.py:302
  160.6 10.6 %collective-permute-start.18 = (bf16[64,2048]{1,0:T(8,128)(2,1)}, bf16[64,2048]{1,0:T(8,128)(2,1)S(1)}, u32[]{:S(2)}, u32[]{:S(2)}) collective-permute-start(bf16[64,2048]{1,0:T(8,128)(2,1)} %get-tuple-element.28), channel_id=1, source_target_pairs={{0,4},{1,5},{4,8},{5,9},{8,12},{9,13},{12,14},{13,15},{14,10},{15,... | collective-permute-start | bytes 786440 | tf_op jit(solution)/shard_map/ppermute | solution.py:298
  162.0 12.9 %collective-permute-start.37 = (bf16[64,2048]{1,0:T(8,128)(2,1)S(1)}, bf16[64,2048]{1,0:T(8,128)(2,1)S(1)}, u32[]{:S(2)}, u32[]{:S(2)}) collective-permute-start(bf16[64,2048]{1,0:T(8,128)(2,1)S(1)} %add_convert_fusion.2), channel_id=1, source_target_pairs={{0,4},{1,5},{4,8},{5,9},{8,12},{9,13},{12,14},{13,15},{14,10},{15,... | collective-permute-start | bytes 786440 | tf_op jit(solution)/shard_map/ppermute | solution.py:302
  164.0 26.0 %copy-start.3 = (bf16[64,2048]{1,0:T(8,128)(2,1)S(1)}, bf16[64,2048]{1,0:T(8,128)(2,1)}, u32[]{:S(2)}) copy-start(bf16[64,2048]{1,0:T(8,128)(2,1)} %get-tuple-element.31) | copy-start | bytes 786436
  164.1 11.9 %collective-permute-start.33 = (bf16[64,2048]{1,0:T(8,128)(2,1)S(1)}, bf16[64,2048]{1,0:T(8,128)(2,1)S(1)}, u32[]{:S(2)}, u32[]{:S(2)}) collective-permute-start(bf16[64,2048]{1,0:T(8,128)(2,1)S(1)} %add_convert_fusion.5), channel_id=1, source_target_pairs={{0,2},{1,3},{4,0},{5,1},{8,4},{9,5},{12,8},{13,9},{14,12},{15,13},... | collective-permute-start | bytes 786440 | tf_op jit(solution)/shard_map/ppermute | solution.py:298
  170.4 10.1 %collective-permute-start.23 = (bf16[64,2048]{1,0:T(8,128)(2,1)S(1)}, bf16[64,2048]{1,0:T(8,128)(2,1)S(1)}, u32[]{:S(2)}, u32[]{:S(2)}) collective-permute-start(bf16[64,2048]{1,0:T(8,128)(2,1)S(1)} %add_convert_fusion.8), channel_id=1, source_target_pairs={{0,2},{1,3},{4,0},{5,1},{8,4},{9,5},{12,8},{13,9},{14,12},{15,13},... | collective-permute-start | bytes 786440 | tf_op jit(solution)/shard_map/ppermute | solution.py:302
  172.2 9.3 %collective-permute-start.19 = (bf16[64,2048]{1,0:T(8,128)(2,1)S(1)}, bf16[64,2048]{1,0:T(8,128)(2,1)S(1)}, u32[]{:S(2)}, u32[]{:S(2)}) collective-permute-start(bf16[64,2048]{1,0:T(8,128)(2,1)S(1)} %add_convert_fusion.11), channel_id=1, source_target_pairs={{0,4},{1,5},{4,8},{5,9},{8,12},{9,13},{12,14},{13,15},{14,10},{15,... | collective-permute-start | bytes 786440 | tf_op jit(solution)/shard_map/ppermute | solution.py:298
  175.0 17.0 %collective-permute-start.38 = (bf16[64,2048]{1,0:T(8,128)(2,1)S(1)}, bf16[64,2048]{1,0:T(8,128)(2,1)S(1)}, u32[]{:S(2)}, u32[]{:S(2)}) collective-permute-start(bf16[64,2048]{1,0:T(8,128)(2,1)S(1)} %add_convert_fusion.1), channel_id=1, source_target_pairs={{0,4},{1,5},{4,8},{5,9},{8,12},{9,13},{12,14},{13,15},{14,10},{15,... | collective-permute-start | bytes 786440 | tf_op jit(solution)/shard_map/ppermute | solution.py:303
  176.0 10.1 %collective-permute-start.34 = (bf16[64,2048]{1,0:T(8,128)(2,1)S(1)}, bf16[64,2048]{1,0:T(8,128)(2,1)S(1)}, u32[]{:S(2)}, u32[]{:S(2)}) collective-permute-start(bf16[64,2048]{1,0:T(8,128)(2,1)S(1)} %add_convert_fusion.4), channel_id=1, source_target_pairs={{0,2},{1,3},{4,0},{5,1},{8,4},{9,5},{12,8},{13,9},{14,12},{15,13},... | collective-permute-start | bytes 786440 | tf_op jit(solution)/shard_map/ppermute | solution.py:298
  180.6 12.3 %collective-permute-start.24 = (bf16[64,2048]{1,0:T(8,128)(2,1)S(1)}, bf16[64,2048]{1,0:T(8,128)(2,1)S(1)}, u32[]{:S(2)}, u32[]{:S(2)}) collective-permute-start(bf16[64,2048]{1,0:T(8,128)(2,1)S(1)} %add_convert_fusion.7), channel_id=1, source_target_pairs={{0,2},{1,3},{4,0},{5,1},{8,4},{9,5},{12,8},{13,9},{14,12},{15,13},... | collective-permute-start | bytes 786440 | tf_op jit(solution)/shard_map/ppermute | solution.py:303
  181.6 8.4 %collective-permute-start.20 = (bf16[64,2048]{1,0:T(8,128)(2,1)S(1)}, bf16[64,2048]{1,0:T(8,128)(2,1)S(1)}, u32[]{:S(2)}, u32[]{:S(2)}) collective-permute-start(bf16[64,2048]{1,0:T(8,128)(2,1)S(1)} %add_convert_fusion.10), channel_id=1, source_target_pairs={{0,4},{1,5},{4,8},{5,9},{8,12},{9,13},{12,14},{13,15},{14,10},{15,... | collective-permute-start | bytes 786440 | tf_op jit(solution)/shard_map/ppermute | solution.py:298
  186.2 6.6 %collective-permute-start.35 = (bf16[64,2048]{1,0:T(8,128)(2,1)S(1)}, bf16[64,2048]{1,0:T(8,128)(2,1)S(1)}, u32[]{:S(2)}, u32[]{:S(2)}) collective-permute-start(bf16[64,2048]{1,0:T(8,128)(2,1)S(1)} %add_convert_fusion.3), channel_id=1, source_target_pairs={{0,2},{1,3},{4,0},{5,1},{8,4},{9,5},{12,8},{13,9},{14,12},{15,13},... | collective-permute-start | bytes 786440 | tf_op jit(solution)/shard_map/ppermute | solution.py:299
  190.1 6.4 %collective-permute-start.21 = (bf16[64,2048]{1,0:T(8,128)(2,1)S(1)}, bf16[64,2048]{1,0:T(8,128)(2,1)S(1)}, u32[]{:S(2)}, u32[]{:S(2)}) collective-permute-start(bf16[64,2048]{1,0:T(8,128)(2,1)S(1)} %add_convert_fusion.9), channel_id=1, source_target_pairs={{0,4},{1,5},{4,8},{5,9},{8,12},{9,13},{12,14},{13,15},{14,10},{15,... | collective-permute-start | bytes 786440 | tf_op jit(solution)/shard_map/ppermute | solution.py:299
  (19 other events, 265.2 us)

commit v2 on v1

v2 whole, which is shorter than its diff:
```python
import functools

import jax
import jax.numpy as jnp
import numpy as np
from jax import lax
from jax.experimental import pallas as pl
from jax.experimental.pallas import tpu as pltpu
from jax.sharding import PartitionSpec as P

D = 2048
HEAD_DIM = 64
KV_HEADS = 2
TOP = 4
LANES = 128
PARTS = 2
BF = jnp.bfloat16
F32 = jnp.float32
MIB = 1024 * 1024


def chip_ring(chips):
    if chips == 8:
        return [0, 2, 4, 6, 7, 5, 3, 1]
    return list(range(chips))


def ring_perm(ring, step):
    chips = len(ring)
    return [
        (ring[i] * 2 + core, ring[(i + step) % chips] * 2 + core)
        for i in range(chips)
        for core in range(2)
    ]


def core_perm(chips):
    return [(i, i ^ 1) for i in range(2 * chips)]


def meta_table(ring):
    chips = len(ring)
    long, short = chips // 2, chips - 1 - chips // 2
    table = np.zeros((2 * chips, chips + 2), np.int32)
    for place, chip in enumerate(ring):
        offsets = [0] + [-s for s in range(1, long + 1)] + [s for s in range(1, short + 1)]
        earlier = [i for i, off in enumerate(offsets) if ring[(place + off) % chips] < chip]
        for core in range(2):
            row = table[chip * 2 + core]
            row[0] = core
            row[1] = len(earlier)
            row[2 : 2 + len(earlier)] = earlier
    return table


def attend_kernel(
    part, chips, together, table, q_ref, hid_ref, kv0, kv1, gain, router_t, ids_t,
    msg_ref, mixed_ref, q_buf, kbuf, vbuf, s_scr, mx, tot, acc, wide,
):
    rows = mixed_ref.shape[0]
    pairs = D // LANES // KV_HEADS
    m_rows = pairs * rows
    mine = pl.ds(part * rows, rows)
    me = lax.axis_index("ctx")
    core, count = table[me, 0], table[me, 1]

    def swap_halves(a):
        return jnp.concatenate([a[:, HEAD_DIM:], a[:, :HEAD_DIM]], axis=1)

    for t in range(chips):
        at = slice(t * LANES, (t + 1) * LANES)
        k = jnp.concatenate([kv0[at, :LANES], kv1[at, :LANES]], axis=0)
        v = jnp.concatenate([kv0[at, LANES:], kv1[at, LANES:]], axis=0)
        kbuf[0, t], kbuf[1, t] = k, swap_halves(k)
        vbuf[0, t], vbuf[1, t] = v, swap_halves(v)

    lane = lax.broadcasted_iota(jnp.int32, (rows, LANES), 1)
    sets = [(0, 0), (1, 1), (0, 1), (1, 0)]
    for n, (g, par) in enumerate(sets):
        for j in range(pairs):
            c = (g * pairs + j) * LANES
            q = q_ref[mine, c : c + LANES].astype(F32) * (HEAD_DIM**-0.5)
            q = jnp.where((lane < HEAD_DIM) == (par == 0), q, 0.0).astype(BF)
            q_buf[n, j * rows : (j + 1) * rows] = q

    row_in = lax.rem(lax.broadcasted_iota(jnp.int32, (m_rows, 2 * LANES), 0), rows) + part * rows
    col = lax.broadcasted_iota(jnp.int32, (m_rows, 2 * LANES), 1)
    allowed = col <= jnp.where(col < LANES, row_in, core * (4 * LANES) - 1)

    for start in range(0, 4, together):
        group = range(start, start + together)

        def score(n, idx):
            return lax.dot_general(
                q_buf[n], kbuf[n // 2, idx], (((1,), (1,)), ((), ())), preferred_element_type=F32
            )

        for n in group:
            s = jnp.where(allowed, score(n, 0), -1e30)
            s_scr[0, n - start] = s
            mx[n - start] = jnp.maximum(s[:, :LANES], s[:, LANES:])

        def first(t, carry):
            for n in group:
                s = score(n, table[me, 2 + t])
                s_scr[t + 1, n - start] = s
                mx[n - start] = jnp.maximum(mx[n - start], jnp.maximum(s[:, :LANES], s[:, LANES:]))
            return carry

        lax.fori_loop(0, count, first, 0)
        for n in group:
            row_max = jnp.max(mx[n - start], axis=1, keepdims=True)
            mx[n - start] = jnp.broadcast_to(row_max, (m_rows, LANES))

        def weigh(n, slot, idx):
            top = mx[n - start]
            p = jnp.exp(s_scr[slot, n - start] - jnp.concatenate([top, top], axis=1))
            part_sum = p[:, :LANES] + p[:, LANES:]
            part_acc = jnp.dot(p.astype(BF), vbuf[n // 2, idx], preferred_element_type=F32)
            return part_sum, part_acc

        for n in group:
            tot[n], acc[n] = weigh(n, 0, 0)

        def second(t, carry):
            for n in group:
                part_sum, part_acc = weigh(n, t + 1, table[me, 2 + t])
                tot[n] += part_sum
                acc[n] += part_acc
            return carry

        lax.fori_loop(0, count, second, 0)

    for g, even, odd in ((0, 0, 2), (1, 3, 1)):
        for j in range(pairs):
            at = slice(j * rows, (j + 1) * rows)
            c = (g * pairs + j) * LANES
            one = acc[even, at] / jnp.sum(tot[even, at], axis=1, keepdims=True)
            two = acc[odd, at] / jnp.sum(tot[odd, at], axis=1, keepdims=True)
            attn = jnp.where(lane < HEAD_DIM, one, two).astype(BF).astype(F32)
            mixed_ref[:, c : c + LANES] = hid_ref[mine, c : c + LANES].astype(F32) + attn

    mixed = mixed_ref[...]
    mean_sq = jnp.mean(mixed * mixed, axis=-1, keepdims=True)
    wide_gain = gain[...].astype(F32).reshape(1, D)
    normed = (mixed * lax.rsqrt(mean_sq + 1e-06) * wide_gain).astype(BF)
    msg_ref[:, :D] = normed

    experts = router_t.shape[0]
    wide[...] = jnp.zeros_like(wide)
    wide[:experts] = router_t[...]
    logits = lax.dot_general(
        normed, wide[...], (((1,), (1,)), ((), ())), preferred_element_type=F32
    )
    expert = lax.broadcasted_iota(jnp.int32, (LANES, LANES), 0)
    picked = expert == ids_t[0:1, :]
    for k in range(1, TOP):
        picked = jnp.logical_or(picked, expert == ids_t[k : k + 1, :])
    picked = jnp.where(picked, 1.0, 0.0).T[part * rows : (part + 1) * rows]
    sig = jnp.where(picked > 0.0, 1.0 / (1.0 + jnp.exp(-logits)), 0.0)
    gates = sig / jnp.sum(sig, axis=-1, keepdims=True)
    high = gates.astype(BF).astype(F32)
    low = gates - high
    low = jnp.concatenate([low[:, HEAD_DIM:], low[:, :HEAD_DIM]], axis=1)
    msg_ref[:, D:] = jnp.where(lane < HEAD_DIM, high, low).astype(BF)


def attend(part, chips, table, queries, hidden, kv0, kv1, gain, router_t, ids_t):
    rows = queries.shape[0] // PARTS
    m_rows = D // LANES // KV_HEADS * rows
    together = 4 if chips <= 8 else 1
    vmem = pl.BlockSpec(memory_space=pltpu.VMEM)
    return pl.pallas_call(
        functools.partial(attend_kernel, part, chips, together),
        in_specs=[pl.BlockSpec(memory_space=pltpu.SMEM)] + [vmem] * 7,
        out_specs=[vmem, vmem],
        out_shape=[
            jax.ShapeDtypeStruct((rows, D + LANES), BF),
            jax.ShapeDtypeStruct((rows, D), F32),
        ],
        scratch_shapes=[
            pltpu.VMEM((4, m_rows, LANES), BF),
            pltpu.VMEM((2, chips, 2 * LANES, LANES), BF),
            pltpu.VMEM((2, chips, 2 * LANES, LANES), BF),
            pltpu.VMEM((chips, together, m_rows, 2 * LANES), F32),
            pltpu.VMEM((together, m_rows, LANES), F32),
            pltpu.VMEM((4, m_rows, LANES), F32),
            pltpu.VMEM((4, m_rows, LANES), F32),
            pltpu.VMEM((LANES, D), BF),
        ],
        compiler_params=pltpu.CompilerParams(vmem_limit_bytes=34 * MIB),
        cost_estimate=cost(9),
        name="attend",
    )(table, queries, hidden, kv0, kv1, gain, router_t, ids_t)


def cost(micros):
    return pl.CostEstimate(flops=int(micros * 1.15e9), bytes_accessed=1 << 20, transcendentals=0)


def expert_kernel(blocks, last, *refs):
    msgs, refs = refs[:blocks], refs[blocks:]
    if last:
        prev, refs = refs[0], refs[1:]
    wg, wu, wd = refs[:3]
    outs, x = refs[3:-1], refs[-1]
    rows = msgs[0].shape[0]
    for b in range(blocks):
        x[b * rows : (b + 1) * rows] = msgs[b][:, :D]
    gate_val = jnp.dot(x[...], wg[0], preferred_element_type=F32)
    up_val = jnp.dot(x[...], wu[0], preferred_element_type=F32)
    up_part = (gate_val / (1.0 + jnp.exp(-gate_val)) * up_val).astype(BF)
    made = jnp.dot(up_part, wd[0], preferred_element_type=F32).astype(BF)
    if not last:
        outs[0][...] = made
        return
    me = lax.axis_index("ctx")
    lane = lax.broadcasted_iota(jnp.int32, (rows, LANES), 1)
    half = lax.rem(lane, HEAD_DIM)
    for b in range(blocks):
        at = slice(b * rows, (b + 1) * rows)
        gates = msgs[b][:, D:].astype(F32)
        gate0 = jnp.sum(jnp.where(half == me, gates, 0.0), axis=1, keepdims=True)
        gate1 = jnp.sum(jnp.where(half == (me ^ 1), gates, 0.0), axis=1, keepdims=True)
        both = gate0 * prev[at].astype(F32) + gate1 * made[at].astype(F32)
        outs[b][...] = both.astype(BF)


def expert(msgs, prev, wg, wu, wd):
    blocks, rows, last = len(msgs), msgs[0].shape[0], prev is not None
    m_rows = blocks * rows
    ins = list(msgs) + ([prev] if last else [])
    if last:
        out_shape = [jax.ShapeDtypeStruct((rows, D), BF)] * blocks
    else:
        out_shape = [jax.ShapeDtypeStruct((m_rows, D), BF)]
    vmem = pl.BlockSpec(memory_space=pltpu.VMEM)
    return pl.pallas_call(
        functools.partial(expert_kernel, blocks, last),
        in_specs=[vmem] * (len(ins) + 3),
        out_specs=[vmem] * len(out_shape),
        out_shape=out_shape,
        scratch_shapes=[pltpu.VMEM((m_rows, D), BF)],
        compiler_params=pltpu.CompilerParams(vmem_limit_bytes=32 * MIB),
        cost_estimate=cost(6),
        name="experts",
    )(*ins, wg, wu, wd)


def experts_of(msgs, own, other):
    out = []
    for first in range(0, len(msgs), 8):
        some = msgs[first : first + 8]
        prev = expert(some, None, *own)[0]
        out += expert(some, prev, *other)
    return out


def add(a, b):
    return (a.astype(F32) + b.astype(F32)).astype(BF)


def spread(block, ring, sign):
    chips = len(ring)
    behind, ahead = [], []
    now = block
    for _ in range(chips // 2):
        now = lax.ppermute(now, "ctx", ring_perm(ring, sign))
        behind.append(now)
    now = block
    for _ in range(chips - 1 - chips // 2):
        now = lax.ppermute(now, "ctx", ring_perm(ring, -sign))
        ahead.append(now)
    return behind, ahead


def collect(behind, ahead, ring, sign):
    now = behind[-1]
    for term in ahead[::-1]:
        now = add(lax.ppermute(now, "ctx", ring_perm(ring, sign)), term)
    one = lax.ppermute(now, "ctx", ring_perm(ring, sign))
    now = behind[-2]
    for term in behind[:-2][::-1]:
        now = add(lax.ppermute(now, "ctx", ring_perm(ring, -sign)), term)
    two = lax.ppermute(now, "ctx", ring_perm(ring, -sign))
    return one, two


def local(hidden_in, queries, keys, values, norm_gain, router, w_gate, w_up, w_down, expert_ids):
    chips = lax.axis_size("ctx") // 2
    ring = chip_ring(chips)
    table = jnp.asarray(meta_table(ring))
    router_t = router.T
    ids_t = expert_ids.T

    swap = core_perm(chips)
    kv = jnp.concatenate([keys, values], axis=1)
    behind, ahead = spread(kv, ring, 1)
    kv0 = jnp.concatenate([kv] + behind + ahead, axis=0)
    kv1 = lax.ppermute(kv0, "ctx", swap)
    own = (w_gate, w_up, w_down)
    other = tuple(lax.ppermute(w, "ctx", swap) for w in own)

    signs = [1, -1]
    outs = []
    sent = [
        attend(part, chips, table, queries, hidden_in, kv0, kv1, norm_gain, router_t, ids_t)
        for part in range(PARTS)
    ]
    for part in range(PARTS):
        msg, mixed = sent[part]
        behind, ahead = spread(msg, ring, signs[part])
        terms = experts_of([msg] + behind + ahead, own, other)
        mid = 1 + len(behind)
        one, two = collect(terms[1:mid], terms[mid:], ring, signs[part])
        total = mixed + (terms[0].astype(F32) + one.astype(F32) + two.astype(F32))
        outs.append(total.astype(BF))
    return jnp.concatenate(outs, axis=0)


def solution(mesh):
    placed = (
        P(("groups", "ctx"), None),
        P(("groups", "ctx"), None),
        P(("groups", "ctx"), None),
        P(("groups", "ctx"), None),
        P(),
        P(),
        P("ctx", None, None),
        P("ctx", None, None),
        P("ctx", None, None),
        P(("groups", "ctx"), None),
    )
    return jax.shard_map(
        local, mesh=mesh, in_specs=placed, out_specs=P(("groups", "ctx"), None), check_vma=False
    )
```

time: 198 us -> 151 us (0.76)
  Pallas kernels: 58.1 us -> 26.1 us
  starting transfers between devices: 75 us -> 58.6 us
  waiting for transfers between devices: 49.7 us -> 57.5 us
  local copies, waits for them, and re-layouts: 9.86 us -> 6.59 us
  other arithmetic: 4.38 us -> 1.71 us
    pallas_call x6, Pallas kernels: 58.1 us -> 26.1 us  [the longest x4 20.6 us: expert(): pl.pallas_call(functools.partial(expert_kernel, blocks, last), in_specs=[...]
    ppermute x12, starting transfers between devices: 40.2 us -> 29.5 us  [spread(): now = lax.ppermute(now, 'ctx', ring_perm(ring, sign))]
    ppermute x12, waiting for transfers between devices: 23.1 us -> 27.5 us  [spread(): now = lax.ppermute(now, 'ctx', ring_perm(ring, sign))]
    ppermute x9, starting transfers between devices: 18 us -> 13.8 us  [spread(): now = lax.ppermute(now, 'ctx', ring_perm(ring, -sign))]
    ppermute x2, waiting for transfers between devices: 4.37 us -> 6.87 us  [collect(): one = lax.ppermute(now, 'ctx', ring_perm(ring, sign))]
    convert_element_type x10, other arithmetic: 2.64 us -> 0.64 us  [add(): return (a.astype(F32) + b.astype(F32)).astype(BF)]
    unnamed x65 -> x25, local copies, waits for them, and re-layouts: 5.67 us -> 5.8 us
  transfers between devices with their start and end apart: 39 -> 39, of which waited for: 19 -> 23; matrix products, arithmetic and copies ran while one was open for 5% -> 1% of each run, Pallas kernels for 23% -> 14%
where the time goes in v2:
time: 151 us
  starting transfers between devices  58.6 us (39%)
  waiting for transfers between devices  57.5 us (38%)
  Pallas kernels  26.1 us (17%)
  local copies, waits for them, and re-layouts  6.59 us (4%)
  other arithmetic  1.71 us (1%)
    ppermute x12, starting transfers between devices, spread(): now = lax.ppermute(now, 'ctx', ring_perm(ring, sign))  29.5 us
    ppermute x12, waiting for transfers between devices, spread(): now = lax.ppermute(now, 'ctx', ring_perm(ring, sign))  27.5 us
    pallas_call x4, Pallas kernels, expert(): pl.pallas_call(functools.partial(expert_kernel, blocks, last), in_specs=[...  20.6 us
    ppermute x9, starting transfers between devices, spread(): now = lax.ppermute(now, 'ctx', ring_perm(ring, -sign))  13.8 us
    ppermute x4, waiting for transfers between devices, collect(): now = add(lax.ppermute(now, 'ctx', ring_perm(ring, -sign)), term)  11.6 us
    ppermute x2, waiting for transfers between devices, collect(): one = lax.ppermute(now, 'ctx', ring_perm(ring, sign))  6.87 us
    ppermute x6, waiting for transfers between devices, collect(): now = add(lax.ppermute(now, 'ctx', ring_perm(ring, sign)), term)  6.14 us
    ppermute x4, starting transfers between devices, collect(): now = add(lax.ppermute(now, 'ctx', ring_perm(ring, -sign)), term)  6.09 us
  transfers between devices with their start and end apart: 39, of which 23 were waited for; matrix products, arithmetic and copies ran while one was open for 1% of the time, Pallas kernels for 14%

profile of v2, /device:TPU:0, one launch (start us, length us, event | category | flops | bytes accessed | tf_op | source)
XLA Modules:
  0.0 150.8 jit_solution(13066301767722715132)
XLA Ops:
  1.6 3.1 %collective-permute-start = (bf16[128,256]{1,0:T(8,128)(2,1)S(1)}, bf16[128,256]{1,0:T(8,128)(2,1)S(1)}, u32[]{:S(2)}, u32[]{:S(2)}) collective-permute-start(bf16[128,256]{1,0:T(8,128)(2,1)S(1)} %get-tuple-element.45), channel_id=1, source_target_pairs={{0,4},{1,5},{4,8},{5,9},{8,12},{9,13},{12,14},{13,15},{14,10},{15,... | collective-permute-start | bytes 196616 | tf_op jit(solution)/shard_map/ppermute | solution.py:268
  4.6 2.2 %collective-permute-done = bf16[128,256]{1,0:T(8,128)(2,1)S(1)} collective-permute-done((bf16[128,256]{1,0:T(8,128)(2,1)S(1)}, bf16[128,256]{1,0:T(8,128)(2,1)S(1)}, u32[]{:S(2)}, u32[]{:S(2)}) %collective-permute-start) | collective-permute-done | bytes 65568 | tf_op jit(solution)/shard_map/ppermute | solution.py:268
  6.8 2.1 %collective-permute-start.1 = (bf16[128,256]{1,0:T(8,128)(2,1)S(1)}, bf16[128,256]{1,0:T(8,128)(2,1)S(1)}, u32[]{:S(2)}, u32[]{:S(2)}) collective-permute-start(bf16[128,256]{1,0:T(8,128)(2,1)S(1)} %collective-permute-done), channel_id=1, source_target_pairs={{0,4},{1,5},{4,8},{5,9},{8,12},{9,13},{12,14},{13,15},{14,10},{15,... | collective-permute-start | bytes 196616 | tf_op jit(solution)/shard_map/ppermute | solution.py:268
  8.9 2.2 %collective-permute-done.1 = bf16[128,256]{1,0:T(8,128)(2,1)S(1)} collective-permute-done((bf16[128,256]{1,0:T(8,128)(2,1)S(1)}, bf16[128,256]{1,0:T(8,128)(2,1)S(1)}, u32[]{:S(2)}, u32[]{:S(2)}) %collective-permute-start.1) | collective-permute-done | bytes 65568 | tf_op jit(solution)/shard_map/ppermute | solution.py:268
  11.1 2.1 %collective-permute-start.2 = (bf16[128,256]{1,0:T(8,128)(2,1)S(1)}, bf16[128,256]{1,0:T(8,128)(2,1)S(1)}, u32[]{:S(2)}, u32[]{:S(2)}) collective-permute-start(bf16[128,256]{1,0:T(8,128)(2,1)S(1)} %collective-permute-done.1), channel_id=1, source_target_pairs={{0,4},{1,5},{4,8},{5,9},{8,12},{9,13},{12,14},{13,15},{14,10},{15,... | collective-permute-start | bytes 196616 | tf_op jit(solution)/shard_map/ppermute | solution.py:268
  13.2 2.8 %collective-permute-done.2 = bf16[128,256]{1,0:T(8,128)(2,1)S(1)} collective-permute-done((bf16[128,256]{1,0:T(8,128)(2,1)S(1)}, bf16[128,256]{1,0:T(8,128)(2,1)S(1)}, u32[]{:S(2)}, u32[]{:S(2)}) %collective-permute-start.2) | collective-permute-done | bytes 65568 | tf_op jit(solution)/shard_map/ppermute | solution.py:268
  16.0 1.8 %collective-permute-start.3 = (bf16[128,256]{1,0:T(8,128)(2,1)S(1)}, bf16[128,256]{1,0:T(8,128)(2,1)S(1)}, u32[]{:S(2)}, u32[]{:S(2)}) collective-permute-start(bf16[128,256]{1,0:T(8,128)(2,1)S(1)} %collective-permute-done.2), channel_id=1, source_target_pairs={{0,4},{1,5},{4,8},{5,9},{8,12},{9,13},{12,14},{13,15},{14,10},{15,... | collective-permute-start | bytes 196616 | tf_op jit(solution)/shard_map/ppermute | solution.py:268
  17.8 2.4 %collective-permute-done.3 = bf16[128,256]{1,0:T(8,128)(2,1)S(1)} collective-permute-done((bf16[128,256]{1,0:T(8,128)(2,1)S(1)}, bf16[128,256]{1,0:T(8,128)(2,1)S(1)}, u32[]{:S(2)}, u32[]{:S(2)}) %collective-permute-start.3) | collective-permute-done | bytes 65568 | tf_op jit(solution)/shard_map/ppermute | solution.py:268
  27.3 2.8 %attend.3 = (bf16[64,2176]{1,0:T(8,128)(2,1)S(1)}, f32[64,2048]{1,0:T(8,128)S(1)}) custom-call(s32[16,10]{1,0:T(8,128)S(1)} %copy-done.8, bf16[128,2048]{1,0:T(8,128)(2,1)S(1)} %copy-done.3, bf16[128,2048]{1,0:T(8,128)(2,1)S(1)} %copy-done.4, bf16[1024,256]{1,0:T(8,128)(2,1)S(1)} %constant_dynamic-update-slice_fusion.2.kv0, ...), custom_call_target="tpu_custom_call" | custom-call | flops 10350000128 | bytes 1048576 | tf_op jit(solution)/shard_map/attend/pallas_call | solution.py:173
  30.1 2.8 %collective-permute-start.25 = (bf16[64,2176]{1,0:T(8,128)(2,1)S(1)}, bf16[64,2176]{1,0:T(8,128)(2,1)S(1)}, u32[]{:S(2)}, u32[]{:S(2)}) collective-permute-start(bf16[64,2176]{1,0:T(8,128)(2,1)S(1)} %get-tuple-element.36.refs_0_), channel_id=1, source_target_pairs={{0,2},{1,3},{4,0},{5,1},{8,4},{9,5},{12,8},{13,9},{14,12},{15,13},... | collective-permute-start | bytes 835592 | tf_op jit(solution)/shard_map/ppermute | solution.py:268
  33.9 2.7 %attend.2 = (bf16[64,2176]{1,0:T(8,128)(2,1)S(1)}, f32[64,2048]{1,0:T(8,128)S(1)}) custom-call(s32[16,10]{1,0:T(8,128)S(1)} %copy-done.8, bf16[128,2048]{1,0:T(8,128)(2,1)S(1)} %copy-done.3, bf16[128,2048]{1,0:T(8,128)(2,1)S(1)} %copy-done.4, bf16[1024,256]{1,0:T(8,128)(2,1)S(1)} %constant_dynamic-update-slice_fusion.2.kv0, ...), custom_call_target="tpu_custom_call" | custom-call | flops 10350000128 | bytes 1048576 | tf_op jit(solution)/shard_map/attend/pallas_call | solution.py:173
  36.6 4.1 %collective-permute-done.25.refs_1_ = bf16[64,2176]{1,0:T(8,128)(2,1)S(1)} collective-permute-done((bf16[64,2176]{1,0:T(8,128)(2,1)S(1)}, bf16[64,2176]{1,0:T(8,128)(2,1)S(1)}, u32[]{:S(2)}, u32[]{:S(2)}) %collective-permute-start.25) | collective-permute-done | bytes 278560 | tf_op jit(solution)/shard_map/ppermute | solution.py:268
  40.8 3.4 %collective-permute-start.8 = (bf16[64,2176]{1,0:T(8,128)(2,1)S(1)}, bf16[64,2176]{1,0:T(8,128)(2,1)S(1)}, u32[]{:S(2)}, u32[]{:S(2)}) collective-permute-start(bf16[64,2176]{1,0:T(8,128)(2,1)S(1)} %get-tuple-element.26.refs_0_), channel_id=1, source_target_pairs={{0,4},{1,5},{4,8},{5,9},{8,12},{9,13},{12,14},{13,15},{14,10},{15,... | collective-permute-start | bytes 835592 | tf_op jit(solution)/shard_map/ppermute | solution.py:268
  44.2 2.6 %collective-permute-start.12 = (bf16[64,2176]{1,0:T(8,128)(2,1)S(1)}, bf16[64,2176]{1,0:T(8,128)(2,1)S(1)}, u32[]{:S(2)}, u32[]{:S(2)}) collective-permute-start(bf16[64,2176]{1,0:T(8,128)(2,1)S(1)} %get-tuple-element.26.refs_0_), channel_id=1, source_target_pairs={{0,2},{1,3},{4,0},{5,1},{8,4},{9,5},{12,8},{13,9},{14,12},{15,13},... | collective-permute-start | bytes 835592 | tf_op jit(solution)/shard_map/ppermute | solution.py:272
  46.8 3.1 %collective-permute-done.8.refs_1_ = bf16[64,2176]{1,0:T(8,128)(2,1)S(1)} collective-permute-done((bf16[64,2176]{1,0:T(8,128)(2,1)S(1)}, bf16[64,2176]{1,0:T(8,128)(2,1)S(1)}, u32[]{:S(2)}, u32[]{:S(2)}) %collective-permute-start.8) | collective-permute-done | bytes 278560 | tf_op jit(solution)/shard_map/ppermute | solution.py:268
  49.9 2.6 %collective-permute-start.26 = (bf16[64,2176]{1,0:T(8,128)(2,1)S(1)}, bf16[64,2176]{1,0:T(8,128)(2,1)S(1)}, u32[]{:S(2)}, u32[]{:S(2)}) collective-permute-start(bf16[64,2176]{1,0:T(8,128)(2,1)S(1)} %collective-permute-done.25.refs_1_), channel_id=1, source_target_pairs={{0,2},{1,3},{4,0},{5,1},{8,4},{9,5},{12,8},{13,9},{14,12},{15,13},... | collective-permute-start | bytes 835592 | tf_op jit(solution)/shard_map/ppermute | solution.py:268
  52.5 2.5 %collective-permute-done.12.refs_5_ = bf16[64,2176]{1,0:T(8,128)(2,1)S(1)} collective-permute-done((bf16[64,2176]{1,0:T(8,128)(2,1)S(1)}, bf16[64,2176]{1,0:T(8,128)(2,1)S(1)}, u32[]{:S(2)}, u32[]{:S(2)}) %collective-permute-start.12) | collective-permute-done | bytes 278560 | tf_op jit(solution)/shard_map/ppermute | solution.py:272
  55.0 3.8 %collective-permute-start.30 = (bf16[64,2176]{1,0:T(8,128)(2,1)S(1)}, bf16[64,2176]{1,0:T(8,128)(2,1)S(1)}, u32[]{:S(2)}, u32[]{:S(2)}) collective-permute-start(bf16[64,2176]{1,0:T(8,128)(2,1)S(1)} %collective-permute-done.29.refs_5_), channel_id=1, source_target_pairs={{0,4},{1,5},{4,8},{5,9},{8,12},{9,13},{12,14},{13,15},{14,10},{15,... | collective-permute-start | bytes 835592 | tf_op jit(solution)/shard_map/ppermute | solution.py:272
  58.8 1.4 collective-permute-done.26.refs_2_
  60.1 4.0 %collective-permute-start.9 = (bf16[64,2176]{1,0:T(8,128)(2,1)S(1)}, bf16[64,2176]{1,0:T(8,128)(2,1)S(1)}, u32[]{:S(2)}, u32[]{:S(2)}) collective-permute-start(bf16[64,2176]{1,0:T(8,128)(2,1)S(1)} %collective-permute-done.8.refs_1_), channel_id=1, source_target_pairs={{0,4},{1,5},{4,8},{5,9},{8,12},{9,13},{12,14},{13,15},{14,10},{15,... | collective-permute-start | bytes 835592 | tf_op jit(solution)/shard_map/ppermute | solution.py:268
  64.5 3.6 %collective-permute-start.13 = (bf16[64,2176]{1,0:T(8,128)(2,1)S(1)}, bf16[64,2176]{1,0:T(8,128)(2,1)S(1)}, u32[]{:S(2)}, u32[]{:S(2)}) collective-permute-start(bf16[64,2176]{1,0:T(8,128)(2,1)S(1)} %collective-permute-done.12.refs_5_), channel_id=1, source_target_pairs={{0,2},{1,3},{4,0},{5,1},{8,4},{9,5},{12,8},{13,9},{14,12},{15,13},... | collective-permute-start | bytes 835592 | tf_op jit(solution)/shard_map/ppermute | solution.py:272
  68.1 1.2 collective-permute-done.9.refs_2_
  69.2 3.3 %collective-permute-start.27 = (bf16[64,2176]{1,0:T(8,128)(2,1)S(1)}, bf16[64,2176]{1,0:T(8,128)(2,1)S(1)}, u32[]{:S(2)}, u32[]{:S(2)}) collective-permute-start(bf16[64,2176]{1,0:T(8,128)(2,1)S(1)} %collective-permute-done.26.refs_2_), channel_id=1, source_target_pairs={{0,2},{1,3},{4,0},{5,1},{8,4},{9,5},{12,8},{13,9},{14,12},{15,13},... | collective-permute-start | bytes 835592 | tf_op jit(solution)/shard_map/ppermute | solution.py:268
  72.6 1.2 collective-permute-done.13.refs_6_
  73.7 1.1 collective-permute-start.31
  74.8 3.5 %collective-permute-done.27.refs_3_ = bf16[64,2176]{1,0:T(8,128)(2,1)S(1)} collective-permute-done((bf16[64,2176]{1,0:T(8,128)(2,1)S(1)}, bf16[64,2176]{1,0:T(8,128)(2,1)S(1)}, u32[]{:S(2)}, u32[]{:S(2)}) %collective-permute-start.27) | collective-permute-done | bytes 278560 | tf_op jit(solution)/shard_map/ppermute | solution.py:268
  78.2 1.7 %collective-permute-start.10 = (bf16[64,2176]{1,0:T(8,128)(2,1)S(1)}, bf16[64,2176]{1,0:T(8,128)(2,1)S(1)}, u32[]{:S(2)}, u32[]{:S(2)}) collective-permute-start(bf16[64,2176]{1,0:T(8,128)(2,1)S(1)} %collective-permute-done.9.refs_2_), channel_id=1, source_target_pairs={{0,4},{1,5},{4,8},{5,9},{8,12},{9,13},{12,14},{13,15},{14,10},{15,... | collective-permute-start | bytes 835592 | tf_op jit(solution)/shard_map/ppermute | solution.py:268
  80.5 1.6 %collective-permute-start.28 = (bf16[64,2176]{1,0:T(8,128)(2,1)S(1)}, bf16[64,2176]{1,0:T(8,128)(2,1)S(1)}, u32[]{:S(2)}, u32[]{:S(2)}) collective-permute-start(bf16[64,2176]{1,0:T(8,128)(2,1)S(1)} %collective-permute-done.27.refs_3_), channel_id=1, source_target_pairs={{0,2},{1,3},{4,0},{5,1},{8,4},{9,5},{12,8},{13,9},{14,12},{15,13},... | collective-permute-start | bytes 835592 | tf_op jit(solution)/shard_map/ppermute | solution.py:268
  82.1 4.1 %collective-permute-done.10.refs_3_ = bf16[64,2176]{1,0:T(8,128)(2,1)S(1)} collective-permute-done((bf16[64,2176]{1,0:T(8,128)(2,1)S(1)}, bf16[64,2176]{1,0:T(8,128)(2,1)S(1)}, u32[]{:S(2)}, u32[]{:S(2)}) %collective-permute-start.10) | collective-permute-done | bytes 278560 | tf_op jit(solution)/shard_map/ppermute | solution.py:268
  86.2 1.7 %collective-permute-start.14 = (bf16[64,2176]{1,0:T(8,128)(2,1)S(1)}, bf16[64,2176]{1,0:T(8,128)(2,1)S(1)}, u32[]{:S(2)}, u32[]{:S(2)}) collective-permute-start(bf16[64,2176]{1,0:T(8,128)(2,1)S(1)} %collective-permute-done.13.refs_6_), channel_id=1, source_target_pairs={{0,2},{1,3},{4,0},{5,1},{8,4},{9,5},{12,8},{13,9},{14,12},{15,13},... | collective-permute-start | bytes 835592 | tf_op jit(solution)/shard_map/ppermute | solution.py:272
  88.9 5.1 %experts.6.refs_8_ = bf16[512,2048]{1,0:T(8,128)(2,1)S(1)} custom-call(bf16[64,2176]{1,0:T(8,128)(2,1)S(1)} %get-tuple-element.36.refs_0_, bf16[64,2176]{1,0:T(8,128)(2,1)S(1)} %collective-permute-done.25.refs_1_, bf16[64,2176]{1,0:T(8,128)(2,1)S(1)} %collective-permute-done.26.refs_2_, bf16[64,2176]{1,0:T(8,128)(2,1)S(1)} %collective-permute-done.27.refs_3_, ...), custom_call_target="tpu_custom_call" | custom-call | flops 6899999744 | bytes 1048576 | tf_op jit(solution)/shard_map/experts/pallas_call | solution.py:238
  94.5 5.1 %experts.4.refs_8_ = bf16[512,2048]{1,0:T(8,128)(2,1)S(1)} custom-call(bf16[64,2176]{1,0:T(8,128)(2,1)S(1)} %get-tuple-element.26.refs_0_, bf16[64,2176]{1,0:T(8,128)(2,1)S(1)} %collective-permute-done.8.refs_1_, bf16[64,2176]{1,0:T(8,128)(2,1)S(1)} %collective-permute-done.9.refs_2_, bf16[64,2176]{1,0:T(8,128)(2,1)S(1)} %collective-permute-done.10.refs_3_, ...), custom_call_target="tpu_custom_call" | custom-call | flops 6899999744 | bytes 1048576 | tf_op jit(solution)/shard_map/experts/pallas_call | solution.py:238
  99.6 5.3 %experts.7 = (bf16[64,2048]{1,0:T(8,128)(2,1)S(1)}, bf16[64,2048]{1,0:T(8,128)(2,1)S(1)}, bf16[64,2048]{1,0:T(8,128)(2,1)S(1)}, bf16[64,2048]{1,0:T(8,128)(2,1)S...) custom-call(bf16[64,2176]{1,0:T(8,128)(2,1)S(1)} %get-tuple-element., ...), custom_call_target="tpu_custom_call" | custom-call | flops 6899999744 | bytes 1048576 | tf_op jit(solution)/shard_map/experts/pallas_call | solution.py:238
  104.8 1.5 %collective-permute-start.36 = (bf16[64,2048]{1,0:T(8,128)(2,1)S(1)}, bf16[64,2048]{1,0:T(8,128)(2,1)S(1)}, u32[]{:S(2)}, u32[]{:S(2)}) collective-permute-start(bf16[64,2048]{1,0:T(8,128)(2,1)S(1)} %get-tuple-element.42), channel_id=1, source_target_pairs={{0,4},{1,5},{4,8},{5,9},{8,12},{9,13},{12,14},{13,15},{14,10},{15,... | collective-permute-start | bytes 786440 | tf_op jit(solution)/shard_map/ppermute | solution.py:284
  106.9 5.2 %experts.5 = (bf16[64,2048]{1,0:T(8,128)(2,1)S(1)}, bf16[64,2048]{1,0:T(8,128)(2,1)S(1)}, bf16[64,2048]{1,0:T(8,128)(2,1)S(1)}, bf16[64,2048]{1,0:T(8,128)(2,1)S...) custom-call(bf16[64,2176]{1,0:T(8,128)(2,1)S(1)} %get-tuple-element., ...), custom_call_target="tpu_custom_call" | custom-call | flops 6899999744 | bytes 1048576 | tf_op jit(solution)/shard_map/experts/pallas_call | solution.py:238
  112.2 1.3 collective-permute-start.22
  114.3 1.9 %collective-permute-start.37 = (bf16[64,2048]{1,0:T(8,128)(2,1)S(1)}, bf16[64,2048]{1,0:T(8,128)(2,1)S(1)}, u32[]{:S(2)}, u32[]{:S(2)}) collective-permute-start(bf16[64,2048]{1,0:T(8,128)(2,1)S(1)} %add_convert_fusion.2), channel_id=1, source_target_pairs={{0,4},{1,5},{4,8},{5,9},{8,12},{9,13},{12,14},{13,15},{14,10},{15,... | collective-permute-start | bytes 786440 | tf_op jit(solution)/shard_map/ppermute | solution.py:284
  116.5 4.9 %collective-permute-done.22 = bf16[64,2048]{1,0:T(8,128)(2,1)S(1)} collective-permute-done((bf16[64,2048]{1,0:T(8,128)(2,1)S(1)}, bf16[64,2048]{1,0:T(8,128)(2,1)S(1)}, u32[]{:S(2)}, u32[]{:S(2)}) %collective-permute-start.22) | collective-permute-done | bytes 262176 | tf_op jit(solution)/shard_map/ppermute | solution.py:284
  121.5 1.3 collective-permute-start.23
  123.7 4.4 %collective-permute-done.37 = bf16[64,2048]{1,0:T(8,128)(2,1)S(1)} collective-permute-done((bf16[64,2048]{1,0:T(8,128)(2,1)S(1)}, bf16[64,2048]{1,0:T(8,128)(2,1)S(1)}, u32[]{:S(2)}, u32[]{:S(2)}) %collective-permute-start.37) | collective-permute-done | bytes 262176 | tf_op jit(solution)/shard_map/ppermute | solution.py:284
  128.4 2.1 %collective-permute-start.34 = (bf16[64,2048]{1,0:T(8,128)(2,1)S(1)}, bf16[64,2048]{1,0:T(8,128)(2,1)S(1)}, u32[]{:S(2)}, u32[]{:S(2)}) collective-permute-start(bf16[64,2048]{1,0:T(8,128)(2,1)S(1)} %add_convert_fusion.4), channel_id=1, source_target_pairs={{0,2},{1,3},{4,0},{5,1},{8,4},{9,5},{12,8},{13,9},{14,12},{15,13},... | collective-permute-start | bytes 786440 | tf_op jit(solution)/shard_map/ppermute | solution.py:280
  130.5 2.2 %collective-permute-done.23 = bf16[64,2048]{1,0:T(8,128)(2,1)S(1)} collective-permute-done((bf16[64,2048]{1,0:T(8,128)(2,1)S(1)}, bf16[64,2048]{1,0:T(8,128)(2,1)S(1)}, u32[]{:S(2)}, u32[]{:S(2)}) %collective-permute-start.23) | collective-permute-done | bytes 262176 | tf_op jit(solution)/shard_map/ppermute | solution.py:284
  132.8 1.3 collective-permute-start.24
  135.0 3.3 %collective-permute-done.34 = bf16[64,2048]{1,0:T(8,128)(2,1)S(1)} collective-permute-done((bf16[64,2048]{1,0:T(8,128)(2,1)S(1)}, bf16[64,2048]{1,0:T(8,128)(2,1)S(1)}, u32[]{:S(2)}, u32[]{:S(2)}) %collective-permute-start.34) | collective-permute-done | bytes 262176 | tf_op jit(solution)/shard_map/ppermute | solution.py:280
  138.4 1.5 collective-permute-start.35
  139.9 2.8 %collective-permute-done.20 = bf16[64,2048]{1,0:T(8,128)(2,1)S(1)} collective-permute-done((bf16[64,2048]{1,0:T(8,128)(2,1)S(1)}, bf16[64,2048]{1,0:T(8,128)(2,1)S(1)}, u32[]{:S(2)}, u32[]{:S(2)}) %collective-permute-start.20) | collective-permute-done | bytes 262176 | tf_op jit(solution)/shard_map/ppermute | solution.py:280
  142.8 3.9 %collective-permute-done.35 = bf16[64,2048]{1,0:T(8,128)(2,1)S(1)} collective-permute-done((bf16[64,2048]{1,0:T(8,128)(2,1)S(1)}, bf16[64,2048]{1,0:T(8,128)(2,1)S(1)}, u32[]{:S(2)}, u32[]{:S(2)}) %collective-permute-start.35) | collective-permute-done | bytes 262176 | tf_op jit(solution)/shard_map/ppermute | solution.py:281
  146.9 2.9 %collective-permute-done.21 = bf16[64,2048]{1,0:T(8,128)(2,1)S(1)} collective-permute-done((bf16[64,2048]{1,0:T(8,128)(2,1)S(1)}, bf16[64,2048]{1,0:T(8,128)(2,1)S(1)}, u32[]{:S(2)}, u32[]{:S(2)}) %collective-permute-start.21) | collective-permute-done | bytes 262176 | tf_op jit(solution)/shard_map/ppermute | solution.py:281
  (76 shorter events, 16.9 us)
Async XLA Ops:
  1.6 5.3 %collective-permute-start = (bf16[128,256]{1,0:T(8,128)(2,1)S(1)}, bf16[128,256]{1,0:T(8,128)(2,1)S(1)}, u32[]{:S(2)}, u32[]{:S(2)}) collective-permute-start(bf16[128,256]{1,0:T(8,128)(2,1)S(1)} %get-tuple-element.45), channel_id=1, source_target_pairs={{0,4},{1,5},{4,8},{5,9},{8,12},{9,13},{12,14},{13,15},{14,10},{15,... | collective-permute-start | bytes 196616 | tf_op jit(solution)/shard_map/ppermute | solution.py:268
  4.6 4.3 %collective-permute-start.4 = (bf16[128,256]{1,0:T(8,128)(2,1)S(1)}, bf16[128,256]{1,0:T(8,128)(2,1)S(1)}, u32[]{:S(2)}, u32[]{:S(2)}) collective-permute-start(bf16[128,256]{1,0:T(8,128)(2,1)S(1)} %get-tuple-element.45), channel_id=1, source_target_pairs={{0,2},{1,3},{4,0},{5,1},{8,4},{9,5},{12,8},{13,9},{14,12},{15,13},... | collective-permute-start | bytes 196616 | tf_op jit(solution)/shard_map/ppermute | solution.py:272
  6.8 4.3 %collective-permute-start.1 = (bf16[128,256]{1,0:T(8,128)(2,1)S(1)}, bf16[128,256]{1,0:T(8,128)(2,1)S(1)}, u32[]{:S(2)}, u32[]{:S(2)}) collective-permute-start(bf16[128,256]{1,0:T(8,128)(2,1)S(1)} %collective-permute-done), channel_id=1, source_target_pairs={{0,4},{1,5},{4,8},{5,9},{8,12},{9,13},{12,14},{13,15},{14,10},{15,... | collective-permute-start | bytes 196616 | tf_op jit(solution)/shard_map/ppermute | solution.py:268
  8.9 4.3 %collective-permute-start.5 = (bf16[128,256]{1,0:T(8,128)(2,1)S(1)}, bf16[128,256]{1,0:T(8,128)(2,1)S(1)}, u32[]{:S(2)}, u32[]{:S(2)}) collective-permute-start(bf16[128,256]{1,0:T(8,128)(2,1)S(1)} %collective-permute-done.4), channel_id=1, source_target_pairs={{0,2},{1,3},{4,0},{5,1},{8,4},{9,5},{12,8},{13,9},{14,12},{15,13},... | collective-permute-start | bytes 196616 | tf_op jit(solution)/shard_map/ppermute | solution.py:272
  11.1 4.9 %collective-permute-start.2 = (bf16[128,256]{1,0:T(8,128)(2,1)S(1)}, bf16[128,256]{1,0:T(8,128)(2,1)S(1)}, u32[]{:S(2)}, u32[]{:S(2)}) collective-permute-start(bf16[128,256]{1,0:T(8,128)(2,1)S(1)} %collective-permute-done.1), channel_id=1, source_target_pairs={{0,4},{1,5},{4,8},{5,9},{8,12},{9,13},{12,14},{13,15},{14,10},{15,... | collective-permute-start | bytes 196616 | tf_op jit(solution)/shard_map/ppermute | solution.py:268
  13.2 7.1 %collective-permute-start.6 = (bf16[128,256]{1,0:T(8,128)(2,1)S(1)}, bf16[128,256]{1,0:T(8,128)(2,1)S(1)}, u32[]{:S(2)}, u32[]{:S(2)}) collective-permute-start(bf16[128,256]{1,0:T(8,128)(2,1)S(1)} %collective-permute-done.5), channel_id=1, source_target_pairs={{0,2},{1,3},{4,0},{5,1},{8,4},{9,5},{12,8},{13,9},{14,12},{15,13},... | collective-permute-start | bytes 196616 | tf_op jit(solution)/shard_map/ppermute | solution.py:272
  16.0 4.3 %collective-permute-start.3 = (bf16[128,256]{1,0:T(8,128)(2,1)S(1)}, bf16[128,256]{1,0:T(8,128)(2,1)S(1)}, u32[]{:S(2)}, u32[]{:S(2)}) collective-permute-start(bf16[128,256]{1,0:T(8,128)(2,1)S(1)} %collective-permute-done.2), channel_id=1, source_target_pairs={{0,4},{1,5},{4,8},{5,9},{8,12},{9,13},{12,14},{13,15},{14,10},{15,... | collective-permute-start | bytes 196616 | tf_op jit(solution)/shard_map/ppermute | solution.py:268
  20.3 2.0 %collective-permute-start.7 = (bf16[1024,256]{1,0:T(8,128)(2,1)S(1)}, bf16[1024,256]{1,0:T(8,128)(2,1)S(1)}, u32[]{:S(2)}, u32[]{:S(2)}) collective-permute-start(bf16[1024,256]{1,0:T(8,128)(2,1)S(1)} %constant_dynamic-update-slice_fusion.2.kv0), channel_id=1, source_target_pairs={{0,1},{1,0},{2,3},{3,2},{4,5},{5,4},{6,7},{7,6},{8,9},{9,8},{10,11... | collective-permute-start | bytes 1572872 | tf_op jit(solution)/shard_map/ppermute | solution.py:300
  20.4 79.2 %collective-permute-start.15 = (bf16[1,2048,768]{2,1,0:T(8,128)(2,1)}, bf16[1,2048,768]{2,1,0:T(8,128)(2,1)S(1)}, u32[]{:S(2)}, u32[]{:S(2)}) collective-permute-start(bf16[1,2048,768]{2,1,0:T(8,128)(2,1)} %refs_8_.3), channel_id=1, source_target_pairs={{0,1},{1,0},{2,3},{3,2},{4,5},{5,4},{6,7},{7,6},{8,9},{9,8},{10,11... | collective-permute-start | bytes 9437192 | tf_op jit(solution)/shard_map/ppermute | solution.py:302
  20.9 78.7 %collective-permute-start.16 = (bf16[1,2048,768]{2,1,0:T(8,128)(2,1)}, bf16[1,2048,768]{2,1,0:T(8,128)(2,1)S(1)}, u32[]{:S(2)}, u32[]{:S(2)}) collective-permute-start(bf16[1,2048,768]{2,1,0:T(8,128)(2,1)} %refs_9_.3), channel_id=1, source_target_pairs={{0,1},{1,0},{2,3},{3,2},{4,5},{5,4},{6,7},{7,6},{8,9},{9,8},{10,11... | collective-permute-start | bytes 9437192 | tf_op jit(solution)/shard_map/ppermute | solution.py:302
  21.0 78.6 %collective-permute-start.17 = (bf16[1,768,2048]{2,1,0:T(8,128)(2,1)}, bf16[1,768,2048]{2,1,0:T(8,128)(2,1)S(1)}, u32[]{:S(2)}, u32[]{:S(2)}) collective-permute-start(bf16[1,768,2048]{2,1,0:T(8,128)(2,1)} %refs_10_.3), channel_id=1, source_target_pairs={{0,1},{1,0},{2,3},{3,2},{4,5},{5,4},{6,7},{7,6},{8,9},{9,8},{10,11... | collective-permute-start | bytes 9437192 | tf_op jit(solution)/shard_map/ppermute | solution.py:302
  22.3 1.0 copy-start.3
  23.3 1.0 copy-start.4
  24.4 0.8 copy-start.5
  25.2 0.7 copy-start.6
  25.9 0.7 copy-start.7
  26.6 0.7 copy-start.8
  30.0 58.8 %copy-start = (bf16[1,2048,768]{2,1,0:T(8,128)(2,1)S(1)}, bf16[1,2048,768]{2,1,0:T(8,128)(2,1)}, u32[]{:S(2)}) copy-start(bf16[1,2048,768]{2,1,0:T(8,128)(2,1)} %refs_8_.3) | copy-start | bytes 9437188
  30.0 58.8 %copy-start.1 = (bf16[1,2048,768]{2,1,0:T(8,128)(2,1)S(1)}, bf16[1,2048,768]{2,1,0:T(8,128)(2,1)}, u32[]{:S(2)}) copy-start(bf16[1,2048,768]{2,1,0:T(8,128)(2,1)} %refs_9_.3) | copy-start | bytes 9437188
  30.1 58.8 %copy-start.2 = (bf16[1,768,2048]{2,1,0:T(8,128)(2,1)S(1)}, bf16[1,768,2048]{2,1,0:T(8,128)(2,1)}, u32[]{:S(2)}) copy-start(bf16[1,768,2048]{2,1,0:T(8,128)(2,1)} %refs_10_.3) | copy-start | bytes 9437188
  30.1 10.7 %collective-permute-start.25 = (bf16[64,2176]{1,0:T(8,128)(2,1)S(1)}, bf16[64,2176]{1,0:T(8,128)(2,1)S(1)}, u32[]{:S(2)}, u32[]{:S(2)}) collective-permute-start(bf16[64,2176]{1,0:T(8,128)(2,1)S(1)} %get-tuple-element.36.refs_0_), channel_id=1, source_target_pairs={{0,2},{1,3},{4,0},{5,1},{8,4},{9,5},{12,8},{13,9},{14,12},{15,13},... | collective-permute-start | bytes 835592 | tf_op jit(solution)/shard_map/ppermute | solution.py:268
  32.8 11.4 %collective-permute-start.29 = (bf16[64,2176]{1,0:T(8,128)(2,1)S(1)}, bf16[64,2176]{1,0:T(8,128)(2,1)S(1)}, u32[]{:S(2)}, u32[]{:S(2)}) collective-permute-start(bf16[64,2176]{1,0:T(8,128)(2,1)S(1)} %get-tuple-element.36.refs_0_), channel_id=1, source_target_pairs={{0,4},{1,5},{4,8},{5,9},{8,12},{9,13},{12,14},{13,15},{14,10},{15,... | collective-permute-start | bytes 835592 | tf_op jit(solution)/shard_map/ppermute | solution.py:272
  40.8 9.2 %collective-permute-start.8 = (bf16[64,2176]{1,0:T(8,128)(2,1)S(1)}, bf16[64,2176]{1,0:T(8,128)(2,1)S(1)}, u32[]{:S(2)}, u32[]{:S(2)}) collective-permute-start(bf16[64,2176]{1,0:T(8,128)(2,1)S(1)} %get-tuple-element.26.refs_0_), channel_id=1, source_target_pairs={{0,4},{1,5},{4,8},{5,9},{8,12},{9,13},{12,14},{13,15},{14,10},{15,... | collective-permute-start | bytes 835592 | tf_op jit(solution)/shard_map/ppermute | solution.py:268
  44.2 10.7 %collective-permute-start.12 = (bf16[64,2176]{1,0:T(8,128)(2,1)S(1)}, bf16[64,2176]{1,0:T(8,128)(2,1)S(1)}, u32[]{:S(2)}, u32[]{:S(2)}) collective-permute-start(bf16[64,2176]{1,0:T(8,128)(2,1)S(1)} %get-tuple-element.26.refs_0_), channel_id=1, source_target_pairs={{0,2},{1,3},{4,0},{5,1},{8,4},{9,5},{12,8},{13,9},{14,12},{15,13},... | collective-permute-start | bytes 835592 | tf_op jit(solution)/shard_map/ppermute | solution.py:272
  49.9 10.2 %collective-permute-start.26 = (bf16[64,2176]{1,0:T(8,128)(2,1)S(1)}, bf16[64,2176]{1,0:T(8,128)(2,1)S(1)}, u32[]{:S(2)}, u32[]{:S(2)}) collective-permute-start(bf16[64,2176]{1,0:T(8,128)(2,1)S(1)} %collective-permute-done.25.refs_1_), channel_id=1, source_target_pairs={{0,2},{1,3},{4,0},{5,1},{8,4},{9,5},{12,8},{13,9},{14,12},{15,13},... | collective-permute-start | bytes 835592 | tf_op jit(solution)/shard_map/ppermute | solution.py:268
  55.0 9.5 %collective-permute-start.30 = (bf16[64,2176]{1,0:T(8,128)(2,1)S(1)}, bf16[64,2176]{1,0:T(8,128)(2,1)S(1)}, u32[]{:S(2)}, u32[]{:S(2)}) collective-permute-start(bf16[64,2176]{1,0:T(8,128)(2,1)S(1)} %collective-permute-done.29.refs_5_), channel_id=1, source_target_pairs={{0,4},{1,5},{4,8},{5,9},{8,12},{9,13},{12,14},{13,15},{14,10},{15,... | collective-permute-start | bytes 835592 | tf_op jit(solution)/shard_map/ppermute | solution.py:272
  60.1 9.1 %collective-permute-start.9 = (bf16[64,2176]{1,0:T(8,128)(2,1)S(1)}, bf16[64,2176]{1,0:T(8,128)(2,1)S(1)}, u32[]{:S(2)}, u32[]{:S(2)}) collective-permute-start(bf16[64,2176]{1,0:T(8,128)(2,1)S(1)} %collective-permute-done.8.refs_1_), channel_id=1, source_target_pairs={{0,4},{1,5},{4,8},{5,9},{8,12},{9,13},{12,14},{13,15},{14,10},{15,... | collective-permute-start | bytes 835592 | tf_op jit(solution)/shard_map/ppermute | solution.py:268
  64.5 9.3 %collective-permute-start.13 = (bf16[64,2176]{1,0:T(8,128)(2,1)S(1)}, bf16[64,2176]{1,0:T(8,128)(2,1)S(1)}, u32[]{:S(2)}, u32[]{:S(2)}) collective-permute-start(bf16[64,2176]{1,0:T(8,128)(2,1)S(1)} %collective-permute-done.12.refs_5_), channel_id=1, source_target_pairs={{0,2},{1,3},{4,0},{5,1},{8,4},{9,5},{12,8},{13,9},{14,12},{15,13},... | collective-permute-start | bytes 835592 | tf_op jit(solution)/shard_map/ppermute | solution.py:272
  69.2 9.0 %collective-permute-start.27 = (bf16[64,2176]{1,0:T(8,128)(2,1)S(1)}, bf16[64,2176]{1,0:T(8,128)(2,1)S(1)}, u32[]{:S(2)}, u32[]{:S(2)}) collective-permute-start(bf16[64,2176]{1,0:T(8,128)(2,1)S(1)} %collective-permute-done.26.refs_2_), channel_id=1, source_target_pairs={{0,2},{1,3},{4,0},{5,1},{8,4},{9,5},{12,8},{13,9},{14,12},{15,13},... | collective-permute-start | bytes 835592 | tf_op jit(solution)/shard_map/ppermute | solution.py:268
  73.7 6.8 %collective-permute-start.31 = (bf16[64,2176]{1,0:T(8,128)(2,1)S(1)}, bf16[64,2176]{1,0:T(8,128)(2,1)S(1)}, u32[]{:S(2)}, u32[]{:S(2)}) collective-permute-start(bf16[64,2176]{1,0:T(8,128)(2,1)S(1)} %collective-permute-done.30.refs_6_), channel_id=1, source_target_pairs={{0,4},{1,5},{4,8},{5,9},{8,12},{9,13},{12,14},{13,15},{14,10},{15,... | collective-permute-start | bytes 835592 | tf_op jit(solution)/shard_map/ppermute | solution.py:272
  78.2 8.0 %collective-permute-start.10 = (bf16[64,2176]{1,0:T(8,128)(2,1)S(1)}, bf16[64,2176]{1,0:T(8,128)(2,1)S(1)}, u32[]{:S(2)}, u32[]{:S(2)}) collective-permute-start(bf16[64,2176]{1,0:T(8,128)(2,1)S(1)} %collective-permute-done.9.refs_2_), channel_id=1, source_target_pairs={{0,4},{1,5},{4,8},{5,9},{8,12},{9,13},{12,14},{13,15},{14,10},{15,... | collective-permute-start | bytes 835592 | tf_op jit(solution)/shard_map/ppermute | solution.py:268
  80.5 7.5 %collective-permute-start.28 = (bf16[64,2176]{1,0:T(8,128)(2,1)S(1)}, bf16[64,2176]{1,0:T(8,128)(2,1)S(1)}, u32[]{:S(2)}, u32[]{:S(2)}) collective-permute-start(bf16[64,2176]{1,0:T(8,128)(2,1)S(1)} %collective-permute-done.27.refs_3_), channel_id=1, source_target_pairs={{0,2},{1,3},{4,0},{5,1},{8,4},{9,5},{12,8},{13,9},{14,12},{15,13},... | collective-permute-start | bytes 835592 | tf_op jit(solution)/shard_map/ppermute | solution.py:268
  86.2 7.7 %collective-permute-start.14 = (bf16[64,2176]{1,0:T(8,128)(2,1)S(1)}, bf16[64,2176]{1,0:T(8,128)(2,1)S(1)}, u32[]{:S(2)}, u32[]{:S(2)}) collective-permute-start(bf16[64,2176]{1,0:T(8,128)(2,1)S(1)} %collective-permute-done.13.refs_6_), channel_id=1, source_target_pairs={{0,2},{1,3},{4,0},{5,1},{8,4},{9,5},{12,8},{13,9},{14,12},{15,13},... | collective-permute-start | bytes 835592 | tf_op jit(solution)/shard_map/ppermute | solution.py:272
  87.9 6.5 %collective-permute-start.11 = (bf16[64,2176]{1,0:T(8,128)(2,1)S(1)}, bf16[64,2176]{1,0:T(8,128)(2,1)S(1)}, u32[]{:S(2)}, u32[]{:S(2)}) collective-permute-start(bf16[64,2176]{1,0:T(8,128)(2,1)S(1)} %collective-permute-done.10.refs_3_), channel_id=1, source_target_pairs={{0,4},{1,5},{4,8},{5,9},{8,12},{9,13},{12,14},{13,15},{14,10},{15,... | collective-permute-start | bytes 835592 | tf_op jit(solution)/shard_map/ppermute | solution.py:268
  104.8 9.4 %collective-permute-start.36 = (bf16[64,2048]{1,0:T(8,128)(2,1)S(1)}, bf16[64,2048]{1,0:T(8,128)(2,1)S(1)}, u32[]{:S(2)}, u32[]{:S(2)}) collective-permute-start(bf16[64,2048]{1,0:T(8,128)(2,1)S(1)} %get-tuple-element.42), channel_id=1, source_target_pairs={{0,4},{1,5},{4,8},{5,9},{8,12},{9,13},{12,14},{13,15},{14,10},{15,... | collective-permute-start | bytes 786440 | tf_op jit(solution)/shard_map/ppermute | solution.py:284
  106.4 9.8 %collective-permute-start.32 = (bf16[64,2048]{1,0:T(8,128)(2,1)S(1)}, bf16[64,2048]{1,0:T(8,128)(2,1)S(1)}, u32[]{:S(2)}, u32[]{:S(2)}) collective-permute-start(bf16[64,2048]{1,0:T(8,128)(2,1)S(1)} %get-tuple-element.38), channel_id=1, source_target_pairs={{0,2},{1,3},{4,0},{5,1},{8,4},{9,5},{12,8},{13,9},{14,12},{15,13},... | collective-permute-start | bytes 786440 | tf_op jit(solution)/shard_map/ppermute | solution.py:280
  112.2 9.3 %collective-permute-start.22 = (bf16[64,2048]{1,0:T(8,128)(2,1)S(1)}, bf16[64,2048]{1,0:T(8,128)(2,1)S(1)}, u32[]{:S(2)}, u32[]{:S(2)}) collective-permute-start(bf16[64,2048]{1,0:T(8,128)(2,1)S(1)} %get-tuple-element.32), channel_id=1, source_target_pairs={{0,2},{1,3},{4,0},{5,1},{8,4},{9,5},{12,8},{13,9},{14,12},{15,13},... | collective-permute-start | bytes 786440 | tf_op jit(solution)/shard_map/ppermute | solution.py:284
  113.5 9.4 %collective-permute-start.18 = (bf16[64,2048]{1,0:T(8,128)(2,1)S(1)}, bf16[64,2048]{1,0:T(8,128)(2,1)S(1)}, u32[]{:S(2)}, u32[]{:S(2)}) collective-permute-start(bf16[64,2048]{1,0:T(8,128)(2,1)S(1)} %get-tuple-element.28), channel_id=1, source_target_pairs={{0,4},{1,5},{4,8},{5,9},{8,12},{9,13},{12,14},{13,15},{14,10},{15,... | collective-permute-start | bytes 786440 | tf_op jit(solution)/shard_map/ppermute | solution.py:280
  114.3 13.9 %collective-permute-start.37 = (bf16[64,2048]{1,0:T(8,128)(2,1)S(1)}, bf16[64,2048]{1,0:T(8,128)(2,1)S(1)}, u32[]{:S(2)}, u32[]{:S(2)}) collective-permute-start(bf16[64,2048]{1,0:T(8,128)(2,1)S(1)} %add_convert_fusion.2), channel_id=1, source_target_pairs={{0,4},{1,5},{4,8},{5,9},{8,12},{9,13},{12,14},{13,15},{14,10},{15,... | collective-permute-start | bytes 786440 | tf_op jit(solution)/shard_map/ppermute | solution.py:284
  116.3 12.0 %collective-permute-start.33 = (bf16[64,2048]{1,0:T(8,128)(2,1)S(1)}, bf16[64,2048]{1,0:T(8,128)(2,1)S(1)}, u32[]{:S(2)}, u32[]{:S(2)}) collective-permute-start(bf16[64,2048]{1,0:T(8,128)(2,1)S(1)} %add_convert_fusion.5), channel_id=1, source_target_pairs={{0,2},{1,3},{4,0},{5,1},{8,4},{9,5},{12,8},{13,9},{14,12},{15,13},... | collective-permute-start | bytes 786440 | tf_op jit(solution)/shard_map/ppermute | solution.py:280
  121.5 11.2 %collective-permute-start.23 = (bf16[64,2048]{1,0:T(8,128)(2,1)S(1)}, bf16[64,2048]{1,0:T(8,128)(2,1)S(1)}, u32[]{:S(2)}, u32[]{:S(2)}) collective-permute-start(bf16[64,2048]{1,0:T(8,128)(2,1)S(1)} %add_convert_fusion.8), channel_id=1, source_target_pairs={{0,2},{1,3},{4,0},{5,1},{8,4},{9,5},{12,8},{13,9},{14,12},{15,13},... | collective-permute-start | bytes 786440 | tf_op jit(solution)/shard_map/ppermute | solution.py:284
  122.9 11.2 %collective-permute-start.19 = (bf16[64,2048]{1,0:T(8,128)(2,1)S(1)}, bf16[64,2048]{1,0:T(8,128)(2,1)S(1)}, u32[]{:S(2)}, u32[]{:S(2)}) collective-permute-start(bf16[64,2048]{1,0:T(8,128)(2,1)S(1)} %add_convert_fusion.11), channel_id=1, source_target_pairs={{0,4},{1,5},{4,8},{5,9},{8,12},{9,13},{12,14},{13,15},{14,10},{15,... | collective-permute-start | bytes 786440 | tf_op jit(solution)/shard_map/ppermute | solution.py:280
  128.2 14.5 %collective-permute-start.38 = (bf16[64,2048]{1,0:T(8,128)(2,1)S(1)}, bf16[64,2048]{1,0:T(8,128)(2,1)S(1)}, u32[]{:S(2)}, u32[]{:S(2)}) collective-permute-start(bf16[64,2048]{1,0:T(8,128)(2,1)S(1)} %add_convert_fusion.1), channel_id=1, source_target_pairs={{0,4},{1,5},{4,8},{5,9},{8,12},{9,13},{12,14},{13,15},{14,10},{15,... | collective-permute-start | bytes 786440 | tf_op jit(solution)/shard_map/ppermute | solution.py:285
  128.4 9.9 %collective-permute-start.34 = (bf16[64,2048]{1,0:T(8,128)(2,1)S(1)}, bf16[64,2048]{1,0:T(8,128)(2,1)S(1)}, u32[]{:S(2)}, u32[]{:S(2)}) collective-permute-start(bf16[64,2048]{1,0:T(8,128)(2,1)S(1)} %add_convert_fusion.4), channel_id=1, source_target_pairs={{0,2},{1,3},{4,0},{5,1},{8,4},{9,5},{12,8},{13,9},{14,12},{15,13},... | collective-permute-start | bytes 786440 | tf_op jit(solution)/shard_map/ppermute | solution.py:280
  132.8 14.1 %collective-permute-start.24 = (bf16[64,2048]{1,0:T(8,128)(2,1)S(1)}, bf16[64,2048]{1,0:T(8,128)(2,1)S(1)}, u32[]{:S(2)}, u32[]{:S(2)}) collective-permute-start(bf16[64,2048]{1,0:T(8,128)(2,1)S(1)} %add_convert_fusion.7), channel_id=1, source_target_pairs={{0,2},{1,3},{4,0},{5,1},{8,4},{9,5},{12,8},{13,9},{14,12},{15,13},... | collective-permute-start | bytes 786440 | tf_op jit(solution)/shard_map/ppermute | solution.py:285
  134.2 8.5 %collective-permute-start.20 = (bf16[64,2048]{1,0:T(8,128)(2,1)S(1)}, bf16[64,2048]{1,0:T(8,128)(2,1)S(1)}, u32[]{:S(2)}, u32[]{:S(2)}) collective-permute-start(bf16[64,2048]{1,0:T(8,128)(2,1)S(1)} %add_convert_fusion.10), channel_id=1, source_target_pairs={{0,4},{1,5},{4,8},{5,9},{8,12},{9,13},{12,14},{13,15},{14,10},{15,... | collective-permute-start | bytes 786440 | tf_op jit(solution)/shard_map/ppermute | solution.py:280
  138.4 8.4 %collective-permute-start.35 = (bf16[64,2048]{1,0:T(8,128)(2,1)S(1)}, bf16[64,2048]{1,0:T(8,128)(2,1)S(1)}, u32[]{:S(2)}, u32[]{:S(2)}) collective-permute-start(bf16[64,2048]{1,0:T(8,128)(2,1)S(1)} %add_convert_fusion.3), channel_id=1, source_target_pairs={{0,2},{1,3},{4,0},{5,1},{8,4},{9,5},{12,8},{13,9},{14,12},{15,13},... | collective-permute-start | bytes 786440 | tf_op jit(solution)/shard_map/ppermute | solution.py:281
  142.7 7.1 %collective-permute-start.21 = (bf16[64,2048]{1,0:T(8,128)(2,1)S(1)}, bf16[64,2048]{1,0:T(8,128)(2,1)S(1)}, u32[]{:S(2)}, u32[]{:S(2)}) collective-permute-start(bf16[64,2048]{1,0:T(8,128)(2,1)S(1)} %add_convert_fusion.9), channel_id=1, source_target_pairs={{0,4},{1,5},{4,8},{5,9},{8,12},{9,13},{12,14},{13,15},{14,10},{15,... | collective-permute-start | bytes 786440 | tf_op jit(solution)/shard_map/ppermute | solution.py:281

commit v3 on v2

v3 whole, which is shorter than its diff:
```python
import functools

import jax
import jax.numpy as jnp
from jax import lax
from jax.experimental import pallas as pl
from jax.experimental.pallas import tpu as pltpu
from jax.sharding import PartitionSpec as P

D = 2048
HEAD_DIM = 64
KV_HEADS = 2
TOP = 4
LANES = 128
PARTS = 2
BF = jnp.bfloat16
F32 = jnp.float32
MIB = 1024 * 1024
LIGHT = pl.CostEstimate(flops=1 << 20, bytes_accessed=1 << 16, transcendentals=0)


def chip_ring(chips):
    if chips == 8:
        return [0, 2, 4, 6, 7, 5, 3, 1]
    return list(range(chips))


def ring_perm(ring, step):
    chips = len(ring)
    return [
        (ring[i] * 2 + core, ring[(i + step) % chips] * 2 + core)
        for i in range(chips)
        for core in range(2)
    ]


def core_perm(chips):
    return [(i, i ^ 1) for i in range(2 * chips)]


def place_of(chip, chips):
    if chips == 8:
        row, column = chip // 2, chip % 2
        return jnp.where(column == 0, row, chips - 1 - row)
    return chip


def block_of(chip, mine, chips):
    back = lax.rem(place_of(mine, chips) - place_of(chip, chips) + chips, chips)
    long = chips // 2
    return jnp.where(back <= long, back, long + chips - back)


SETS = [(0, 0), (1, 1), (0, 1), (1, 0)]


def prepare_rows_kernel(queries, hidden, q_sets, hid_out, q_ref, hid, sems):
    copies = [
        pltpu.make_async_copy(queries, q_ref, sems.at[0]),
        pltpu.make_async_copy(hidden, hid, sems.at[1]),
    ]
    for copy in copies:
        copy.start()
    rows = q_ref.shape[0] // PARTS
    pairs = D // LANES // KV_HEADS
    lane = lax.broadcasted_iota(jnp.int32, (rows, LANES), 1)
    copies[0].wait()
    for part in range(PARTS):
        for n, (g, par) in enumerate(SETS):
            for j in range(pairs):
                c = (g * pairs + j) * LANES
                q = q_ref[part * rows : (part + 1) * rows, c : c + LANES].astype(F32)
                q = jnp.where((lane < HEAD_DIM) == (par == 0), q * (HEAD_DIM**-0.5), 0.0)
                q_sets[part, n, j * rows : (j + 1) * rows] = q.astype(BF)
    copies[1].wait()
    hid_out[...] = hid[...]


def prepare_rows(queries, hidden):
    rows = queries.shape[0] // PARTS
    m_rows = D // LANES // KV_HEADS * rows
    vmem = pl.BlockSpec(memory_space=pltpu.VMEM)
    anywhere = pl.BlockSpec(memory_space=pl.ANY)
    return pl.pallas_call(
        prepare_rows_kernel,
        in_specs=[anywhere] * 2,
        out_specs=[vmem] * 2,
        out_shape=[
            jax.ShapeDtypeStruct((PARTS, len(SETS), m_rows, LANES), BF),
            jax.ShapeDtypeStruct(hidden.shape, BF),
        ],
        scratch_shapes=[
            pltpu.VMEM(queries.shape, BF),
            pltpu.VMEM(hidden.shape, BF),
            pltpu.SemaphoreType.DMA((2,)),
        ],
        compiler_params=pltpu.CompilerParams(vmem_limit_bytes=20 * MIB),
        cost_estimate=LIGHT,
        name="prepare_rows",
    )(queries, hidden)


def prepare_gates_kernel(gain, router_t, ids_t, gain_out, wide, named):
    gain_out[...] = gain[...].astype(F32).reshape(1, D)
    experts = router_t.shape[0]
    wide[...] = jnp.zeros_like(wide)
    wide[:experts] = router_t[...]
    expert = lax.broadcasted_iota(jnp.int32, (LANES, LANES), 0)
    picked = expert == ids_t[0:1, :]
    for k in range(1, TOP):
        picked = jnp.logical_or(picked, expert == ids_t[k : k + 1, :])
    named[...] = jnp.where(picked, 1.0, 0.0).T


def prepare_gates(gain, router_t, ids_t):
    vmem = pl.BlockSpec(memory_space=pltpu.VMEM)
    return pl.pallas_call(
        prepare_gates_kernel,
        in_specs=[vmem] * 3,
        out_specs=[vmem] * 3,
        out_shape=[
            jax.ShapeDtypeStruct((1, D), F32),
            jax.ShapeDtypeStruct((LANES, D), BF),
            jax.ShapeDtypeStruct((LANES, LANES), F32),
        ],
        compiler_params=pltpu.CompilerParams(vmem_limit_bytes=20 * MIB),
        cost_estimate=LIGHT,
        name="prepare_gates",
    )(gain, router_t, ids_t)


def attend_kernel(
    part, chips, together, q_sets, hid, gain, wide, named, kv0, kv1,
    msg_ref, mixed_ref, kbuf, vbuf, s_scr, mx, tot, acc,
):
    rows = mixed_ref.shape[0]
    pairs = D // LANES // KV_HEADS
    m_rows = pairs * rows
    mine = slice(part * rows, (part + 1) * rows)
    me = lax.axis_index("ctx")
    core, count = lax.rem(me, 2), me // 2

    def swap_halves(a):
        return jnp.concatenate([a[:, HEAD_DIM:], a[:, :HEAD_DIM]], axis=1)

    for t in range(chips):
        at = slice(t * LANES, (t + 1) * LANES)
        k = jnp.concatenate([kv0[at, :LANES], kv1[at, :LANES]], axis=0)
        v = jnp.concatenate([kv0[at, LANES:], kv1[at, LANES:]], axis=0)
        kbuf[0, t], kbuf[1, t] = k, swap_halves(k)
        vbuf[0, t], vbuf[1, t] = v, swap_halves(v)

    lane = lax.broadcasted_iota(jnp.int32, (rows, LANES), 1)
    row_in = lax.rem(lax.broadcasted_iota(jnp.int32, (m_rows, 2 * LANES), 0), rows) + part * rows
    col = lax.broadcasted_iota(jnp.int32, (m_rows, 2 * LANES), 1)
    allowed = col <= jnp.where(col < LANES, row_in, core * (4 * LANES) - 1)

    for start in range(0, len(SETS), together):
        group = range(start, start + together)

        def score(n, idx):
            return lax.dot_general(
                q_sets[part, n], kbuf[n // 2, idx], (((1,), (1,)), ((), ())),
                preferred_element_type=F32,
            )

        for n in group:
            s = jnp.where(allowed, score(n, 0), -1e30)
            s_scr[0, n - start] = s
            mx[n - start] = jnp.maximum(s[:, :LANES], s[:, LANES:])

        def first(t, carry):
            for n in group:
                s = score(n, block_of(t, count, chips))
                s_scr[t + 1, n - start] = s
                mx[n - start] = jnp.maximum(mx[n - start], jnp.maximum(s[:, :LANES], s[:, LANES:]))
            return carry

        lax.fori_loop(0, count, first, 0)
        for n in group:
            row_max = jnp.max(mx[n - start], axis=1, keepdims=True)
            mx[n - start] = jnp.broadcast_to(row_max, (m_rows, LANES))

        def weigh(n, slot, idx):
            top = mx[n - start]
            p = jnp.exp(s_scr[slot, n - start] - jnp.concatenate([top, top], axis=1))
            part_sum = p[:, :LANES] + p[:, LANES:]
            part_acc = jnp.dot(p.astype(BF), vbuf[n // 2, idx], preferred_element_type=F32)
            return part_sum, part_acc

        for n in group:
            tot[n], acc[n] = weigh(n, 0, 0)

        def second(t, carry):
            for n in group:
                part_sum, part_acc = weigh(n, t + 1, block_of(t, count, chips))
                tot[n] += part_sum
                acc[n] += part_acc
            return carry

        lax.fori_loop(0, count, second, 0)

    for g in range(KV_HEADS):
        even, odd = SETS.index((g, 0)), SETS.index((g, 1))
        for j in range(pairs):
            at = slice(j * rows, (j + 1) * rows)
            c = (g * pairs + j) * LANES
            one = acc[even, at] / jnp.sum(tot[even, at], axis=1, keepdims=True)
            two = acc[odd, at] / jnp.sum(tot[odd, at], axis=1, keepdims=True)
            attn = jnp.where(lane < HEAD_DIM, one, two).astype(BF).astype(F32)
            mixed_ref[:, c : c + LANES] = hid[mine, c : c + LANES].astype(F32) + attn

    mixed = mixed_ref[...]
    mean_sq = jnp.mean(mixed * mixed, axis=-1, keepdims=True)
    normed = (mixed * lax.rsqrt(mean_sq + 1e-06) * gain[...]).astype(BF)
    msg_ref[:, :D] = normed
    logits = lax.dot_general(
        normed, wide[...], (((1,), (1,)), ((), ())), preferred_element_type=F32
    )
    sig = jnp.where(named[mine] > 0.0, 1.0 / (1.0 + jnp.exp(-logits)), 0.0)
    gates = sig / jnp.sum(sig, axis=-1, keepdims=True)
    high = gates.astype(BF).astype(F32)
    low = gates - high
    low = jnp.concatenate([low[:, HEAD_DIM:], low[:, :HEAD_DIM]], axis=1)
    msg_ref[:, D:] = jnp.where(lane < HEAD_DIM, high, low).astype(BF)


def attend(part, chips, prepared, kv0, kv1):
    rows = prepared[1].shape[0] // PARTS
    m_rows = D // LANES // KV_HEADS * rows
    sets = len(SETS)
    together = sets if chips <= 8 else 1
    vmem = pl.BlockSpec(memory_space=pltpu.VMEM)
    return pl.pallas_call(
        functools.partial(attend_kernel, part, chips, together),
        in_specs=[vmem] * 7,
        out_specs=[vmem, vmem],
        out_shape=[
            jax.ShapeDtypeStruct((rows, D + LANES), BF),
            jax.ShapeDtypeStruct((rows, D), F32),
        ],
        scratch_shapes=[
            pltpu.VMEM((2, chips, 2 * LANES, LANES), BF),
            pltpu.VMEM((2, chips, 2 * LANES, LANES), BF),
            pltpu.VMEM((chips, together, m_rows, 2 * LANES), F32),
            pltpu.VMEM((together, m_rows, LANES), F32),
            pltpu.VMEM((sets, m_rows, LANES), F32),
            pltpu.VMEM((sets, m_rows, LANES), F32),
        ],
        compiler_params=pltpu.CompilerParams(vmem_limit_bytes=(25 if chips <= 8 else 36) * MIB),
        cost_estimate=pl.CostEstimate(flops=10**10, bytes_accessed=1 << 16, transcendentals=0),
        name="attend",
    )(*prepared, kv0, kv1)


def expert_kernel(blocks, last, *refs):
    msgs, refs = refs[:blocks], refs[blocks:]
    if last:
        before, refs = refs[0], refs[1:]
    wg, wu, wd = refs[:3]
    outs, x = refs[3:-1], refs[-1]
    rows = msgs[0].shape[0]
    for b in range(blocks):
        x[b * rows : (b + 1) * rows] = msgs[b][:, :D]
    gate_val = jnp.dot(x[...], wg[0], preferred_element_type=F32)
    up_val = jnp.dot(x[...], wu[0], preferred_element_type=F32)
    up_part = (gate_val / (1.0 + jnp.exp(-gate_val)) * up_val).astype(BF)
    made = jnp.dot(up_part, wd[0], preferred_element_type=F32).astype(BF)
    if not last:
        outs[0][...] = made
        return
    me = lax.axis_index("ctx")
    lane = lax.broadcasted_iota(jnp.int32, (rows, LANES), 1)
    half = lax.rem(lane, HEAD_DIM)
    for b in range(blocks):
        at = slice(b * rows, (b + 1) * rows)
        gates = msgs[b][:, D:].astype(F32)
        gate0 = jnp.sum(jnp.where(half == me, gates, 0.0), axis=1, keepdims=True)
        gate1 = jnp.sum(jnp.where(half == (me ^ 1), gates, 0.0), axis=1, keepdims=True)
        both = gate0 * before[at].astype(F32) + gate1 * made[at].astype(F32)
        outs[b][...] = both.astype(BF)


def expert(msgs, before, weights):
    blocks, rows, last = len(msgs), msgs[0].shape[0], before is not None
    vmem = pl.BlockSpec(memory_space=pltpu.VMEM)
    ins = list(msgs) + ([before] if last else []) + list(weights)
    if last:
        out_shape = [jax.ShapeDtypeStruct((rows, D), BF)] * blocks
    else:
        out_shape = [jax.ShapeDtypeStruct((blocks * rows, D), BF)]
    return pl.pallas_call(
        functools.partial(expert_kernel, blocks, last),
        in_specs=[vmem] * len(ins),
        out_specs=[vmem] * len(out_shape),
        out_shape=out_shape,
        scratch_shapes=[pltpu.VMEM((blocks * rows, D), BF)],
        compiler_params=pltpu.CompilerParams(vmem_limit_bytes=24 * MIB),
        cost_estimate=LIGHT,
        name="experts",
    )(*ins)


def add(a, b):
    return (a.astype(F32) + b.astype(F32)).astype(BF)


def spread(block, ring, sign, meanwhile):
    chips = len(ring)
    behind, ahead = [], []
    now = block
    for step in range(chips // 2):
        now = meanwhile(step, now)
        now = lax.ppermute(now, "ctx", ring_perm(ring, sign))
        behind.append(now)
    now = block
    for _ in range(chips - 1 - chips // 2):
        now = lax.ppermute(now, "ctx", ring_perm(ring, -sign))
        ahead.append(now)
    return behind, ahead


def tie(array, *others):
    return lax.optimization_barrier((array, *others))[0]


class Order:
    def __init__(self):
        self.token = []

    def tied(self, array):
        return tie(array, *self.token) if self.token else array

    def wait(self, *arrays):
        self.token = self.token[:1] + list(arrays)

    def ran(self, array):
        self.token = [array]


class Part:
    def __init__(self, order, ring, sign, own, other):
        self.order, self.ring, self.sign, self.own, self.other = order, ring, sign, own, other
        self.long = len(ring) // 2
        self.short = len(ring) - 1 - self.long
        self.blocks, self.made, self.terms = {}, {}, {}

    def send(self, block, ahead):
        sign = -self.sign if ahead else self.sign
        return lax.ppermute(self.order.tied(block), "ctx", ring_perm(self.ring, sign))

    def out(self, step, which=(-1, 1)):
        if step <= self.long and -1 in which:
            self.blocks[-step] = self.send(self.blocks[1 - step], False)
        if step <= self.short and 1 in which:
            self.blocks[step] = self.send(self.blocks[step - 1], True)

    def wait_out(self, step, which=(-1, 1)):
        self.order.wait(*[self.blocks[n * step] for n in which if n * step in self.blocks])

    def compute(self, names, which):
        msgs = [self.blocks[n] for n in names]
        msgs[0] = self.order.tied(msgs[0])
        key = tuple(names)
        if which == 0:
            self.made[key] = expert(msgs, None, self.own)[0]
            self.order.ran(self.made[key])
        else:
            self.terms.update(zip(names, expert(msgs, self.made[key], self.other)))
            self.order.ran(self.terms[names[0]])

    def back(self, step):
        if step == 1:
            self.one, self.two = self.terms[-self.long], self.terms[1 - self.long]
        else:
            if step <= self.long:
                self.one = add(self.order.tied(self.one), self.terms[self.long + 1 - step])
            if step <= self.short:
                self.two = add(self.order.tied(self.two), self.terms[step - self.long])
        if step <= self.long:
            self.one = self.send(self.one, False)
        if step <= self.short:
            self.two = self.send(self.two, True)

    def wait_back(self, step):
        self.order.wait(*([self.one] if step <= self.long else []), *([self.two] if step <= self.short else []))

    def total(self, mixed):
        both = self.terms[0].astype(F32) + self.one.astype(F32) + self.two.astype(F32)
        return (mixed + both).astype(BF)


def local(hidden_in, queries, keys, values, norm_gain, router, w_gate, w_up, w_down, expert_ids):
    chips = lax.axis_size("ctx") // 2
    ring = chip_ring(chips)
    router_t = router.T
    ids_t = expert_ids.T

    swap = core_perm(chips)
    kv = jnp.pad(keys, ((0, 0), (0, LANES))) + jnp.pad(values, ((0, 0), (LANES, 0)))
    prepared = list(prepare_rows(queries, hidden_in))

    def meanwhile(step, now):
        if step == 1:
            return tie(now, prepared[1])
        if step == 2:
            prepared.extend(prepare_gates(norm_gain, router_t, tie(ids_t, now)))
            return tie(now, prepared[2])
        return now

    behind, ahead = spread(kv, ring, 1, meanwhile)
    kv0 = jnp.concatenate([kv] + behind + ahead, axis=0)
    kv1 = lax.ppermute(kv0, "ctx", swap)
    own = (w_gate, w_up, w_down)
    other = tuple(lax.ppermute(w, "ctx", swap) for w in own)

    long = chips // 2
    order = Order()
    a = Part(order, ring, 1, own, other)
    b = Part(order, ring, -1, own, other)
    near, last = [0, -1, 1], [-long, 1 - long]
    rest = [n for n in range(2 - long, long) if n not in near]
    mids = [rest[i : i + 4] for i in range(0, len(rest), 4)]

    a.blocks[0], mixed_a = attend(0, chips, prepared, kv0, kv1)
    a.out(1)
    order.ran(a.blocks[0])
    b.blocks[0], mixed_b = attend(1, chips, [order.tied(prepared[0])] + prepared[1:], kv0, kv1)
    order.ran(b.blocks[0])
    a.wait_out(1)
    a.out(2)
    a.compute(near, 0)
    b.out(1)
    a.compute(near, 1)
    a.wait_out(2)
    a.out(3)
    b.wait_out(1)
    b.out(2)
    b.compute(near, 0)
    for step in range(4, long):
        a.wait_out(step - 1)
        a.out(step)
        b.wait_out(step - 2)
        b.out(step - 1)
    a.wait_out(long - 1, (-1,))
    a.out(long)
    for mid in mids:
        a.compute(mid, 0)
    b.wait_out(long - 2, (-1,))
    b.out(long - 1, (-1,))
    for mid in mids:
        a.compute(mid, 1)
    b.wait_out(long - 2, (1,))
    b.out(long - 1, (1,))
    b.compute(near, 1)
    b.wait_out(long - 1, (-1,))
    b.out(long)
    a.wait_out(long)
    a.compute(last, 0)
    a.compute(last, 1)
    a.back(1)
    b.wait_out(long)
    b.compute(last, 0)
    b.compute(last, 1)
    b.back(1)
    a.wait_back(1)
    a.back(2)
    for mid in mids:
        b.compute(mid, 0)
        b.compute(mid, 1)
    for step in range(2, long):
        b.wait_back(step - 1)
        b.back(step)
        a.wait_back(step)
        a.back(step + 1)
    b.wait_back(long - 1)
    b.back(long)
    return jnp.concatenate([a.total(mixed_a), b.total(mixed_b)], axis=0)


def solution(mesh):
    placed = (
        P(("groups", "ctx"), None),
        P(("groups", "ctx"), None),
        P(("groups", "ctx"), None),
        P(("groups", "ctx"), None),
        P(),
        P(),
        P("ctx", None, None),
        P("ctx", None, None),
        P("ctx", None, None),
        P(("groups", "ctx"), None),
    )
    return jax.shard_map(
        local, mesh=mesh, in_specs=placed, out_specs=P(("groups", "ctx"), None), check_vma=False
    )
```

time: 151 us -> 133 us (0.88)
  starting transfers between devices: 58.6 us -> 44 us
  waiting for transfers between devices: 57.5 us -> 54.5 us
  local copies, waits for them, and re-layouts: 6.59 us -> 4.35 us
    ppermute x12 -> x4, starting transfers between devices: 29.5 us -> 8.79 us  [spread(): now = lax.ppermute(now, 'ctx', ring_perm(ring, sign))]
    ppermute x14 -> x28, waiting for transfers between devices: 24.6 us -> 45.2 us  [send(): lax.ppermute(self.order.tied(block), 'ctx', ring_perm(self.ring, sign))]
    ppermute x12 -> x4, waiting for transfers between devices: 27.5 us -> 7.38 us  [spread(): now = lax.ppermute(now, 'ctx', ring_perm(ring, sign))]
    ppermute x14 -> x28, starting transfers between devices: 14.2 us -> 34.3 us  [send(): lax.ppermute(self.order.tied(block), 'ctx', ring_perm(self.ring, sign))]
    ppermute x9 -> x3, starting transfers between devices: 13.8 us -> 0.25 us  [spread(): now = lax.ppermute(now, 'ctx', ring_perm(ring, -sign))]
    ppermute x9 -> x3, waiting for transfers between devices: 4.43 us -> 0.01 us  [spread(): now = lax.ppermute(now, 'ctx', ring_perm(ring, -sign))]
    pallas_call x4 -> x12, Pallas kernels: 20.6 us -> 22.7 us  [expert(): pl.pallas_call(functools.partial(expert_kernel, blocks, last), in_specs=[...]
    pallas_call x2, Pallas kernels: 5.5 us -> 3.97 us  [attend(): pl.pallas_call(functools.partial(attend_kernel, part, chips, together), i...]
  transfers between devices with their start and end apart: 39 -> 39, of which waited for: 23 -> 22; matrix products, arithmetic and copies ran while one was open for 1% -> 1% of each run, Pallas kernels for 14% -> 19%
where the time goes in v3:
time: 133 us
  waiting for transfers between devices  54.5 us (41%)
  starting transfers between devices  44 us (33%)
  Pallas kernels  27.2 us (20%)
  local copies, waits for them, and re-layouts  4.35 us (3%)
  other arithmetic  2.51 us (2%)
    ppermute x28, waiting for transfers between devices, send(): lax.ppermute(self.order.tied(block), 'ctx', ring_perm(self.ring, sign))  45.2 us
    ppermute x28, starting transfers between devices, send(): lax.ppermute(self.order.tied(block), 'ctx', ring_perm(self.ring, sign))  34.3 us
    pallas_call x12, Pallas kernels, expert(): pl.pallas_call(functools.partial(expert_kernel, blocks, last), in_specs=[...  22.7 us
    ppermute x4, starting transfers between devices, spread(): now = lax.ppermute(now, 'ctx', ring_perm(ring, sign))  8.79 us
    ppermute x4, waiting for transfers between devices, spread(): now = lax.ppermute(now, 'ctx', ring_perm(ring, sign))  7.38 us
    unnamed x22, local copies, waits for them, and re-layouts  4.34 us
    pallas_call x2, Pallas kernels, attend(): pl.pallas_call(functools.partial(attend_kernel, part, chips, together), i...  3.97 us
  transfers between devices with their start and end apart: 39, of which 22 were waited for; matrix products, arithmetic and copies ran while one was open for 1% of the time, Pallas kernels for 19%

profile of v3, /device:TPU:0, one launch (start us, length us, event | category | flops | bytes accessed | tf_op | source)
XLA Modules:
  0.0 132.8 jit_solution(17570963118731775701)
XLA Ops:
  0.8 3.1 %collective-permute-start = (bf16[128,256]{1,0:T(8,128)(2,1)S(1)}, bf16[128,256]{1,0:T(8,128)(2,1)S(1)}, u32[]{:S(2)}, u32[]{:S(2)}) collective-permute-start(bf16[128,256]{1,0:T(8,128)(2,1)S(1)} %get-tuple-element.158), channel_id=1, source_target_pairs={{0,4},{1,5},{4,8},{5,9},{8,12},{9,13},{12,14},{13,15},{14,10},{15,... | collective-permute-start | bytes 196616 | tf_op jit(solution)/shard_map/ppermute | solution.py:314
  6.9 2.1 %collective-permute-start.1 = (bf16[128,256]{1,0:T(8,128)(2,1)S(1)}, bf16[128,256]{1,0:T(8,128)(2,1)S(1)}, u32[]{:S(2)}, u32[]{:S(2)}) collective-permute-start(bf16[128,256]{1,0:T(8,128)(2,1)S(1)} %collective-permute-done), channel_id=1, source_target_pairs={{0,4},{1,5},{4,8},{5,9},{8,12},{9,13},{12,14},{13,15},{14,10},{15,... | collective-permute-start | bytes 196616 | tf_op jit(solution)/shard_map/ppermute | solution.py:314
  9.0 2.7 %collective-permute-done.1 = bf16[128,256]{1,0:T(8,128)(2,1)S(1)} collective-permute-done((bf16[128,256]{1,0:T(8,128)(2,1)S(1)}, bf16[128,256]{1,0:T(8,128)(2,1)S(1)}, u32[]{:S(2)}, u32[]{:S(2)}) %collective-permute-start.1) | collective-permute-done | bytes 65568 | tf_op jit(solution)/shard_map/ppermute | solution.py:314
  14.0 1.8 %collective-permute-start.2 = (bf16[128,256]{1,0:T(8,128)(2,1)S(1)}, bf16[128,256]{1,0:T(8,128)(2,1)S(1)}, u32[]{:S(2)}, u32[]{:S(2)}) collective-permute-start(bf16[128,256]{1,0:T(8,128)(2,1)S(1)} %collective-permute-done.1), channel_id=1, source_target_pairs={{0,4},{1,5},{4,8},{5,9},{8,12},{9,13},{12,14},{13,15},{14,10},{15,... | collective-permute-start | bytes 196616 | tf_op jit(solution)/shard_map/ppermute | solution.py:314
  16.1 2.2 %collective-permute-done.2 = bf16[128,256]{1,0:T(8,128)(2,1)S(1)} collective-permute-done((bf16[128,256]{1,0:T(8,128)(2,1)S(1)}, bf16[128,256]{1,0:T(8,128)(2,1)S(1)}, u32[]{:S(2)}, u32[]{:S(2)}) %collective-permute-start.2) | collective-permute-done | bytes 65568 | tf_op jit(solution)/shard_map/ppermute | solution.py:314
  18.3 1.8 %collective-permute-start.3 = (bf16[128,256]{1,0:T(8,128)(2,1)S(1)}, bf16[128,256]{1,0:T(8,128)(2,1)S(1)}, u32[]{:S(2)}, u32[]{:S(2)}) collective-permute-start(bf16[128,256]{1,0:T(8,128)(2,1)S(1)} %collective-permute-done.2), channel_id=1, source_target_pairs={{0,4},{1,5},{4,8},{5,9},{8,12},{9,13},{12,14},{13,15},{14,10},{15,... | collective-permute-start | bytes 196616 | tf_op jit(solution)/shard_map/ppermute | solution.py:314
  20.1 2.5 %collective-permute-done.3 = bf16[128,256]{1,0:T(8,128)(2,1)S(1)} collective-permute-done((bf16[128,256]{1,0:T(8,128)(2,1)S(1)}, bf16[128,256]{1,0:T(8,128)(2,1)S(1)}, u32[]{:S(2)}, u32[]{:S(2)}) %collective-permute-start.3) | collective-permute-done | bytes 65568 | tf_op jit(solution)/shard_map/ppermute | solution.py:314
  22.7 1.9 %collective-permute-done.7.kv1 = bf16[1024,256]{1,0:T(8,128)(2,1)S(1)} collective-permute-done((bf16[1024,256]{1,0:T(8,128)(2,1)S(1)}, bf16[1024,256]{1,0:T(8,128)(2,1)S(1)}, u32[]{:S(2)}, u32[]{:S(2)}) %collective-permute-start.7) | collective-permute-done | bytes 524320 | tf_op jit(solution)/shard_map/ppermute | solution.py:413
  24.6 2.0 %attend.2 = (bf16[64,2176]{1,0:T(8,128)(2,1)S(1)}, f32[64,2048]{1,0:T(8,128)S(1)}) custom-call(bf16[2,4,512,128]{3,2,1,0:T(8,128)(2,1)S(1)} %get-tuple-element.91.q_sets, bf16[128,2048]{1,0:T(8,128)(2,1)S(1)} %get-tuple-element.82.hid, f32[1,2048]{1,0:T(1,128)S(1)} %get-tuple-element.85.gain, bf16[128,2048]{1,0:T(8,128)(2,1)S(1)} %get-tuple-element.86.wide, ...), custom_call_target="tpu_custom_call" | custom-call | flops 10000000000 | bytes 65536 | tf_op jit(solution)/shard_map/attend/pallas_call | solution.py:234
  26.6 3.7 %collective-permute-start.8 = (bf16[64,2176]{1,0:T(8,128)(2,1)S(1)}, bf16[64,2176]{1,0:T(8,128)(2,1)S(1)}, u32[]{:S(2)}, u32[]{:S(2)}) collective-permute-start(bf16[64,2176]{1,0:T(8,128)(2,1)S(1)} %get-tuple-element.94.refs_0_), channel_id=1, source_target_pairs={{0,4},{1,5},{4,8},{5,9},{8,12},{9,13},{12,14},{13,15},{14,10},{15,... | collective-permute-start | bytes 835592 | tf_op jit(solution)/shard_map/ppermute | solution.py:350
  30.3 2.0 %attend.3 = (bf16[64,2176]{1,0:T(8,128)(2,1)S(1)}, f32[64,2048]{1,0:T(8,128)S(1)}) custom-call(bf16[2,4,512,128]{3,2,1,0:T(8,128)(2,1)S(1)} %get-tuple-element.91.q_sets, bf16[128,2048]{1,0:T(8,128)(2,1)S(1)} %get-tuple-element.82.hid, f32[1,2048]{1,0:T(1,128)S(1)} %get-tuple-element.85.gain, bf16[128,2048]{1,0:T(8,128)(2,1)S(1)} %get-tuple-element.86.wide, ...), custom_call_target="tpu_custom_call" | custom-call | flops 10000000000 | bytes 65536 | tf_op jit(solution)/shard_map/attend/pallas_call | solution.py:234
  32.3 4.2 %collective-permute-done.8.refs_1_ = bf16[64,2176]{1,0:T(8,128)(2,1)S(1)} collective-permute-done((bf16[64,2176]{1,0:T(8,128)(2,1)S(1)}, bf16[64,2176]{1,0:T(8,128)(2,1)S(1)}, u32[]{:S(2)}, u32[]{:S(2)}) %collective-permute-start.8) | collective-permute-done | bytes 278560 | tf_op jit(solution)/shard_map/ppermute | solution.py:350
  36.6 3.9 %collective-permute-done.9.refs_2_ = bf16[64,2176]{1,0:T(8,128)(2,1)S(1)} collective-permute-done((bf16[64,2176]{1,0:T(8,128)(2,1)S(1)}, bf16[64,2176]{1,0:T(8,128)(2,1)S(1)}, u32[]{:S(2)}, u32[]{:S(2)}) %collective-permute-start.9) | collective-permute-done | bytes 278560 | tf_op jit(solution)/shard_map/ppermute | solution.py:350
  40.5 3.5 %collective-permute-start.13 = (bf16[64,2176]{1,0:T(8,128)(2,1)S(1)}, bf16[64,2176]{1,0:T(8,128)(2,1)S(1)}, u32[]{:S(2)}, u32[]{:S(2)}) collective-permute-start(bf16[64,2176]{1,0:T(8,128)(2,1)S(1)} %collective-permute-done.8.refs_1_), channel_id=1, source_target_pairs={{0,4},{1,5},{4,8},{5,9},{8,12},{9,13},{12,14},{13,15},{14,10},{15,... | collective-permute-start | bytes 835592 | tf_op jit(solution)/shard_map/ppermute | solution.py:350
  44.0 2.1 %experts.12.refs_3_ = bf16[192,2048]{1,0:T(8,128)(2,1)S(1)} custom-call(bf16[64,2176]{1,0:T(8,128)(2,1)S(1)} %get-tuple-element.94.refs_0_, bf16[64,2176]{1,0:T(8,128)(2,1)S(1)} %collective-permute-done.8.refs_1_, bf16[64,2176]{1,0:T(8,128)(2,1)S(1)} %collective-permute-done.9.refs_2_, bf16[1,2048,768]{2,1,0:T(8,128)(2,1)S(1)} %copy-done, ...), custom_call_target="tpu_custom_call" | custom-call | flops 1048576 | bytes 65536 | tf_op jit(solution)/shard_map/experts/pallas_call | solution.py:292
  46.1 2.5 %collective-permute-start.17 = (bf16[64,2176]{1,0:T(8,128)(2,1)S(1)}, bf16[64,2176]{1,0:T(8,128)(2,1)S(1)}, u32[]{:S(2)}, u32[]{:S(2)}) collective-permute-start(bf16[64,2176]{1,0:T(8,128)(2,1)S(1)} %get-tuple-element.108.refs_0_), channel_id=1, source_target_pairs={{0,4},{1,5},{4,8},{5,9},{8,12},{9,13},{12,14},{13,15},{14,10},{15,... | collective-permute-start | bytes 835592 | tf_op jit(solution)/shard_map/ppermute | solution.py:350
  48.7 2.1 %experts.13 = (bf16[64,2048]{1,0:T(8,128)(2,1)S(1)}, bf16[64,2048]{1,0:T(8,128)(2,1)S(1)}, bf16[64,2048]{1,0:T(8,128)(2,1)S(1)}) custom-call(bf16[64,2176]{1,0:T(8,128)(2,1)S(1)} %get-tuple-element.94.refs_0_, bf16[64,2176]{1,0:T(8,128)(2,1)S(1)} %collective-permute-done.8.refs_1_, bf16[64,2176]{1,0:T(8,128)(2,1)S(1)} %collective-permute-done.9.refs_2_, ...), custom_call_target="tpu_custom_call" | custom-call | flops 1048576 | bytes 65536 | tf_op jit(solution)/shard_map/experts/pallas_call | solution.py:292
  50.8 3.2 %collective-permute-done.14.refs_1_ = bf16[64,2176]{1,0:T(8,128)(2,1)S(1)} collective-permute-done((bf16[64,2176]{1,0:T(8,128)(2,1)S(1)}, bf16[64,2176]{1,0:T(8,128)(2,1)S(1)}, u32[]{:S(2)}, u32[]{:S(2)}) %collective-permute-start.14) | collective-permute-done | bytes 278560 | tf_op jit(solution)/shard_map/ppermute | solution.py:350
  54.0 2.0 %collective-permute-start.15 = (bf16[64,2176]{1,0:T(8,128)(2,1)S(1)}, bf16[64,2176]{1,0:T(8,128)(2,1)S(1)}, u32[]{:S(2)}, u32[]{:S(2)}) collective-permute-start(bf16[64,2176]{1,0:T(8,128)(2,1)S(1)} %collective-permute-done.13.refs_0_), channel_id=1, source_target_pairs={{0,4},{1,5},{4,8},{5,9},{8,12},{9,13},{12,14},{13,15},{14,10},{15,... | collective-permute-start | bytes 835592 | tf_op jit(solution)/shard_map/ppermute | solution.py:350
  56.0 3.9 %collective-permute-done.16.refs_1_ = bf16[64,2176]{1,0:T(8,128)(2,1)S(1)} collective-permute-done((bf16[64,2176]{1,0:T(8,128)(2,1)S(1)}, bf16[64,2176]{1,0:T(8,128)(2,1)S(1)}, u32[]{:S(2)}, u32[]{:S(2)}) %collective-permute-start.16) | collective-permute-done | bytes 278560 | tf_op jit(solution)/shard_map/ppermute | solution.py:350
  60.2 1.7 %collective-permute-start.21 = (bf16[64,2176]{1,0:T(8,128)(2,1)S(1)}, bf16[64,2176]{1,0:T(8,128)(2,1)S(1)}, u32[]{:S(2)}, u32[]{:S(2)}) collective-permute-start(bf16[64,2176]{1,0:T(8,128)(2,1)S(1)} %collective-permute-done.17.refs_2_), channel_id=1, source_target_pairs={{0,4},{1,5},{4,8},{5,9},{8,12},{9,13},{12,14},{13,15},{14,10},{15,... | collective-permute-start | bytes 835592 | tf_op jit(solution)/shard_map/ppermute | solution.py:350
  62.0 2.0 %experts.14.refs_3_ = bf16[192,2048]{1,0:T(8,128)(2,1)S(1)} custom-call(bf16[64,2176]{1,0:T(8,128)(2,1)S(1)} %get-tuple-element.108.refs_0_, bf16[64,2176]{1,0:T(8,128)(2,1)S(1)} %collective-permute-done.16.refs_1_, bf16[64,2176]{1,0:T(8,128)(2,1)S(1)} %collective-permute-done.17.refs_2_, bf16[1,2048,768]{2,1,0:T(8,128)(2,1)S(1)} %copy-done, ...), custom_call_target="tpu_custom_call" | custom-call | flops 1048576 | bytes 65536 | tf_op jit(solution)/shard_map/experts/pallas_call | solution.py:292
  64.0 1.9 %collective-permute-done.19.refs_2_ = bf16[64,2176]{1,0:T(8,128)(2,1)S(1)} collective-permute-done((bf16[64,2176]{1,0:T(8,128)(2,1)S(1)}, bf16[64,2176]{1,0:T(8,128)(2,1)S(1)}, u32[]{:S(2)}, u32[]{:S(2)}) %collective-permute-start.19) | collective-permute-done | bytes 278560 | tf_op jit(solution)/shard_map/ppermute | solution.py:350
  65.9 2.0 %experts.15.refs_3_ = bf16[192,2048]{1,0:T(8,128)(2,1)S(1)} custom-call(bf16[64,2176]{1,0:T(8,128)(2,1)S(1)} %collective-permute-done.13.refs_0_, bf16[64,2176]{1,0:T(8,128)(2,1)S(1)} %collective-permute-done.14.refs_1_, bf16[64,2176]{1,0:T(8,128)(2,1)S(1)} %collective-permute-done.19.refs_2_, bf16[1,2048,768]{2,1,0:T(8,128)(2,1)S(1)} %copy-done, ...), custom_call_target="tpu_custom_call" | custom-call | flops 1048576 | bytes 65536 | tf_op jit(solution)/shard_map/experts/pallas_call | solution.py:292
  68.0 2.2 %collective-permute-done.20.refs_0_ = bf16[64,2176]{1,0:T(8,128)(2,1)S(1)} collective-permute-done((bf16[64,2176]{1,0:T(8,128)(2,1)S(1)}, bf16[64,2176]{1,0:T(8,128)(2,1)S(1)}, u32[]{:S(2)}, u32[]{:S(2)}) %collective-permute-start.20) | collective-permute-done | bytes 278560 | tf_op jit(solution)/shard_map/ppermute | solution.py:350
  70.2 2.0 %collective-permute-start.18 = (bf16[64,2176]{1,0:T(8,128)(2,1)S(1)}, bf16[64,2176]{1,0:T(8,128)(2,1)S(1)}, u32[]{:S(2)}, u32[]{:S(2)}) collective-permute-start(bf16[64,2176]{1,0:T(8,128)(2,1)S(1)} %collective-permute-done.15.refs_1_), channel_id=1, source_target_pairs={{0,4},{1,5},{4,8},{5,9},{8,12},{9,13},{12,14},{13,15},{14,10},{15,... | collective-permute-start | bytes 835592 | tf_op jit(solution)/shard_map/ppermute | solution.py:350
  72.2 2.1 %experts.16 = (bf16[64,2048]{1,0:T(8,128)(2,1)S(1)}, bf16[64,2048]{1,0:T(8,128)(2,1)S(1)}, bf16[64,2048]{1,0:T(8,128)(2,1)S(1)}) custom-call(bf16[64,2176]{1,0:T(8,128)(2,1)S(1)} %collective-permute-done.13.refs_0_, bf16[64,2176]{1,0:T(8,128)(2,1)S(1)} %collective-permute-done.14.refs_1_, bf16[64,2176]{1,0:T(8,128)(2,1)S(1)} %collective-permute-done.19.refs_2_, ...), custom_call_target="tpu_custom_call" | custom-call | flops 1048576 | bytes 65536 | tf_op jit(solution)/shard_map/experts/pallas_call | solution.py:292
  74.3 2.1 %experts.17 = (bf16[64,2048]{1,0:T(8,128)(2,1)S(1)}, bf16[64,2048]{1,0:T(8,128)(2,1)S(1)}, bf16[64,2048]{1,0:T(8,128)(2,1)S(1)}) custom-call(bf16[64,2176]{1,0:T(8,128)(2,1)S(1)} %get-tuple-element.108.refs_0_, bf16[64,2176]{1,0:T(8,128)(2,1)S(1)} %collective-permute-done.16.refs_1_, bf16[64,2176]{1,0:T(8,128)(2,1)S(1)} %collective-permute-done.17.refs_2_, ...), custom_call_target="tpu_custom_call" | custom-call | flops 1048576 | bytes 65536 | tf_op jit(solution)/shard_map/experts/pallas_call | solution.py:292
  77.4 2.5 %collective-permute-start.27 = (bf16[64,2176]{1,0:T(8,128)(2,1)S(1)}, bf16[64,2176]{1,0:T(8,128)(2,1)S(1)}, u32[]{:S(2)}, u32[]{:S(2)}) collective-permute-start(bf16[64,2176]{1,0:T(8,128)(2,1)S(1)} %collective-permute-done.21.refs_1_), channel_id=1, source_target_pairs={{0,4},{1,5},{4,8},{5,9},{8,12},{9,13},{12,14},{13,15},{14,10},{15,... | collective-permute-start | bytes 835592 | tf_op jit(solution)/shard_map/ppermute | solution.py:350
  81.4 1.5 %experts.19 = (bf16[64,2048]{1,0:T(8,128)(2,1)S(1)}, bf16[64,2048]{1,0:T(8,128)(2,1)S(1)}) custom-call(bf16[64,2176]{1,0:T(8,128)(2,1)S(1)} %collective-permute-done.18.refs_0_, bf16[64,2176]{1,0:T(8,128)(2,1)S(1)} %collective-permute-done.15.refs_1_, bf16[128,2048]{1,0:T(8,128)(2,1)S(1)} %experts.18.refs_2_, ...), custom_call_target="tpu_custom_call" | custom-call | flops 1048576 | bytes 65536 | tf_op jit(solution)/shard_map/experts/pallas_call | solution.py:292
  83.0 2.1 %collective-permute-start.22 = (bf16[64,2048]{1,0:T(8,128)(2,1)S(1)}, bf16[64,2048]{1,0:T(8,128)(2,1)S(1)}, u32[]{:S(2)}, u32[]{:S(2)}) collective-permute-start(bf16[64,2048]{1,0:T(8,128)(2,1)S(1)} %get-tuple-element.113), channel_id=1, source_target_pairs={{0,4},{1,5},{4,8},{5,9},{8,12},{9,13},{12,14},{13,15},{14,10},{15,... | collective-permute-start | bytes 786440 | tf_op jit(solution)/shard_map/ppermute | solution.py:350
  86.5 1.5 %experts.21 = (bf16[64,2048]{1,0:T(8,128)(2,1)S(1)}, bf16[64,2048]{1,0:T(8,128)(2,1)S(1)}) custom-call(bf16[64,2176]{1,0:T(8,128)(2,1)S(1)} %collective-permute-done.24.refs_0_, bf16[64,2176]{1,0:T(8,128)(2,1)S(1)} %collective-permute-done.23.refs_1_, bf16[128,2048]{1,0:T(8,128)(2,1)S(1)} %experts.20.refs_2_, ...), custom_call_target="tpu_custom_call" | custom-call | flops 1048576 | bytes 65536 | tf_op jit(solution)/shard_map/experts/pallas_call | solution.py:292
  88.1 1.6 %collective-permute-done.22 = bf16[64,2048]{1,0:T(8,128)(2,1)S(1)} collective-permute-done((bf16[64,2048]{1,0:T(8,128)(2,1)S(1)}, bf16[64,2048]{1,0:T(8,128)(2,1)S(1)}, u32[]{:S(2)}, u32[]{:S(2)}) %collective-permute-start.22) | collective-permute-done | bytes 262176 | tf_op jit(solution)/shard_map/ppermute | solution.py:350
  89.6 1.8 %collective-permute-done.25 = bf16[64,2048]{1,0:T(8,128)(2,1)S(1)} collective-permute-done((bf16[64,2048]{1,0:T(8,128)(2,1)S(1)}, bf16[64,2048]{1,0:T(8,128)(2,1)S(1)}, u32[]{:S(2)}, u32[]{:S(2)}) %collective-permute-start.25) | collective-permute-done | bytes 262176 | tf_op jit(solution)/shard_map/ppermute | solution.py:350
  91.4 2.0 %experts.22.refs_3_ = bf16[192,2048]{1,0:T(8,128)(2,1)S(1)} custom-call(bf16[64,2176]{1,0:T(8,128)(2,1)S(1)} %collective-permute-done.20.refs_0_, bf16[64,2176]{1,0:T(8,128)(2,1)S(1)} %collective-permute-done.21.refs_1_, bf16[64,2176]{1,0:T(8,128)(2,1)S(1)} %collective-permute-done.27.refs_2_, bf16[1,2048,768]{2,1,0:T(8,128)(2,1)S(1)} %copy-done, ...), custom_call_target="tpu_custom_call" | custom-call | flops 1048576 | bytes 65536 | tf_op jit(solution)/shard_map/experts/pallas_call | solution.py:292
  93.5 1.8 %collective-permute-start.33 = (bf16[64,2048]{1,0:T(8,128)(2,1)S(1)}, bf16[64,2048]{1,0:T(8,128)(2,1)S(1)}, u32[]{:S(2)}, u32[]{:S(2)}) collective-permute-start(bf16[64,2048]{1,0:T(8,128)(2,1)S(1)} %get-tuple-element.142), channel_id=1, source_target_pairs={{0,4},{1,5},{4,8},{5,9},{8,12},{9,13},{12,14},{13,15},{14,10},{15,... | collective-permute-start | bytes 786440 | tf_op jit(solution)/shard_map/ppermute | solution.py:350
  96.1 1.6 %collective-permute-start.26 = (bf16[64,2048]{1,0:T(8,128)(2,1)S(1)}, bf16[64,2048]{1,0:T(8,128)(2,1)S(1)}, u32[]{:S(2)}, u32[]{:S(2)}) collective-permute-start(bf16[64,2048]{1,0:T(8,128)(2,1)S(1)} %get-tuple-element.123), channel_id=1, source_target_pairs={{0,4},{1,5},{4,8},{5,9},{8,12},{9,13},{12,14},{13,15},{14,10},{15,... | collective-permute-start | bytes 786440 | tf_op jit(solution)/shard_map/ppermute | solution.py:350
  97.8 2.1 %experts.23 = (bf16[64,2048]{1,0:T(8,128)(2,1)S(1)}, bf16[64,2048]{1,0:T(8,128)(2,1)S(1)}, bf16[64,2048]{1,0:T(8,128)(2,1)S(1)}) custom-call(bf16[64,2176]{1,0:T(8,128)(2,1)S(1)} %collective-permute-done.20.refs_0_, bf16[64,2176]{1,0:T(8,128)(2,1)S(1)} %collective-permute-done.21.refs_1_, bf16[64,2176]{1,0:T(8,128)(2,1)S(1)} %collective-permute-done.27.refs_2_, ...), custom_call_target="tpu_custom_call" | custom-call | flops 1048576 | bytes 65536 | tf_op jit(solution)/shard_map/experts/pallas_call | solution.py:292
  99.9 1.6 %collective-permute-done.33 = bf16[64,2048]{1,0:T(8,128)(2,1)S(1)} collective-permute-done((bf16[64,2048]{1,0:T(8,128)(2,1)S(1)}, bf16[64,2048]{1,0:T(8,128)(2,1)S(1)}, u32[]{:S(2)}, u32[]{:S(2)}) %collective-permute-start.33) | collective-permute-done | bytes 262176 | tf_op jit(solution)/shard_map/ppermute | solution.py:350
  101.5 3.0 %collective-permute-done.32 = bf16[64,2048]{1,0:T(8,128)(2,1)S(1)} collective-permute-done((bf16[64,2048]{1,0:T(8,128)(2,1)S(1)}, bf16[64,2048]{1,0:T(8,128)(2,1)S(1)}, u32[]{:S(2)}, u32[]{:S(2)}) %collective-permute-start.32) | collective-permute-done | bytes 262176 | tf_op jit(solution)/shard_map/ppermute | solution.py:350
  106.7 3.4 %collective-permute-done.28 = bf16[64,2048]{1,0:T(8,128)(2,1)S(1)} collective-permute-done((bf16[64,2048]{1,0:T(8,128)(2,1)S(1)}, bf16[64,2048]{1,0:T(8,128)(2,1)S(1)}, u32[]{:S(2)}, u32[]{:S(2)}) %collective-permute-start.28) | collective-permute-done | bytes 262176 | tf_op jit(solution)/shard_map/ppermute | solution.py:350
  110.3 2.1 %collective-permute-start.29 = (bf16[64,2048]{1,0:T(8,128)(2,1)S(1)}, bf16[64,2048]{1,0:T(8,128)(2,1)S(1)}, u32[]{:S(2)}, u32[]{:S(2)}) collective-permute-start(bf16[64,2048]{1,0:T(8,128)(2,1)S(1)} %add_convert_fusion.9), channel_id=1, source_target_pairs={{0,4},{1,5},{4,8},{5,9},{8,12},{9,13},{12,14},{13,15},{14,10},{15,... | collective-permute-start | bytes 786440 | tf_op jit(solution)/shard_map/ppermute | solution.py:350
  113.4 2.3 %collective-permute-done.34 = bf16[64,2048]{1,0:T(8,128)(2,1)S(1)} collective-permute-done((bf16[64,2048]{1,0:T(8,128)(2,1)S(1)}, bf16[64,2048]{1,0:T(8,128)(2,1)S(1)}, u32[]{:S(2)}, u32[]{:S(2)}) %collective-permute-start.34) | collective-permute-done | bytes 262176 | tf_op jit(solution)/shard_map/ppermute | solution.py:350
  115.8 1.5 %collective-permute-start.37 = (bf16[64,2048]{1,0:T(8,128)(2,1)S(1)}, bf16[64,2048]{1,0:T(8,128)(2,1)S(1)}, u32[]{:S(2)}, u32[]{:S(2)}) collective-permute-start(bf16[64,2048]{1,0:T(8,128)(2,1)S(1)} %add_convert_fusion.2), channel_id=1, source_target_pairs={{0,4},{1,5},{4,8},{5,9},{8,12},{9,13},{12,14},{13,15},{14,10},{15,... | collective-permute-start | bytes 786440 | tf_op jit(solution)/shard_map/ppermute | solution.py:350
  118.0 2.2 %collective-permute-done.30 = bf16[64,2048]{1,0:T(8,128)(2,1)S(1)} collective-permute-done((bf16[64,2048]{1,0:T(8,128)(2,1)S(1)}, bf16[64,2048]{1,0:T(8,128)(2,1)S(1)}, u32[]{:S(2)}, u32[]{:S(2)}) %collective-permute-start.30) | collective-permute-done | bytes 262176 | tf_op jit(solution)/shard_map/ppermute | solution.py:350
  120.3 1.8 %collective-permute-start.31 = (bf16[64,2048]{1,0:T(8,128)(2,1)S(1)}, bf16[64,2048]{1,0:T(8,128)(2,1)S(1)}, u32[]{:S(2)}, u32[]{:S(2)}) collective-permute-start(bf16[64,2048]{1,0:T(8,128)(2,1)S(1)} %add_convert_fusion.7), channel_id=1, source_target_pairs={{0,4},{1,5},{4,8},{5,9},{8,12},{9,13},{12,14},{13,15},{14,10},{15,... | collective-permute-start | bytes 786440 | tf_op jit(solution)/shard_map/ppermute | solution.py:350
  123.3 2.0 %collective-permute-done.36 = bf16[64,2048]{1,0:T(8,128)(2,1)S(1)} collective-permute-done((bf16[64,2048]{1,0:T(8,128)(2,1)S(1)}, bf16[64,2048]{1,0:T(8,128)(2,1)S(1)}, u32[]{:S(2)}, u32[]{:S(2)}) %collective-permute-start.36) | collective-permute-done | bytes 262176 | tf_op jit(solution)/shard_map/ppermute | solution.py:350
  126.9 5.0 %collective-permute-done.38 = bf16[64,2048]{1,0:T(8,128)(2,1)S(1)} collective-permute-done((bf16[64,2048]{1,0:T(8,128)(2,1)S(1)}, bf16[64,2048]{1,0:T(8,128)(2,1)S(1)}, u32[]{:S(2)}, u32[]{:S(2)}) %collective-permute-start.38) | collective-permute-done | bytes 262176 | tf_op jit(solution)/shard_map/ppermute | solution.py:350
  (81 shorter events, 19.6 us)
Async XLA Ops:
  0.8 6.1 %collective-permute-start = (bf16[128,256]{1,0:T(8,128)(2,1)S(1)}, bf16[128,256]{1,0:T(8,128)(2,1)S(1)}, u32[]{:S(2)}, u32[]{:S(2)}) collective-permute-start(bf16[128,256]{1,0:T(8,128)(2,1)S(1)} %get-tuple-element.158), channel_id=1, source_target_pairs={{0,4},{1,5},{4,8},{5,9},{8,12},{9,13},{12,14},{13,15},{14,10},{15,... | collective-permute-start | bytes 196616 | tf_op jit(solution)/shard_map/ppermute | solution.py:314
  3.9 5.1 %collective-permute-start.4 = (bf16[128,256]{1,0:T(8,128)(2,1)S(1)}, bf16[128,256]{1,0:T(8,128)(2,1)S(1)}, u32[]{:S(2)}, u32[]{:S(2)}) collective-permute-start(bf16[128,256]{1,0:T(8,128)(2,1)S(1)} %get-tuple-element.158), channel_id=1, source_target_pairs={{0,2},{1,3},{4,0},{5,1},{8,4},{9,5},{12,8},{13,9},{14,12},{15,13},... | collective-permute-start | bytes 196616 | tf_op jit(solution)/shard_map/ppermute | solution.py:318
  3.9 42.2 %collective-permute-start.10 = (bf16[1,2048,768]{2,1,0:T(8,128)(2,1)}, bf16[1,2048,768]{2,1,0:T(8,128)(2,1)S(1)}, u32[]{:S(2)}, u32[]{:S(2)}) collective-permute-start(bf16[1,2048,768]{2,1,0:T(8,128)(2,1)} %refs_3_.11), channel_id=1, source_target_pairs={{0,1},{1,0},{2,3},{3,2},{4,5},{5,4},{6,7},{7,6},{8,9},{9,8},{10,11... | collective-permute-start | bytes 9437192 | tf_op jit(solution)/shard_map/ppermute | solution.py:415
  3.9 42.3 %collective-permute-start.11 = (bf16[1,2048,768]{2,1,0:T(8,128)(2,1)}, bf16[1,2048,768]{2,1,0:T(8,128)(2,1)S(1)}, u32[]{:S(2)}, u32[]{:S(2)}) collective-permute-start(bf16[1,2048,768]{2,1,0:T(8,128)(2,1)} %refs_4_.11), channel_id=1, source_target_pairs={{0,1},{1,0},{2,3},{3,2},{4,5},{5,4},{6,7},{7,6},{8,9},{9,8},{10,11... | collective-permute-start | bytes 9437192 | tf_op jit(solution)/shard_map/ppermute | solution.py:415
  4.4 44.3 %collective-permute-start.12 = (bf16[1,768,2048]{2,1,0:T(8,128)(2,1)}, bf16[1,768,2048]{2,1,0:T(8,128)(2,1)S(1)}, u32[]{:S(2)}, u32[]{:S(2)}) collective-permute-start(bf16[1,768,2048]{2,1,0:T(8,128)(2,1)} %refs_5_.7), channel_id=1, source_target_pairs={{0,1},{1,0},{2,3},{3,2},{4,5},{5,4},{6,7},{7,6},{8,9},{9,8},{10,11... | collective-permute-start | bytes 9437192 | tf_op jit(solution)/shard_map/ppermute | solution.py:415
  4.4 1.0 copy-start.3
  5.4 1.0 copy-start.4
  6.9 4.8 %collective-permute-start.1 = (bf16[128,256]{1,0:T(8,128)(2,1)S(1)}, bf16[128,256]{1,0:T(8,128)(2,1)S(1)}, u32[]{:S(2)}, u32[]{:S(2)}) collective-permute-start(bf16[128,256]{1,0:T(8,128)(2,1)S(1)} %collective-permute-done), channel_id=1, source_target_pairs={{0,4},{1,5},{4,8},{5,9},{8,12},{9,13},{12,14},{13,15},{14,10},{15,... | collective-permute-start | bytes 196616 | tf_op jit(solution)/shard_map/ppermute | solution.py:314
  8.9 6.9 %collective-permute-start.5 = (bf16[128,256]{1,0:T(8,128)(2,1)S(1)}, bf16[128,256]{1,0:T(8,128)(2,1)S(1)}, u32[]{:S(2)}, u32[]{:S(2)}) collective-permute-start(bf16[128,256]{1,0:T(8,128)(2,1)S(1)} %collective-permute-done.4), channel_id=1, source_target_pairs={{0,2},{1,3},{4,0},{5,1},{8,4},{9,5},{12,8},{13,9},{14,12},{15,13},... | collective-permute-start | bytes 196616 | tf_op jit(solution)/shard_map/ppermute | solution.py:318
  11.6 0.8 copy-start.5
  12.5 0.7 copy-start.6
  13.2 0.7 copy-start.7
  14.0 4.3 %collective-permute-start.2 = (bf16[128,256]{1,0:T(8,128)(2,1)S(1)}, bf16[128,256]{1,0:T(8,128)(2,1)S(1)}, u32[]{:S(2)}, u32[]{:S(2)}) collective-permute-start(bf16[128,256]{1,0:T(8,128)(2,1)S(1)} %collective-permute-done.1), channel_id=1, source_target_pairs={{0,4},{1,5},{4,8},{5,9},{8,12},{9,13},{12,14},{13,15},{14,10},{15,... | collective-permute-start | bytes 196616 | tf_op jit(solution)/shard_map/ppermute | solution.py:314
  15.8 6.8 %collective-permute-start.6 = (bf16[128,256]{1,0:T(8,128)(2,1)S(1)}, bf16[128,256]{1,0:T(8,128)(2,1)S(1)}, u32[]{:S(2)}, u32[]{:S(2)}) collective-permute-start(bf16[128,256]{1,0:T(8,128)(2,1)S(1)} %collective-permute-done.5), channel_id=1, source_target_pairs={{0,2},{1,3},{4,0},{5,1},{8,4},{9,5},{12,8},{13,9},{14,12},{15,13},... | collective-permute-start | bytes 196616 | tf_op jit(solution)/shard_map/ppermute | solution.py:318
  18.3 4.3 %collective-permute-start.3 = (bf16[128,256]{1,0:T(8,128)(2,1)S(1)}, bf16[128,256]{1,0:T(8,128)(2,1)S(1)}, u32[]{:S(2)}, u32[]{:S(2)}) collective-permute-start(bf16[128,256]{1,0:T(8,128)(2,1)S(1)} %collective-permute-done.2), channel_id=1, source_target_pairs={{0,4},{1,5},{4,8},{5,9},{8,12},{9,13},{12,14},{13,15},{14,10},{15,... | collective-permute-start | bytes 196616 | tf_op jit(solution)/shard_map/ppermute | solution.py:314
  22.6 2.0 %collective-permute-start.7 = (bf16[1024,256]{1,0:T(8,128)(2,1)S(1)}, bf16[1024,256]{1,0:T(8,128)(2,1)S(1)}, u32[]{:S(2)}, u32[]{:S(2)}) collective-permute-start(bf16[1024,256]{1,0:T(8,128)(2,1)S(1)} %constant_dynamic-update-slice_fusion.kv0), channel_id=1, source_target_pairs={{0,1},{1,0},{2,3},{3,2},{4,5},{5,4},{6,7},{7,6},{8,9},{9,8},{10,11... | collective-permute-start | bytes 1572872 | tf_op jit(solution)/shard_map/ppermute | solution.py:413
  26.6 17.4 %copy-start = (bf16[1,2048,768]{2,1,0:T(8,128)(2,1)S(1)}, bf16[1,2048,768]{2,1,0:T(8,128)(2,1)}, u32[]{:S(2)}) copy-start(bf16[1,2048,768]{2,1,0:T(8,128)(2,1)} %refs_3_.11) | copy-start | bytes 9437188
  26.6 17.4 %copy-start.1 = (bf16[1,2048,768]{2,1,0:T(8,128)(2,1)S(1)}, bf16[1,2048,768]{2,1,0:T(8,128)(2,1)}, u32[]{:S(2)}) copy-start(bf16[1,2048,768]{2,1,0:T(8,128)(2,1)} %refs_4_.11) | copy-start | bytes 9437188
  26.6 17.4 %copy-start.2 = (bf16[1,768,2048]{2,1,0:T(8,128)(2,1)S(1)}, bf16[1,768,2048]{2,1,0:T(8,128)(2,1)}, u32[]{:S(2)}) copy-start(bf16[1,768,2048]{2,1,0:T(8,128)(2,1)} %refs_5_.7) | copy-start | bytes 9437188
  26.6 9.9 %collective-permute-start.8 = (bf16[64,2176]{1,0:T(8,128)(2,1)S(1)}, bf16[64,2176]{1,0:T(8,128)(2,1)S(1)}, u32[]{:S(2)}, u32[]{:S(2)}) collective-permute-start(bf16[64,2176]{1,0:T(8,128)(2,1)S(1)} %get-tuple-element.94.refs_0_), channel_id=1, source_target_pairs={{0,4},{1,5},{4,8},{5,9},{8,12},{9,13},{12,14},{13,15},{14,10},{15,... | collective-permute-start | bytes 835592 | tf_op jit(solution)/shard_map/ppermute | solution.py:350
  30.3 10.1 %collective-permute-start.9 = (bf16[64,2176]{1,0:T(8,128)(2,1)S(1)}, bf16[64,2176]{1,0:T(8,128)(2,1)S(1)}, u32[]{:S(2)}, u32[]{:S(2)}) collective-permute-start(bf16[64,2176]{1,0:T(8,128)(2,1)S(1)} %get-tuple-element.94.refs_0_), channel_id=1, source_target_pairs={{0,2},{1,3},{4,0},{5,1},{8,4},{9,5},{12,8},{13,9},{14,12},{15,13},... | collective-permute-start | bytes 835592 | tf_op jit(solution)/shard_map/ppermute | solution.py:350
  40.5 10.3 %collective-permute-start.13 = (bf16[64,2176]{1,0:T(8,128)(2,1)S(1)}, bf16[64,2176]{1,0:T(8,128)(2,1)S(1)}, u32[]{:S(2)}, u32[]{:S(2)}) collective-permute-start(bf16[64,2176]{1,0:T(8,128)(2,1)S(1)} %collective-permute-done.8.refs_1_), channel_id=1, source_target_pairs={{0,4},{1,5},{4,8},{5,9},{8,12},{9,13},{12,14},{13,15},{14,10},{15,... | collective-permute-start | bytes 835592 | tf_op jit(solution)/shard_map/ppermute | solution.py:350
  43.9 10.0 %collective-permute-start.14 = (bf16[64,2176]{1,0:T(8,128)(2,1)S(1)}, bf16[64,2176]{1,0:T(8,128)(2,1)S(1)}, u32[]{:S(2)}, u32[]{:S(2)}) collective-permute-start(bf16[64,2176]{1,0:T(8,128)(2,1)S(1)} %collective-permute-done.9.refs_2_), channel_id=1, source_target_pairs={{0,2},{1,3},{4,0},{5,1},{8,4},{9,5},{12,8},{13,9},{14,12},{15,13},... | collective-permute-start | bytes 835592 | tf_op jit(solution)/shard_map/ppermute | solution.py:350
  46.1 13.9 %collective-permute-start.16 = (bf16[64,2176]{1,0:T(8,128)(2,1)S(1)}, bf16[64,2176]{1,0:T(8,128)(2,1)S(1)}, u32[]{:S(2)}, u32[]{:S(2)}) collective-permute-start(bf16[64,2176]{1,0:T(8,128)(2,1)S(1)} %get-tuple-element.108.refs_0_), channel_id=1, source_target_pairs={{0,2},{1,3},{4,0},{5,1},{8,4},{9,5},{12,8},{13,9},{14,12},{15,13},... | collective-permute-start | bytes 835592 | tf_op jit(solution)/shard_map/ppermute | solution.py:350
  46.1 13.8 %collective-permute-start.17 = (bf16[64,2176]{1,0:T(8,128)(2,1)S(1)}, bf16[64,2176]{1,0:T(8,128)(2,1)S(1)}, u32[]{:S(2)}, u32[]{:S(2)}) collective-permute-start(bf16[64,2176]{1,0:T(8,128)(2,1)S(1)} %get-tuple-element.108.refs_0_), channel_id=1, source_target_pairs={{0,4},{1,5},{4,8},{5,9},{8,12},{9,13},{12,14},{13,15},{14,10},{15,... | collective-permute-start | bytes 835592 | tf_op jit(solution)/shard_map/ppermute | solution.py:350
  54.0 10.1 %collective-permute-start.15 = (bf16[64,2176]{1,0:T(8,128)(2,1)S(1)}, bf16[64,2176]{1,0:T(8,128)(2,1)S(1)}, u32[]{:S(2)}, u32[]{:S(2)}) collective-permute-start(bf16[64,2176]{1,0:T(8,128)(2,1)S(1)} %collective-permute-done.13.refs_0_), channel_id=1, source_target_pairs={{0,4},{1,5},{4,8},{5,9},{8,12},{9,13},{12,14},{13,15},{14,10},{15,... | collective-permute-start | bytes 835592 | tf_op jit(solution)/shard_map/ppermute | solution.py:350
  56.0 9.9 %collective-permute-start.19 = (bf16[64,2176]{1,0:T(8,128)(2,1)S(1)}, bf16[64,2176]{1,0:T(8,128)(2,1)S(1)}, u32[]{:S(2)}, u32[]{:S(2)}) collective-permute-start(bf16[64,2176]{1,0:T(8,128)(2,1)S(1)} %collective-permute-done.14.refs_1_), channel_id=1, source_target_pairs={{0,2},{1,3},{4,0},{5,1},{8,4},{9,5},{12,8},{13,9},{14,12},{15,13},... | collective-permute-start | bytes 835592 | tf_op jit(solution)/shard_map/ppermute | solution.py:350
  59.9 10.2 %collective-permute-start.20 = (bf16[64,2176]{1,0:T(8,128)(2,1)S(1)}, bf16[64,2176]{1,0:T(8,128)(2,1)S(1)}, u32[]{:S(2)}, u32[]{:S(2)}) collective-permute-start(bf16[64,2176]{1,0:T(8,128)(2,1)S(1)} %collective-permute-done.16.refs_1_), channel_id=1, source_target_pairs={{0,2},{1,3},{4,0},{5,1},{8,4},{9,5},{12,8},{13,9},{14,12},{15,13},... | collective-permute-start | bytes 835592 | tf_op jit(solution)/shard_map/ppermute | solution.py:350
  60.2 14.0 %collective-permute-start.21 = (bf16[64,2176]{1,0:T(8,128)(2,1)S(1)}, bf16[64,2176]{1,0:T(8,128)(2,1)S(1)}, u32[]{:S(2)}, u32[]{:S(2)}) collective-permute-start(bf16[64,2176]{1,0:T(8,128)(2,1)S(1)} %collective-permute-done.17.refs_2_), channel_id=1, source_target_pairs={{0,4},{1,5},{4,8},{5,9},{8,12},{9,13},{12,14},{13,15},{14,10},{15,... | collective-permute-start | bytes 835592 | tf_op jit(solution)/shard_map/ppermute | solution.py:350
  70.2 6.9 %collective-permute-start.23 = (bf16[64,2176]{1,0:T(8,128)(2,1)S(1)}, bf16[64,2176]{1,0:T(8,128)(2,1)S(1)}, u32[]{:S(2)}, u32[]{:S(2)}) collective-permute-start(bf16[64,2176]{1,0:T(8,128)(2,1)S(1)} %collective-permute-done.20.refs_0_), channel_id=1, source_target_pairs={{0,2},{1,3},{4,0},{5,1},{8,4},{9,5},{12,8},{13,9},{14,12},{15,13},... | collective-permute-start | bytes 835592 | tf_op jit(solution)/shard_map/ppermute | solution.py:350
  70.2 9.8 %collective-permute-start.18 = (bf16[64,2176]{1,0:T(8,128)(2,1)S(1)}, bf16[64,2176]{1,0:T(8,128)(2,1)S(1)}, u32[]{:S(2)}, u32[]{:S(2)}) collective-permute-start(bf16[64,2176]{1,0:T(8,128)(2,1)S(1)} %collective-permute-done.15.refs_1_), channel_id=1, source_target_pairs={{0,4},{1,5},{4,8},{5,9},{8,12},{9,13},{12,14},{13,15},{14,10},{15,... | collective-permute-start | bytes 835592 | tf_op jit(solution)/shard_map/ppermute | solution.py:350
  77.1 7.9 %collective-permute-start.24 = (bf16[64,2176]{1,0:T(8,128)(2,1)S(1)}, bf16[64,2176]{1,0:T(8,128)(2,1)S(1)}, u32[]{:S(2)}, u32[]{:S(2)}) collective-permute-start(bf16[64,2176]{1,0:T(8,128)(2,1)S(1)} %collective-permute-done.23.refs_1_), channel_id=1, source_target_pairs={{0,2},{1,3},{4,0},{5,1},{8,4},{9,5},{12,8},{13,9},{14,12},{15,13},... | collective-permute-start | bytes 835592 | tf_op jit(solution)/shard_map/ppermute | solution.py:350
  77.4 14.0 %collective-permute-start.27 = (bf16[64,2176]{1,0:T(8,128)(2,1)S(1)}, bf16[64,2176]{1,0:T(8,128)(2,1)S(1)}, u32[]{:S(2)}, u32[]{:S(2)}) collective-permute-start(bf16[64,2176]{1,0:T(8,128)(2,1)S(1)} %collective-permute-done.21.refs_1_), channel_id=1, source_target_pairs={{0,4},{1,5},{4,8},{5,9},{8,12},{9,13},{12,14},{13,15},{14,10},{15,... | collective-permute-start | bytes 835592 | tf_op jit(solution)/shard_map/ppermute | solution.py:350
  83.0 6.7 %collective-permute-start.22 = (bf16[64,2048]{1,0:T(8,128)(2,1)S(1)}, bf16[64,2048]{1,0:T(8,128)(2,1)S(1)}, u32[]{:S(2)}, u32[]{:S(2)}) collective-permute-start(bf16[64,2048]{1,0:T(8,128)(2,1)S(1)} %get-tuple-element.113), channel_id=1, source_target_pairs={{0,4},{1,5},{4,8},{5,9},{8,12},{9,13},{12,14},{13,15},{14,10},{15,... | collective-permute-start | bytes 786440 | tf_op jit(solution)/shard_map/ppermute | solution.py:350
  85.0 6.4 %collective-permute-start.25 = (bf16[64,2048]{1,0:T(8,128)(2,1)S(1)}, bf16[64,2048]{1,0:T(8,128)(2,1)S(1)}, u32[]{:S(2)}, u32[]{:S(2)}) collective-permute-start(bf16[64,2048]{1,0:T(8,128)(2,1)S(1)} %get-tuple-element.120), channel_id=1, source_target_pairs={{0,2},{1,3},{4,0},{5,1},{8,4},{9,5},{12,8},{13,9},{14,12},{15,13},... | collective-permute-start | bytes 786440 | tf_op jit(solution)/shard_map/ppermute | solution.py:350
  93.5 8.0 %collective-permute-start.33 = (bf16[64,2048]{1,0:T(8,128)(2,1)S(1)}, bf16[64,2048]{1,0:T(8,128)(2,1)S(1)}, u32[]{:S(2)}, u32[]{:S(2)}) collective-permute-start(bf16[64,2048]{1,0:T(8,128)(2,1)S(1)} %get-tuple-element.142), channel_id=1, source_target_pairs={{0,4},{1,5},{4,8},{5,9},{8,12},{9,13},{12,14},{13,15},{14,10},{15,... | collective-permute-start | bytes 786440 | tf_op jit(solution)/shard_map/ppermute | solution.py:350
  95.3 9.2 %collective-permute-start.32 = (bf16[64,2048]{1,0:T(8,128)(2,1)S(1)}, bf16[64,2048]{1,0:T(8,128)(2,1)S(1)}, u32[]{:S(2)}, u32[]{:S(2)}) collective-permute-start(bf16[64,2048]{1,0:T(8,128)(2,1)S(1)} %get-tuple-element.140), channel_id=1, source_target_pairs={{0,2},{1,3},{4,0},{5,1},{8,4},{9,5},{12,8},{13,9},{14,12},{15,13},... | collective-permute-start | bytes 786440 | tf_op jit(solution)/shard_map/ppermute | solution.py:350
  95.7 14.4 %collective-permute-start.28 = (bf16[64,2048]{1,0:T(8,128)(2,1)S(1)}, bf16[64,2048]{1,0:T(8,128)(2,1)S(1)}, u32[]{:S(2)}, u32[]{:S(2)}) collective-permute-start(bf16[64,2048]{1,0:T(8,128)(2,1)S(1)} %get-tuple-element.129), channel_id=1, source_target_pairs={{0,2},{1,3},{4,0},{5,1},{8,4},{9,5},{12,8},{13,9},{14,12},{15,13},... | collective-permute-start | bytes 786440 | tf_op jit(solution)/shard_map/ppermute | solution.py:350
  96.1 14.0 %collective-permute-start.26 = (bf16[64,2048]{1,0:T(8,128)(2,1)S(1)}, bf16[64,2048]{1,0:T(8,128)(2,1)S(1)}, u32[]{:S(2)}, u32[]{:S(2)}) collective-permute-start(bf16[64,2048]{1,0:T(8,128)(2,1)S(1)} %get-tuple-element.123), channel_id=1, source_target_pairs={{0,4},{1,5},{4,8},{5,9},{8,12},{9,13},{12,14},{13,15},{14,10},{15,... | collective-permute-start | bytes 786440 | tf_op jit(solution)/shard_map/ppermute | solution.py:350
  104.6 8.8 %collective-permute-start.35 = (bf16[64,2048]{1,0:T(8,128)(2,1)S(1)}, bf16[64,2048]{1,0:T(8,128)(2,1)S(1)}, u32[]{:S(2)}, u32[]{:S(2)}) collective-permute-start(bf16[64,2048]{1,0:T(8,128)(2,1)S(1)} %get-tuple-element.147), channel_id=1, source_target_pairs={{0,4},{1,5},{4,8},{5,9},{8,12},{9,13},{12,14},{13,15},{14,10},{15,... | collective-permute-start | bytes 786440 | tf_op jit(solution)/shard_map/ppermute | solution.py:350
  106.1 9.6 %collective-permute-start.34 = (bf16[64,2048]{1,0:T(8,128)(2,1)S(1)}, bf16[64,2048]{1,0:T(8,128)(2,1)S(1)}, u32[]{:S(2)}, u32[]{:S(2)}) collective-permute-start(bf16[64,2048]{1,0:T(8,128)(2,1)S(1)} %get-tuple-element.145), channel_id=1, source_target_pairs={{0,2},{1,3},{4,0},{5,1},{8,4},{9,5},{12,8},{13,9},{14,12},{15,13},... | collective-permute-start | bytes 786440 | tf_op jit(solution)/shard_map/ppermute | solution.py:350
  110.2 10.0 %collective-permute-start.30 = (bf16[64,2048]{1,0:T(8,128)(2,1)S(1)}, bf16[64,2048]{1,0:T(8,128)(2,1)S(1)}, u32[]{:S(2)}, u32[]{:S(2)}) collective-permute-start(bf16[64,2048]{1,0:T(8,128)(2,1)S(1)} %add_convert_fusion.8), channel_id=1, source_target_pairs={{0,2},{1,3},{4,0},{5,1},{8,4},{9,5},{12,8},{13,9},{14,12},{15,13},... | collective-permute-start | bytes 786440 | tf_op jit(solution)/shard_map/ppermute | solution.py:350
  110.3 9.9 %collective-permute-start.29 = (bf16[64,2048]{1,0:T(8,128)(2,1)S(1)}, bf16[64,2048]{1,0:T(8,128)(2,1)S(1)}, u32[]{:S(2)}, u32[]{:S(2)}) collective-permute-start(bf16[64,2048]{1,0:T(8,128)(2,1)S(1)} %add_convert_fusion.9), channel_id=1, source_target_pairs={{0,4},{1,5},{4,8},{5,9},{8,12},{9,13},{12,14},{13,15},{14,10},{15,... | collective-permute-start | bytes 786440 | tf_op jit(solution)/shard_map/ppermute | solution.py:350
  115.8 7.5 %collective-permute-start.37 = (bf16[64,2048]{1,0:T(8,128)(2,1)S(1)}, bf16[64,2048]{1,0:T(8,128)(2,1)S(1)}, u32[]{:S(2)}, u32[]{:S(2)}) collective-permute-start(bf16[64,2048]{1,0:T(8,128)(2,1)S(1)} %add_convert_fusion.2), channel_id=1, source_target_pairs={{0,4},{1,5},{4,8},{5,9},{8,12},{9,13},{12,14},{13,15},{14,10},{15,... | collective-permute-start | bytes 786440 | tf_op jit(solution)/shard_map/ppermute | solution.py:350
  117.4 7.9 %collective-permute-start.36 = (bf16[64,2048]{1,0:T(8,128)(2,1)S(1)}, bf16[64,2048]{1,0:T(8,128)(2,1)S(1)}, u32[]{:S(2)}, u32[]{:S(2)}) collective-permute-start(bf16[64,2048]{1,0:T(8,128)(2,1)S(1)} %add_convert_fusion.3), channel_id=1, source_target_pairs={{0,2},{1,3},{4,0},{5,1},{8,4},{9,5},{12,8},{13,9},{14,12},{15,13},... | collective-permute-start | bytes 786440 | tf_op jit(solution)/shard_map/ppermute | solution.py:350
  120.3 6.4 %collective-permute-start.31 = (bf16[64,2048]{1,0:T(8,128)(2,1)S(1)}, bf16[64,2048]{1,0:T(8,128)(2,1)S(1)}, u32[]{:S(2)}, u32[]{:S(2)}) collective-permute-start(bf16[64,2048]{1,0:T(8,128)(2,1)S(1)} %add_convert_fusion.7), channel_id=1, source_target_pairs={{0,4},{1,5},{4,8},{5,9},{8,12},{9,13},{12,14},{13,15},{14,10},{15,... | collective-permute-start | bytes 786440 | tf_op jit(solution)/shard_map/ppermute | solution.py:350
  125.4 6.4 %collective-permute-start.38 = (bf16[64,2048]{1,0:T(8,128)(2,1)S(1)}, bf16[64,2048]{1,0:T(8,128)(2,1)S(1)}, u32[]{:S(2)}, u32[]{:S(2)}) collective-permute-start(bf16[64,2048]{1,0:T(8,128)(2,1)S(1)} %add_convert_fusion.1), channel_id=1, source_target_pairs={{0,2},{1,3},{4,0},{5,1},{8,4},{9,5},{12,8},{13,9},{14,12},{15,13},... | collective-permute-start | bytes 786440 | tf_op jit(solution)/shard_map/ppermute | solution.py:350
